TPU v7x, 128 devices: a whole 4x4x4 slice. The times are simulated.
128 devices in a mesh: section: 2 (over core), ctx: 16 (over x, z), shard: 4 (over y).
Axes of the slice: x: 4, y: 4, z: 4, core: 2. Of those that a mesh axis runs over, the one named last changes fastest.
Arguments:
- hidden_in: bfloat16 [4, 2, 1024, 1088], P('shard', None, 'ctx'), may hold values from -6 to 6
- cotangent: bfloat16 [4, 2, 1024, 1088], P('shard', None, 'ctx'), may hold values from -6 to 6
- block_order: int32 [2, 32], replicated, may hold values from 0 to 31, as said below
- qkv_weight: bfloat16 [2, 1088, 3264], P('section', 'shard'), may hold values from -0.1875 to 0.1875
- out_weight: bfloat16 [2, 1088, 1088], P('section', 'shard'), may hold values from -0.75 to 0.75
- up_weight: bfloat16 [2, 1088, 4352], P('section', 'shard'), may hold values from -0.1875 to 0.1875
- down_weight: bfloat16 [2, 4352, 1088], P('section', 'shard'), may hold values from -0.09375 to 0.09375
- norm_gains: bfloat16 [2, 2, 1088], P('section', None, 'shard'), may hold values from 0.5 to 1.5
- norm_biases: bfloat16 [2, 2, 1088], P('section', None, 'shard'), may hold values from -3 to 3
Outputs:
- activations: bfloat16 [2, 4, 2, 1024, 1088], P('section', 'shard', None, 'ctx')
- input_grads: bfloat16 [2, 4, 2, 1024, 1088], P('section', 'shard', None, 'ctx')
- qkv_grad: float32 [2, 1088, 3264], P('section', 'shard')
- out_grad: float32 [2, 1088, 1088], P('section', 'shard')
- up_grad: float32 [2, 1088, 4352], P('section', 'shard')
- down_grad: float32 [2, 4352, 1088], P('section', 'shard')
- gain_grad: float32 [2, 2, 1088], P('section', None, 'shard')
- bias_grad: float32 [2, 2, 1088], P('section', None, 'shard')
Inputs may be any that keep to these rules, and one draw needn't show every extreme that they name: `block_order`: each row holds every block number once, and entries 2 c and 2 c + 1 sum to 31.
All inputs are finite; a program needn't handle non-finite values.
Results may differ from a plain program's by a relative error of at most 0.018.
Values may be sent and summed in bfloat16 or wider, within the bound.
A program may use at most 320 MiB of HBM per device.

v0:
```python
import jax
import jax.numpy as jnp
from jax import lax
from jax.sharding import Mesh
from jax.sharding import PartitionSpec as P

HEADS = 17
HEAD_DIM = 64
CTX = ("ctx_0", "ctx_1")


EPSILON = 1e-05
NEG_LARGE = -1e30


def in_one_piece(arrays, axis, dim, along):
    both = jnp.concatenate(arrays, axis=along)
    out, at, outs = (lax.all_gather(both, axis, axis=dim, tiled=True), 0, [])
    for a in arrays:
        outs.append(lax.slice_in_dim(out, at, at + a.shape[along], axis=along))
        at += a.shape[along]
    return tuple(outs)


def shifted(value, axis, steps):
    count = lax.axis_size(axis)
    first, last = (max(0, -steps), min(count, count - steps))
    return lax.ppermute(value, axis, [(source, source + steps) for source in range(first, last)])


def summed_rows(x, axes, dim):
    for axis in axes:
        x = lax.psum_scatter(x, axis, scatter_dimension=dim, tiled=True)
    return x


def in_one_piece_2(arrays, axis, dim, along):
    ends, at = ([], 0)
    for a in arrays[:-1]:
        at += a.shape[along]
        ends.append(at)
    both = jnp.concatenate(arrays, axis=along)
    return tuple(
        jnp.split(lax.psum_scatter(both, axis, scatter_dimension=dim, tiled=True), ends, axis=along)
    )


def for_sending(x):

    def short(part):
        return part.astype(jnp.bfloat16) if part.dtype == jnp.float32 else part

    return jax.tree.map(short, x)


def layer_norm(values, gain_row, shift_row):
    center = values - jnp.mean(values, axis=-1, keepdims=True)
    spread = jnp.mean(center * center, axis=-1, keepdims=True)
    return center * lax.rsqrt(spread + EPSILON) * gain_row + shift_row


def gelu_tanh(values):
    return jax.nn.gelu(values, approximate=True)


def matmul(left_side, right_side):
    return jnp.dot(left_side, right_side, preferred_element_type=jnp.float32)


def matmul_tn(left_side, right_side):
    return lax.dot_general(
        left_side, right_side, (((0,), (0,)), ((), ())), preferred_element_type=jnp.float32
    )


def matmul_nt(left_side, right_side):
    return lax.dot_general(
        left_side, right_side, (((1,), (1,)), ((), ())), preferred_element_type=jnp.float32
    )


def key_positions(block_order, group_len, block_len):
    offsets = lax.broadcasted_iota(jnp.int32, (1, 1, block_len), 2)
    group_ids = lax.broadcasted_iota(jnp.int32, (block_order.shape[0], 1, 1), 0)
    return (group_ids * group_len + block_order[:, :, None] * block_len + offsets).reshape(-1)


def split_heads(matrix):
    return matrix.reshape(matrix.shape[0], HEADS, HEAD_DIM)


def attention_probs(queries, key_rows, query_pos, key_pos):
    scores = jnp.einsum(
        "qhd,khd->hqk",
        split_heads(queries),
        split_heads(key_rows),
        preferred_element_type=jnp.float32,
    ) * HEAD_DIM ** (-0.5)
    scores = jnp.where(query_pos[None, :, None] >= key_pos[None, None, :], scores, NEG_LARGE)
    row_max = jnp.max(scores, axis=-1, keepdims=True)
    exponent = jnp.exp(scores - row_max)
    return exponent / jnp.sum(exponent, axis=-1, keepdims=True)


def layer_tail(
    layer_in, queries, kv_cache, query_pos, key_pos, w_out, w_up, w_down, gain_row, shift_row
):
    model_width = layer_in.shape[1]
    attn_probs = attention_probs(queries, kv_cache[:, :model_width], query_pos, key_pos)
    probs_low = attn_probs.astype(jnp.bfloat16)
    mixed = jnp.einsum(
        "hqk,khd->qhd",
        probs_low,
        split_heads(kv_cache[:, model_width:]),
        preferred_element_type=jnp.float32,
    )
    context_low = mixed.reshape(mixed.shape[0], model_width).astype(jnp.bfloat16)
    residual = layer_in.astype(jnp.float32) + matmul(context_low, w_out)
    normed2 = layer_norm(residual, gain_row, shift_row).astype(jnp.bfloat16)
    pre_act = matmul(normed2, w_up)
    hidden_low = gelu_tanh(pre_act).astype(jnp.bfloat16)
    result = residual + matmul(hidden_low, w_down)
    return (attn_probs, probs_low, context_low, residual, normed2, pre_act, hidden_low, result)


def attention_back(grad_context, attn_probs, probs_low, queries, key_rows, value_rows):
    scale = HEAD_DIM ** (-0.5)
    grad_heads = split_heads(grad_context)
    grad_probs = jnp.einsum(
        "qhd,khd->hqk", grad_heads, split_heads(value_rows), preferred_element_type=jnp.float32
    )
    grad_values = jnp.einsum(
        "hqk,qhd->khd", probs_low, grad_heads, preferred_element_type=jnp.float32
    )
    grad_scores = (
        attn_probs * (grad_probs - jnp.sum(attn_probs * grad_probs, axis=-1, keepdims=True))
    ).astype(jnp.bfloat16)
    grad_queries = (
        jnp.einsum(
            "hqk,khd->qhd", grad_scores, split_heads(key_rows), preferred_element_type=jnp.float32
        )
        * scale
    )
    grad_keys = (
        jnp.einsum(
            "hqk,qhd->khd", grad_scores, split_heads(queries), preferred_element_type=jnp.float32
        )
        * scale
    )
    query_count = grad_queries.shape[0]
    key_count = grad_keys.shape[0]
    grad_queries = grad_queries.reshape(query_count, -1).astype(jnp.bfloat16)
    return (grad_queries, grad_keys.reshape(key_count, -1), grad_values.reshape(key_count, -1))


def gather_weights(qkv_weight, out_weight, up_weight, down_weight, norm_gains, norm_biases):
    return (
        *in_one_piece((qkv_weight[0], out_weight[0], up_weight[0]), "shard", 0, 1),
        lax.all_gather(down_weight[0], "shard", axis=0, tiled=True),
        *in_one_piece((norm_gains[0], norm_biases[0]), "shard", 1, 0),
    )


def shards(
    hidden_in,
    cotangent,
    block_order,
    qkv_weight,
    out_weight,
    up_weight,
    down_weight,
    norm_gains,
    norm_biases,
):
    section_index = lax.axis_index("section")
    ctx_index = lax.axis_index(CTX)
    row_count = hidden_in.shape[2]
    micro_count = hidden_in.shape[1]
    model_width = hidden_in.shape[3]
    group_len = row_count * lax.axis_size(CTX)
    key_pos = key_positions(block_order, group_len, row_count // 2)
    pos_grid = key_pos.reshape(micro_count, group_len)
    is_first = section_index == 0
    is_last = section_index == lax.axis_size("section") - 1
    gathered_weights = gather_weights(
        qkv_weight, out_weight, up_weight, down_weight, norm_gains, norm_biases
    )
    w_qkv, w_out, w_up, w_down, gains, shifts = gathered_weights
    gains32 = gains.astype(jnp.float32)
    shifts32 = shifts.astype(jnp.float32)
    inputs_kept = jnp.zeros((micro_count, row_count, model_width), jnp.bfloat16)
    outputs_kept = jnp.zeros_like(inputs_kept)
    kv_cache = jnp.zeros((micro_count * group_len, 2 * model_width), jnp.bfloat16)
    incoming = jnp.zeros((row_count, model_width), jnp.bfloat16)
    for period in range(micro_count + 1):
        slot_raw = period - section_index
        is_valid = (slot_raw >= 0) & (slot_raw < micro_count)
        slot_index = jnp.clip(slot_raw, 0, micro_count - 1)
        layer_in = jnp.where(is_first, hidden_in[0, min(period, micro_count - 1)], incoming)
        query_pos = lax.dynamic_slice(
            pos_grid, (slot_index, ctx_index * row_count), (1, row_count)
        )[0]
        normed = layer_norm(layer_in.astype(jnp.float32), gains32[0], shifts32[0]).astype(
            jnp.bfloat16
        )
        projected = matmul(normed, w_qkv).astype(jnp.bfloat16)
        gathered = lax.all_gather(projected[:, model_width:], CTX, axis=0, tiled=True)
        old_slot = lax.dynamic_slice_in_dim(kv_cache, slot_index * group_len, group_len, 0)
        kv_cache = lax.dynamic_update_slice_in_dim(
            kv_cache, jnp.where(is_valid, gathered, old_slot), slot_index * group_len, 0
        )
        tail = layer_tail(
            layer_in,
            projected[:, :model_width],
            kv_cache,
            query_pos,
            key_pos,
            w_out,
            w_up,
            w_down,
            gains32[1],
            shifts32[1],
        )
        sent = tail[7].astype(jnp.bfloat16)
        old_in = lax.dynamic_index_in_dim(inputs_kept, slot_index, 0, keepdims=False)
        inputs_kept = lax.dynamic_update_index_in_dim(
            inputs_kept, jnp.where(is_valid, layer_in, old_in), slot_index, 0
        )
        old_out = lax.dynamic_index_in_dim(outputs_kept, slot_index, 0, keepdims=False)
        outputs_kept = lax.dynamic_update_index_in_dim(
            outputs_kept, jnp.where(is_valid, sent, old_out), slot_index, 0
        )
        incoming = shifted(sent, "section", 1)
    gathered_weights = gather_weights(
        qkv_weight, out_weight, up_weight, down_weight, norm_gains, norm_biases
    )
    w_qkv, w_out, w_up, w_down, gains, shifts = gathered_weights
    gains32 = gains.astype(jnp.float32)
    shifts32 = shifts.astype(jnp.float32)
    grad_sum = tuple((jnp.zeros(member.shape, jnp.float32) for member in gathered_weights))
    w_query = w_qkv[:, :model_width]
    key_grads = jnp.zeros((micro_count * group_len, 2 * model_width), jnp.float32)
    grads_kept = jnp.zeros((micro_count, row_count, model_width), jnp.bfloat16)
    incoming = jnp.zeros((row_count, model_width), jnp.bfloat16)
    for period in range(micro_count + 1):
        slot_raw = micro_count - period - section_index
        is_valid = (slot_raw >= 0) & (slot_raw < micro_count)
        live_scale = is_valid.astype(jnp.float32)
        slot_index = jnp.clip(slot_raw, 0, micro_count - 1)
        layer_in = lax.dynamic_index_in_dim(inputs_kept, slot_index, 0, keepdims=False)
        seed_rows = lax.dynamic_index_in_dim(cotangent[0], slot_index, 0, keepdims=False)
        grad_out = jnp.where(is_last, seed_rows, incoming).astype(jnp.float32) * live_scale
        query_pos = lax.dynamic_slice(
            pos_grid, (slot_index, ctx_index * row_count), (1, row_count)
        )[0]
        layer_in32 = layer_in.astype(jnp.float32)
        normed = layer_norm(layer_in32, gains32[0], shifts32[0]).astype(jnp.bfloat16)
        queries = matmul(normed, w_query).astype(jnp.bfloat16)
        attn_probs, probs_low, context_low, residual, normed2, pre_act, hidden_low, result = (
            layer_tail(
                layer_in,
                queries,
                kv_cache,
                query_pos,
                key_pos,
                w_out,
                w_up,
                w_down,
                gains32[1],
                shifts32[1],
            )
        )
        grad_branch = grad_out.astype(jnp.bfloat16)
        grad_down = matmul_tn(hidden_low, grad_branch)
        grad_hidden = matmul_nt(grad_branch, w_down)
        _, gelu_pull = jax.vjp(gelu_tanh, pre_act)
        grad_pre = gelu_pull(grad_hidden)[0].astype(jnp.bfloat16)
        grad_up = matmul_tn(normed2, grad_pre)
        grad_normed2 = matmul_nt(grad_pre, w_up)
        _, norm_pull2 = jax.vjp(layer_norm, residual, gains32[1], shifts32[1])
        grad_mid_part, grad_gain2, grad_shift2 = norm_pull2(grad_normed2)
        grad_mid = grad_out + grad_mid_part
        grad_attn = grad_mid.astype(jnp.bfloat16)
        grad_outw = matmul_tn(context_low, grad_attn)
        grad_context = matmul_nt(grad_attn, w_out).astype(jnp.bfloat16)
        grad_queries, grad_keys, grad_values = attention_back(
            grad_context,
            attn_probs,
            probs_low,
            queries,
            kv_cache[:, :model_width],
            kv_cache[:, model_width:],
        )
        key_grads = key_grads + jnp.concatenate([grad_keys, grad_values], axis=1)
        grad_group = lax.dynamic_slice_in_dim(key_grads, slot_index * group_len, group_len, 0)
        grad_kv = (
            summed_rows(grad_group.astype(jnp.bfloat16), CTX, 0).astype(jnp.float32) * live_scale
        )
        grad_proj = jnp.concatenate([grad_queries, grad_kv.astype(jnp.bfloat16)], axis=1)
        grad_qkvw = matmul_tn(normed, grad_proj)
        grad_normed = matmul_nt(grad_proj, w_qkv)
        _, norm_pull1 = jax.vjp(layer_norm, layer_in32, gains32[0], shifts32[0])
        grad_in_part, grad_gain1, grad_shift1 = norm_pull1(grad_normed)
        grad_in_low = (grad_mid + grad_in_part).astype(jnp.bfloat16)
        old_grad = lax.dynamic_index_in_dim(grads_kept, slot_index, 0, keepdims=False)
        grads_kept = lax.dynamic_update_index_in_dim(
            grads_kept, jnp.where(is_valid, grad_in_low, old_grad), slot_index, 0
        )
        period_grads = (
            grad_qkvw,
            grad_outw,
            grad_up,
            grad_down,
            jnp.stack([grad_gain1, grad_gain2]),
            jnp.stack([grad_shift1, grad_shift2]),
        )
        grad_sum = jax.tree.map(jnp.add, grad_sum, period_grads)
        incoming = shifted(grad_in_low, "section", -1)
    grad_sum = (
        *tuple(
            (
                part.astype(jnp.float32)
                for part in in_one_piece_2(
                    (
                        grad_sum[0].astype(jnp.bfloat16),
                        grad_sum[1].astype(jnp.bfloat16),
                        grad_sum[2].astype(jnp.bfloat16),
                    ),
                    "shard",
                    0,
                    1,
                )
            )
        ),
        lax.psum_scatter(
            grad_sum[3].astype(jnp.bfloat16), "shard", scatter_dimension=0, tiled=True
        ).astype(jnp.float32),
        *tuple(
            (
                part.astype(jnp.float32)
                for part in in_one_piece_2(
                    (grad_sum[4].astype(jnp.bfloat16), grad_sum[5].astype(jnp.bfloat16)),
                    "shard",
                    1,
                    0,
                )
            )
        ),
    )
    grad_sum = jax.tree.map(
        lambda part: part.astype(jnp.float32), lax.psum(for_sending(grad_sum), CTX)
    )
    qkv_grad, out_grad, up_grad, down_grad, gain_grad, bias_grad = grad_sum
    return (
        outputs_kept[None, None],
        grads_kept[None, None],
        qkv_grad[None],
        out_grad[None],
        up_grad[None],
        down_grad[None],
        gain_grad[None],
        bias_grad[None],
    )


def solution(mesh):
    split = Mesh(
        mesh.devices.reshape(mesh.shape["section"], 4, 4, mesh.shape["shard"]),
        ("section", "ctx_0", "ctx_1", "shard"),
    )
    placed = (
        P("shard", None, CTX, None),
        P("shard", None, CTX, None),
        P(),
        P("section", "shard", None),
        P("section", "shard", None),
        P("section", "shard", None),
        P("section", "shard", None),
        P("section", None, "shard"),
        P("section", None, "shard"),
    )
    return jax.shard_map(
        shards,
        mesh=split,
        in_specs=placed,
        out_specs=(
            P("section", "shard", None, CTX, None),
            P("section", "shard", None, CTX, None),
            P("section", "shard", None),
            P("section", "shard", None),
            P("section", "shard", None),
            P("section", "shard", None),
            P("section", None, "shard"),
            P("section", None, "shard"),
        ),
        check_vma=False,
    )
```

profile of v0, /device:TPU:1, one launch (start us, length us, event | category | flops | bytes accessed | tf_op | source)
XLA Modules:
  0.0 1526.5 jit_solution(2360503989936879446)
XLA Ops:
  17.0 10.3 all-gather.1
  27.9 164.8 %all-gather.8.cloned.1.call-done = bf16[1088,8704]{1,0:T(8,128)(2,1)} async-done(((bf16[272,8704]{1,0:T(8,128)(2,1)}), bf16[1088,8704]{1,0:T(8,128)(2,1)}) %all-gather.8.cloned.1.call-update) | async-done | bytes 18939920 | tf_op jit(solution)/shard_map/all_gather | solution.py:18
  201.2 49.8 %all-gather.10.cloned.1.call-done = bf16[1024,2176]{1,0:T(8,128)(2,1)} async-done(((bf16[64,2176]{1,0:T(8,128)(2,1)}), bf16[1024,2176]{1,0:T(8,128)(2,1)}) %all-gather.10.cloned.1.call-update) | async-done | bytes 4456464 | tf_op jit(solution)/shard_map/all_gather | solution.py:207
  293.5 55.8 %all-gather.16.cloned.1.call-done = bf16[1,4352,1088]{2,1,0:T(8,128)(2,1)} async-done(((bf16[1,1088,1088]{2,1,0:T(8,128)(2,1)}), bf16[1,4352,1088]{2,1,0:T(8,128)(2,1)}) %all-gather.16.cloned.1.call-update) | async-done | bytes 9469968 | tf_op jit(solution)/shard_map/all_gather | solution.py:159
  349.3 9.9 bitcast_dynamic-update-slice_fusion.6
  368.7 52.8 %all-gather.12.cloned.1.call-done = bf16[1024,2176]{1,0:T(8,128)(2,1)} async-done(((bf16[64,2176]{1,0:T(8,128)(2,1)}), bf16[1024,2176]{1,0:T(8,128)(2,1)}) %all-gather.12.cloned.1.call-update) | async-done | bytes 4456464 | tf_op jit(solution)/shard_map/all_gather | solution.py:207
  428.3 10.0 fusion.429
  470.1 9.9 bitcast_dynamic-update-slice_fusion.5
  492.5 48.5 %all-gather.14.cloned.1.call-done = bf16[1024,2176]{1,0:T(8,128)(2,1)} async-done(((bf16[64,2176]{1,0:T(8,128)(2,1)}), bf16[1024,2176]{1,0:T(8,128)(2,1)}) %all-gather.14.cloned.1.call-update) | async-done | bytes 4456464 | tf_op jit(solution)/shard_map/all_gather | solution.py:207
  547.9 10.0 fusion.428
  633.5 48.2 %reduce-scatter.18.cloned.1.call-done = bf16[256,2176]{0,1:T(8,128)(2,1)} async-done(((bf16[1024,2176]{0,1:T(8,128)(2,1)}), bf16[256,2176]{0,1:T(8,128)(2,1)}) %reduce-scatter.18.cloned.1.call-update) | async-done | bytes 1114128 | tf_op jit(solution)/shard_map/reduce_scatter | solution.py:33
  689.0 18.1 %reduce-scatter.28.cloned.1.call-done = bf16[64,2176]{1,0:T(8,128)(2,1)} async-done(((bf16[256,2176]{1,0:T(8,128)(2,1)}), bf16[64,2176]{1,0:T(8,128)(2,1)}) %reduce-scatter.28.cloned.1.call-update) | async-done | bytes 278544
  759.6 10.0 multiply_reduce_fusion.1
  782.4 13.5 fusion.8
  802.3 48.1 %reduce-scatter.20.cloned.1.call-done = bf16[256,2176]{0,1:T(8,128)(2,1)} async-done(((bf16[1024,2176]{0,1:T(8,128)(2,1)}), bf16[256,2176]{0,1:T(8,128)(2,1)}) %reduce-scatter.20.cloned.1.call-update) | async-done | bytes 1114128 | tf_op jit(solution)/shard_map/reduce_scatter | solution.py:33
  858.1 17.9 %reduce-scatter.30.cloned.1.call-done = bf16[64,2176]{1,0:T(8,128)(2,1)} async-done(((bf16[256,2176]{1,0:T(8,128)(2,1)}), bf16[64,2176]{1,0:T(8,128)(2,1)}) %reduce-scatter.30.cloned.1.call-update) | async-done | bytes 278544
  947.8 9.9 fusion.24
  959.5 9.8 fusion.424
  979.9 15.9 %convolution_add_fusion.1 = f32[1088,4352]{1,0:T(8,128)} fusion(f32[1088,4352]{1,0:T(8,128)} %fusion.424, bf16[64,4352]{1,0:T(8,128)(2,1)S(1)} %copy-done.56, f32[64,1088]{1,0:T(8,128)S(1)} %get-tuple-element.99, f32[64]{0:T(128)S(1)} %fusion.367, f32[64]{0:T(128)S(1)} %broadcast_multiply_fusion.5, f32[1088]{0:T(1024)S(1)} %get-tuple-element.33, ...), kind=kOutput, calls=%fused_computation.7 | convolution fusion | flops 611160064 | bytes 38724608 | tf_op jit(solution)/shard_map/dot_general | solution.py:71
  995.8 10.2 reduce-scatter.22.cloned.1.call-done
  1008.6 12.5 convolution_add_fusion.5
  1030.2 12.8 fusion.7
  1046.2 10.4 fusion.9
  1056.6 31.1 %concatenate.40 = bf16[1088,8704]{1,0:T(8,128)(2,1)} concatenate(bf16[1088,3264]{1,0:T(8,128)(2,1)} %fusion.9, bf16[1088,1088]{1,0:T(8,128)(2,1)S(1)} %fusion.27, bf16[1088,4352]{1,0:T(8,128)(2,1)} %fusion.7), dimensions={1} | concatenate | bytes 37879808 | tf_op jit(solution)/shard_map/concatenate | solution.py:42
  1088.7 11.6 fusion.184
  1100.3 13.3 convolution_add_fusion.3
  1113.5 11.5 fusion.6
  1133.2 120.2 %reduce-scatter.24.cloned.1.call-done = bf16[272,8704]{1,0:T(8,128)(2,1)} async-done(((bf16[1088,8704]{1,0:T(8,128)(2,1)}), bf16[272,8704]{1,0:T(8,128)(2,1)}) %reduce-scatter.24.cloned.1.call-update) | async-done | bytes 4734992 | tf_op jit(solution)/shard_map/reduce_scatter | solution.py:44
  1259.3 90.3 %reduce-scatter.26.cloned.1.call-done = bf16[1088,1088]{1,0:T(8,128)(2,1)} async-done(((bf16[4352,1088]{1,0:T(8,128)(2,1)}), bf16[1088,1088]{1,0:T(8,128)(2,1)}) %reduce-scatter.26.cloned.1.call-update) | async-done | bytes 2367504 | tf_op jit(solution)/shard_map/reduce_scatter | solution.py:335
  1368.6 10.0 fusion.88
  1380.3 35.1 %all-reduce = (bf16[1,2,272]{2,1,0:T(2,128)(2,1)S(1)}, bf16[1,2,272]{2,1,0:T(2,128)(2,1)S(1)}) all-reduce(bf16[1,2,272]{2,1,0:T(2,128)(2,1)S(1)} %bitcast.476, bf16[1,2,272]{2,1,0:T(2,128)(2,1)S(1)} %bitcast.477), channel_id=1, replica_groups=mesh['section'=2,'ctx_0'=4,'ctx_1'=4,'shard'=4] {'ctx_0','ctx_1'}, use_global_device_ids=true, to_apply=%region_76.77 | all-reduce | flops 1088 | bytes 4352 | tf_op jit(solution)/shard_map/psum | solution.py:351
  1416.5 93.1 %all-reduce.4.cloned.1.call-done = (bf16[1,272,3264]{2,1,0:T(8,128)(2,1)}, bf16[1,272,1088]{2,1,0:T(8,128)(2,1)}, bf16[1,272,4352]{2,1,0:T(8,128)(2,1)}, bf16[1,1088,1088]{2,1,0:T(8,128)(2,1)}) async-done(((bf16[1,272,3264]{2,1,0:T(8,128)(2,1)}, bf16[1,272,1088]{2,1,0:T(8,128)(2,1)}, bf16[1,272,4352]{2,1,0:T(8,128)(2,1)}, bf16[1,1088,1088]{2,1,0:T(8,128)(2,1)}), (bf16[1,272,3264]{2,1,0:T(8,128)(2,1)}, ...) | async-done | bytes 7102480 | tf_op jit(solution)/shard_map/psum | solution.py:351
  (503 shorter events, 434.9 us)
Async XLA Ops:
  7.2 185.5 %all-gather.8.cloned.1.call-start = ((), (), s32[]{:S(2)}) async-start(), calls=%async_computation.9 | async-start | bytes 23674880 | tf_op jit(solution)/shard_map/all_gather | solution.py:18
  16.3 234.7 %all-gather.10.cloned.1.call-start = ((), (), s32[]{:S(2)}) async-start(), calls=%async_computation.10 | async-start | bytes 4734976 | tf_op jit(solution)/shard_map/all_gather | solution.py:207
  197.9 151.4 %all-gather.16.cloned.1.call-start = ((), (), s32[]{:S(2)}) async-start(), calls=%async_computation.18 | async-start | bytes 12533760 | tf_op jit(solution)/shard_map/all_gather | solution.py:159
  198.6 223.0 %all-gather.12.cloned.1.call-start = ((), (), s32[]{:S(2)}) async-start(), calls=%async_computation.11 | async-start | bytes 4734976 | tf_op jit(solution)/shard_map/all_gather | solution.py:207
  359.2 3.3 collective-permute-start
  368.0 173.0 %all-gather.14.cloned.1.call-start = ((), (), s32[]{:S(2)}) async-start(), calls=%async_computation.12 | async-start | bytes 4734976 | tf_op jit(solution)/shard_map/all_gather | solution.py:207
  480.0 3.3 collective-permute-start.1
  488.0 59.9 %copy-start.44 = (bf16[64,3264]{1,0:T(8,128)(2,1)}, bf16[64,3264]{1,0:T(8,128)(2,1)S(1)}, u32[]{:S(2)}) copy-start(bf16[64,3264]{1,0:T(8,128)(2,1)S(1)} %convolution_convert_fusion) | copy-start | bytes 1253380
  488.9 192.7 %reduce-scatter.18.cloned.1.call-start = ((), (), s32[]{:S(2)}) async-start(), calls=%async_computation.13 | async-start | bytes 5570560 | tf_op jit(solution)/shard_map/reduce_scatter | solution.py:33
  633.4 73.7 %reduce-scatter.28.cloned.1.call-start = ((), (), s32[]{:S(2)}) async-start(), calls=%async_computation.19 | async-start | bytes 1392640
  684.0 166.4 %reduce-scatter.20.cloned.1.call-start = ((), (), s32[]{:S(2)}) async-start(), calls=%async_computation.14 | async-start | bytes 5570560 | tf_op jit(solution)/shard_map/reduce_scatter | solution.py:33
  737.6 9.4 collective-permute-start.2
  747.1 159.1 %copy-start.19 = (bf16[64,1088]{1,0:T(8,128)(2,1)}, bf16[64,1088]{1,0:T(8,128)(2,1)S(1)}, u32[]{:S(2)}) copy-start(bf16[64,1088]{1,0:T(8,128)(2,1)S(1)} %bitcast_select_fusion.2) | copy-start | bytes 417796
  802.2 50.9 %copy-start.90 = (f32[64]{0:T(128)S(1)}, f32[64]{0:T(128)}, u32[]{:S(2)}) copy-start(f32[64]{0:T(128)} %get-tuple-element.28) | copy-start | bytes 772
  802.2 73.7 %reduce-scatter.30.cloned.1.call-start = ((), (), s32[]{:S(2)}) async-start(), calls=%async_computation.20 | async-start | bytes 1392640
  852.8 153.1 %reduce-scatter.22.cloned.1.call-start = ((), (), s32[]{:S(2)}) async-start(), calls=%async_computation.15 | async-start | bytes 5570560 | tf_op jit(solution)/shard_map/reduce_scatter | solution.py:33
  895.6 28.1 %slice-start.13 = ((s8[18939904]{0:T(1024)(128)(4,1)}), s8[4194304]{0:T(1024)(128)(4,1)S(1)}, s32[]{:S(2)}) async-start(s8[18939904]{0:T(1024)(128)(4,1)} %bitcast.409), calls=%async_computation.37 | async-start | bytes 8388608
  895.6 28.1 %slice-start.14 = ((s8[18939904]{0:T(1024)(128)(4,1)}), s8[4194304]{0:T(1024)(128)(4,1)S(1)}, s32[]{:S(2)}) async-start(s8[18939904]{0:T(1024)(128)(4,1)} %bitcast.409), calls=%async_computation.38 | async-start | bytes 8388608
  895.6 28.1 %slice-start.15 = ((s8[18939904]{0:T(1024)(128)(4,1)}), s8[4194304]{0:T(1024)(128)(4,1)S(1)}, s32[]{:S(2)}) async-start(s8[18939904]{0:T(1024)(128)(4,1)} %bitcast.409), calls=%async_computation.39 | async-start | bytes 8388608
  906.5 9.9 collective-permute-start.3
  957.7 85.3 %reduce-scatter.32.cloned.1.call-start = ((), (), s32[]{:S(2)}) async-start(), calls=%async_computation.21 | async-start | bytes 1392640
  979.9 28.7 %copy-start.26 = (bf16[64,2176]{0,1:T(8,128)(2,1)S(1)}, bf16[64,2176]{0,1:T(8,128)(2,1)}, u32[]{:S(2)}) copy-start(bf16[64,2176]{0,1:T(8,128)(2,1)} %copy-done.25) | copy-start | bytes 835588
  979.9 28.8 %copy-start.64 = (bf16[17,64,64]{2,1,0:T(8,128)(2,1)S(1)}, bf16[17,64,64]{2,1,0:T(8,128)(2,1)}, u32[]{:S(2)}) copy-start(bf16[17,64,64]{2,1,0:T(8,128)(2,1)} %copy-done.63) | copy-start | bytes 417796
  1008.3 245.1 %reduce-scatter.24.cloned.1.call-start = ((), (), s32[]{:S(2)}) async-start(), calls=%async_computation.16 | async-start | bytes 23674880 | tf_op jit(solution)/shard_map/reduce_scatter | solution.py:44
  1087.8 261.8 %reduce-scatter.26.cloned.1.call-start = ((), (), s32[]{:S(2)}) async-start(), calls=%async_computation.17 | async-start | bytes 12533760 | tf_op jit(solution)/shard_map/reduce_scatter | solution.py:335
  1125.2 253.8 %reduce-scatter.34.cloned.1.call-start = ((), (), s32[]{:S(2)}) async-start(), calls=%async_computation.22 | async-start | bytes 348160
  1133.0 376.6 %all-reduce.4.cloned.1.call-start = ((), (), s32[]{:S(2)}) async-start(), calls=%async_computation.23 | async-start | bytes 14622720 | tf_op jit(solution)/shard_map/psum | solution.py:351
  1258.2 91.4 %copy-start.32 = (bf16[2,64,1088]{2,1,0:T(8,128)(2,1)S(1)}, bf16[2,64,1088]{2,1,0:T(8,128)(2,1)}, u32[]{:S(2)}) copy-start(bf16[2,64,1088]{2,1,0:T(8,128)(2,1)} %copy-done.31) | copy-start | bytes 835588
  1258.2 91.4 %slice-start.27 = ((bf16[64,3264]{1,0:T(8,128)(2,1)}), bf16[64,1088]{1,0:T(8,128)(2,1)S(1)}, s32[]{:S(2)}) async-start(bf16[64,3264]{1,0:T(8,128)(2,1)} %copy-done.44), calls=%async_computation.51 | async-start | bytes 294912 | tf_op jit(solution)/shard_map/slice | solution.py:214
  1259.3 90.6 %copy-start.66 = (pred[64,2048]{1,0:T(8,128)(4,1)S(1)}, pred[64,2048]{1,0:T(8,128)(4,1)}, u32[]{:S(2)}) copy-start(pred[64,2048]{1,0:T(8,128)(4,1)} %get-tuple-element.65) | copy-start | bytes 393220
  1378.6 135.5 %copy-start.57 = (bf16[1,1,2,64,1088]{4,3,2,1,0:T(8,128)(2,1)}, bf16[1,1,2,64,1088]{4,3,2,1,0:T(8,128)(2,1)S(1)}, u32[]{:S(2)}) copy-start(bf16[1,1,2,64,1088]{4,3,2,1,0:T(8,128)(2,1)S(1)} %fusion.88) | copy-start | bytes 835588
  1378.9 137.7 %copy-start.58 = (bf16[1,1,2,64,1088]{4,3,2,1,0:T(8,128)(2,1)}, bf16[1,1,2,64,1088]{4,3,2,1,0:T(8,128)(2,1)S(1)}, u32[]{:S(2)}) copy-start(bf16[1,1,2,64,1088]{4,3,2,1,0:T(8,128)(2,1)S(1)} %fusion.305) | copy-start | bytes 835588
  (108 other events, 926.6 us)
Sparse Core Ops, SparseCore 0:
  16.5 176.1 all-gather.7
  198.0 52.9 all-gather.9
  252.7 96.5 all-gather.15
  368.1 53.3 all-gather.11
  489.0 51.9 all-gather.13
  633.6 48.0 reduce-scatter.17
  684.6 22.4 reduce-scatter.27
  802.4 48.0 reduce-scatter.19
  853.6 22.3 reduce-scatter.29
  957.9 48.0 reduce-scatter.21
  1008.9 22.4 reduce-scatter.31
  1087.9 165.5 reduce-scatter.23
  1256.0 93.4 reduce-scatter.25
  1351.9 18.1 reduce-scatter.33
  1375.0 134.6 all-reduce.3
where the time goes:
time: 1540 us; the launch traced here: 1530 us
  waiting for transfers between devices  823 us (53%)
  matrix products  405 us (26%)
  local copies, waits for them, and re-layouts  151 us (10%)
  other arithmetic  72.1 us (5%)
  blocking collectives  45.4 us (3%)
  between operations  16.2 us (1%)
    all_gather x1, waiting for transfers between devices, in_one_piece(): out, at, outs = (lax.all_gather(both, axis, axis=dim, tiled=True), 0, [])  165 us
    all_gather x3, waiting for transfers between devices, shards(): lax.all_gather(projected[:, model_width:], CTX, axis=0, tiled=True)  151 us
    reduce_scatter x1, waiting for transfers between devices, in_one_piece_2(): lax.psum_scatter(both, axis, scatter_dimension=dim, tiled=True)  120 us
    dot_general x12, matrix products, matmul_tn(): lax.dot_general(left_side, right_side, (((0,), (0,)), ((), ())), preferre...  112 us
    reduce_scatter x3, waiting for transfers between devices, summed_rows(): x = lax.psum_scatter(x, axis, scatter_dimension=dim, tiled=True)  107 us
    psum x1, waiting for transfers between devices, shards(): lax.psum(for_sending(grad_sum), CTX)  93.1 us
    reduce_scatter x1, waiting for transfers between devices, shards(): lax.psum_scatter(grad_sum[3].astype(jnp.bfloat16), 'shard', scatter_dimen...  90.3 us
    dot_general x18, matrix products, matmul(): return jnp.dot(left_side, right_side, preferred_element_type=jnp.float32)  86.3 us
  transfers between devices with their start and end apart: 19, of which 15 were waited for; matrix products, arithmetic and copies ran while one was open for 14% of the time, Pallas kernels for 0%

commit v1 on v0

--- a/solution.py
+++ b/solution.py
@@ -1,16 +1,676 @@
+import types
+
 import jax
 import jax.numpy as jnp
 from jax import lax
-from jax.sharding import Mesh
+from jax.experimental import pallas as pl
+from jax.experimental.pallas import tpu as pltpu
 from jax.sharding import PartitionSpec as P
 
+D = 1088
 HEADS = 17
 HEAD_DIM = 64
-CTX = ("ctx_0", "ctx_1")
-
-
+FF = 4352
+SHARD = 4
+CTX = 16
+ROWS = 64
+GROUP = 1024
+SEQ = 2048
+WINDOW = 640
+SLICE = D // SHARD
 EPSILON = 1e-05
 NEG_LARGE = -1e30
+BF16 = jnp.bfloat16
+F32 = jnp.float32
+MESH = pl.DeviceIdType.MESH
+VMEM = pltpu.VMEM
+ANY = pl.ANY
+VMEM_BYTES = 56 * 2**20
+
+
+def spec(shape, dtype=BF16):
+    return jax.ShapeDtypeStruct(shape, dtype)
+
+
+def call(name, body, ins, outs, scratch, collective_id=None, prefetch=None):
+    in_names, out_names, scratch_names = list(ins), list(outs), list(scratch)
+    names = in_names + out_names + scratch_names
+
+    def kernel(*refs):
+        body(types.SimpleNamespace(**dict(zip(names, refs))))
+
+    extra = {} if collective_id is None else dict(collective_id=collective_id, has_side_effects=True)
+    results = pl.pallas_call(
+        kernel,
+        out_shape=tuple(outs[n][0] for n in out_names),
+        in_specs=[pl.BlockSpec(memory_space=ins[n][1]) for n in in_names],
+        out_specs=tuple(pl.BlockSpec(memory_space=outs[n][1]) for n in out_names),
+        scratch_shapes=[scratch[n] for n in scratch_names],
+        compiler_params=pltpu.CompilerParams(vmem_limit_bytes=VMEM_BYTES, **extra),
+        name=name,
+    )(*(ins[n][0] for n in in_names))
+    return dict(zip(out_names, results))
+
+
+def dot(a, b):
+    return jnp.dot(a, b, preferred_element_type=F32)
+
+
+def dot_nt(a, b):
+    return lax.dot_general(a, b, (((1,), (1,)), ((), ())), preferred_element_type=F32)
+
+
+def dot_tn(a, b):
+    return lax.dot_general(a, b, (((0,), (0,)), ((), ())), preferred_element_type=F32)
+
+
+def norm_parts(values):
+    center = values - jnp.mean(values, axis=-1, keepdims=True)
+    rate = lax.rsqrt(jnp.mean(center * center, axis=-1, keepdims=True) + EPSILON)
+    return center * rate, rate
+
+
+def layer_norm(values, gain, bias):
+    return norm_parts(values)[0] * gain + bias
+
+
+def gelu(u):
+    return 0.5 * u * (1.0 + jnp.tanh(0.7978845608028654 * (u + 0.044715 * u * u * u)))
+
+
+class Here:
+    def __init__(self, sems):
+        self.s = lax.axis_index("section")
+        self.c = lax.axis_index("ctx")
+        self.y = lax.axis_index("shard")
+        self.sems, self.used, self.sent = sems, 0, []
+
+    def sem(self):
+        self.used += 1
+        return self.sems.at[self.used - 1]
+
+    def shard(self, step):
+        return lax.rem(self.y + step, SHARD)
+
+    def rows(self, shard, core):
+        return pl.ds(pl.multiple_of((shard * 2 + core) * ROWS, ROWS), ROWS)
+
+    def barrier(self):
+        sem = pltpu.get_barrier_semaphore()
+        count = 0
+        for step in range(SHARD):
+            for core in range(2):
+                if step or core:
+                    to = (lax.rem(self.s + core, 2), self.c, self.shard(step))
+                    pl.semaphore_signal(sem, inc=1, device_id=to, device_id_type=MESH)
+                    count += 1
+        for step in range(1, CTX):
+            for core in range(2):
+                to = (core, lax.rem(self.c + step, CTX), self.y)
+                pl.semaphore_signal(sem, inc=1, device_id=to, device_id_type=MESH)
+                count += 1
+        pl.semaphore_wait(sem, count)
+
+    def send(self, src, dst, to, arrive, leave=None):
+        copy = pltpu.make_async_remote_copy(
+            src_ref=src, dst_ref=dst, send_sem=self.sem() if leave is None else leave,
+            recv_sem=arrive, device_id=to, device_id_type=MESH)
+        copy.start()
+        if leave is None:
+            self.sent.append(copy)
+        return copy
+
+    def send_or_keep(self, src, dst, to, is_self, arrive):
+        leave = self.sem()
+        copy = pltpu.make_async_remote_copy(
+            src_ref=src, dst_ref=dst, send_sem=leave, recv_sem=arrive, device_id=to, device_id_type=MESH)
+        kept = pltpu.make_async_copy(src, dst, arrive)
+        pl.when(jnp.logical_not(is_self))(copy.start)
+        pl.when(is_self)(kept.start)
+
+        def wait_send():
+            pl.when(jnp.logical_not(is_self))(copy.wait_send)
+
+        self.sent.append(types.SimpleNamespace(wait_send=wait_send))
+
+    def sibling(self):
+        return (1 - self.s, self.c, self.y)
+
+    def finish(self):
+        for copy in self.sent:
+            copy.wait_send()
+        self.sent = []
+
+
+def wait_bytes(ref, sem):
+    pltpu.make_async_copy(ref, ref, sem).wait()
+
+
+class Gather8:
+    def __init__(self, here, full):
+        self.here, self.full = here, full
+        self.own = [here.sem() for _ in range(SHARD)]
+        self.other = [here.sem() for _ in range(SHARD)]
+
+    def start(self, value):
+        h = self.here
+        mine = self.full.at[h.rows(h.y, h.s)]
+        mine[...] = value
+        h.send(mine, mine, h.sibling(), self.other[0])
+        for step in (1, 3, 2):
+            h.send(mine, mine, (h.s, h.c, h.shard(step)), self.own[SHARD - step])
+
+    def relay(self, step):
+        h = self.here
+        part = self.full.at[h.rows(h.shard(step), h.s)]
+        wait_bytes(part, self.own[step])
+        h.send(part, part, h.sibling(), self.other[step])
+
+    def wait(self, step):
+        h = self.here
+        wait_bytes(self.full.at[h.rows(h.shard(step), 1 - h.s)], self.other[step])
+
+
+class Scatter8:
+    def __init__(self, here, bufs):
+        self.here = here
+        self.to_core, self.mine, self.from_core, self.to_shard, self.from_shard = bufs
+        self.core = [here.sem() for _ in range(SHARD)]
+        self.shard = [here.sem() for _ in range(SHARD)]
+
+    def put(self, step, block):
+        h = self.here
+        low, high = block[:ROWS], block[ROWS:]
+        self.to_core[step] = jnp.where(h.s == 0, high, low).astype(BF16)
+        self.mine[step] = jnp.where(h.s == 0, low, high)
+        h.send(self.to_core.at[step], self.from_core.at[step], h.sibling(), self.core[step])
+
+    def relay(self, step):
+        h = self.here
+        wait_bytes(self.from_core.at[step], self.core[step])
+        self.to_shard[step] = (self.mine[step] + self.from_core[step].astype(F32)).astype(BF16)
+        h.send(self.to_shard.at[step], self.from_shard.at[step], (h.s, h.c, h.shard(step)), self.shard[step])
+
+    def result(self):
+        wait_bytes(self.from_core.at[0], self.core[0])
+        total = self.mine[0] + self.from_core[0].astype(F32)
+        for step in (1, 3, 2):
+            wait_bytes(self.from_shard.at[step], self.shard[step])
+            total = total + self.from_shard[step].astype(F32)
+        return total
+
+
+def scatter_scratch(name):
+    quarter = (SHARD, ROWS, D)
+    return {
+        name + "_to_core": VMEM(quarter, BF16),
+        name + "_mine": VMEM(quarter, F32),
+        name + "_from_core": VMEM(quarter, BF16),
+        name + "_to_shard": VMEM(quarter, BF16),
+        name + "_from_shard": VMEM(quarter, BF16),
+    }
+
+
+def scatter(here, r, name):
+    parts = ("_to_core", "_mine", "_from_core", "_to_shard", "_from_shard")
+    return Scatter8(here, [getattr(r, name + p) for p in parts])
+
+
+ORDER = (0, 1, 3, 2)
+
+
+def window_offset(group):
+    return 32 * lax.rem(group, 4)
+
+
+class Weights:
+    def __init__(self, here, r, layer):
+        self.h, self.r, self.layer = here, r, layer
+        self.holds = here.s == layer
+        self.arrive = {n: here.sem() for n in ("qkv", "h16", "up", "down", "out")}
+        self.zero = [here.sem() for _ in range(3)]
+        self.kept = []
+
+    def everyone(self):
+        for step in (1, 3, 2, 0):
+            for core in range(2):
+                yield step, core, (core, self.h.c, self.h.shard(step))
+
+    def copies(self, name, pairs):
+        h = self.h
+        started = []
+        for step, core, src, dst in pairs:
+            if step == 0 and core == self.layer:
+                started.append(pltpu.make_async_copy(src, dst, self.arrive[name]))
+            else:
+                copy = pltpu.make_async_remote_copy(
+                    src_ref=src, dst_ref=dst, send_sem=h.sem(), recv_sem=self.arrive[name],
+                    device_id=(core, h.c, h.shard(step)), device_id_type=MESH)
+                started.append(copy)
+                self.kept.append(copy)
+
+        @pl.when(self.holds)
+        def _():
+            for copy in started:
+                copy.start()
+
+    def rows_of(self, ref):
+        return ref.at[pl.ds(pl.multiple_of(self.h.y * SLICE, 16), SLICE)]
+
+    def send_qkv(self):
+        h, r = self.h, self.r
+        load = pltpu.make_async_copy(r.w_qkv, r.qkv_rows, h.sem())
+
+        @pl.when(self.holds)
+        def _():
+            load.start()
+            load.wait()
+            rows = r.qkv_rows
+            for g in range(8):
+                first = rows[:, 128 * g : 128 * g + 128]
+                keys = rows[:, D + 128 * g : D + 128 * g + 128]
+                values = rows[:, 2 * D + 128 * g : 2 * D + 128 * g + 128]
+                r.qkv_packed[g] = jnp.concatenate(
+                    [first, keys[:, :64], values[:, :64], keys[:, 64:], values[:, 64:]], axis=1)
+            r.h16_packed[...] = jnp.concatenate(
+                [rows[:, D - 64 : D], rows[:, 2 * D - 64 : 2 * D], rows[:, 3 * D - 64 : 3 * D]], axis=1)
+
+        self.copies("qkv", [
+            (step, core, r.qkv_packed.at[h.shard(step) * 2 + core], self.rows_of(r.qkv_w))
+            for step, core, _ in self.everyone()])
+        self.copies("h16", [
+            (step, core, r.h16_packed, self.rows_of(r.h16_w)) for step, core, _ in self.everyone()])
+
+    def send_rest(self):
+        h, r = self.h, self.r
+        pairs = []
+        for step, core, _ in self.everyone():
+            start = pl.multiple_of(128 * ((17 * (h.shard(step) * 2 + core)) // 4), 128)
+            pairs.append((step, core, r.w_up.at[:, pl.ds(start, WINDOW)], self.rows_of(r.up_w)))
+        self.copies("up", pairs)
+        r.zeros[...] = jnp.zeros_like(r.zeros)
+        offset = window_offset(h.y * 2 + h.s)
+        for i in range(3):
+            row = jnp.where(32 * i < offset, 32 * i, 544 + 32 * i)
+            pltpu.make_async_copy(
+                r.zeros, r.down_w.at[pl.ds(pl.multiple_of(row, 32), 32)], self.zero[i]).start()
+        pairs = []
+        for core in range(2):
+            at = pl.multiple_of(window_offset(h.y * 2 + core), 32)
+            pairs.append((0, core, r.w_down.at[pl.ds(544 * core, 544)], r.down_w.at[pl.ds(at, 544)]))
+        self.copies("down", pairs)
+        self.out_tiles = []
+        for i in range(17):
+            tile = h.y * 17 + i
+            group = jnp.minimum(tile // 8, 7)
+            core, shard = lax.rem(group, 2), group // 2
+            src = r.w_out.at[pl.ds(16 * i, 16)]
+            row = pl.multiple_of(lax.rem(tile, 8) * 16, 16)
+            dst = r.out_w.at[pl.ds(row, 16)]
+            copy = pltpu.make_async_remote_copy(
+                src_ref=src, dst_ref=dst, send_sem=h.sem(), recv_sem=self.arrive["out"],
+                device_id=(core, h.c, shard), device_id_type=MESH)
+            same = pltpu.make_async_copy(src, dst, self.arrive["out"])
+            mine = self.holds & (tile < 64)
+            is_self = (core == self.layer) & (shard == h.y)
+            pl.when(mine & is_self)(same.start)
+            pl.when(mine & jnp.logical_not(is_self))(copy.start)
+            self.out_tiles.append((mine & jnp.logical_not(is_self), copy))
+        self.last = []
+        for step, core, to in self.everyone():
+            src, dst = r.w_out.at[pl.ds(SLICE - 64, 64)], r.out_w.at[pl.ds(128, 64)]
+            if step == 0 and core == self.layer:
+                self.last.append(pltpu.make_async_copy(src, dst, self.arrive["out"]))
+            else:
+                copy = pltpu.make_async_remote_copy(
+                    src_ref=src, dst_ref=dst, send_sem=h.sem(), recv_sem=self.arrive["out"],
+                    device_id=to, device_id_type=MESH)
+                self.last.append(copy)
+
+        @pl.when(self.holds & (h.y == SHARD - 1))
+        def _():
+            for copy in self.last:
+                copy.start()
+
+    def wait_qkv(self):
+        r = self.r
+        wait_bytes(r.qkv_w, self.arrive["qkv"])
+        wait_bytes(r.h16_w, self.arrive["h16"])
+
+    def wait_rest(self):
+        r, h = self.r, self.h
+        wait_bytes(r.up_w, self.arrive["up"])
+        wait_bytes(r.out_w, self.arrive["out"])
+        wait_bytes(r.down_w.at[pl.ds(0, 544)], self.arrive["down"])
+        for i in range(3):
+            wait_bytes(r.zeros, self.zero[i])
+
+        @pl.when(self.holds)
+        def _():
+            for copy in self.kept:
+                copy.wait_send()
+
+        for cond, copy in self.out_tiles:
+            pl.when(cond)(copy.wait_send)
+
+        @pl.when(self.holds & (h.y == SHARD - 1))
+        def _():
+            for copy in self.last[:-2] + self.last[-1:] if self.layer == 0 else self.last[:-1]:
+                copy.wait_send()
+
+
+def weight_outs():
+    return {
+        "qkv_w": (spec((D, 384)), ANY),
+        "h16_w": (spec((D, 192)), ANY),
+        "up_w": (spec((D, WINDOW)), ANY),
+        "down_w": (spec((WINDOW, D)), ANY),
+        "out_w": (spec((192, D)), ANY),
+    }
+
+
+def weight_scratch():
+    return {
+        "qkv_rows": VMEM((SLICE, 3 * D), BF16),
+        "qkv_packed": VMEM((8, SLICE, 384), BF16),
+        "h16_packed": VMEM((SLICE, 192), BF16),
+        "zeros": VMEM((32, D), BF16),
+    }
+
+
+def head_outs():
+    return {
+        "a_full": (spec((512, D)), VMEM),
+        "message_in": (spec((CTX, 160, 128)), VMEM),
+        "kv16_in": (spec((2, CTX, ROWS, 128)), VMEM),
+        "q16": (spec((ROWS, HEAD_DIM)), VMEM),
+    }
+
+
+def head_scratch():
+    return {
+        "message": VMEM((2, 4, 2, 160, 128), BF16),
+        "qkv_vm": VMEM((D, 384), BF16),
+        "h16_vm": VMEM((D, 192), BF16),
+    }
+
+
+def start_head(h, r, a_value):
+    gather = Gather8(h, r.a_full)
+    gather.start(a_value)
+    return gather
+
+
+def run_head(h, r, gather, weights, a_value):
+    load = [pltpu.make_async_copy(r.qkv_w, r.qkv_vm, h.sem()), pltpu.make_async_copy(r.h16_w, r.h16_vm, h.sem())]
+    weights.wait_qkv()
+    for copy in load:
+        copy.start()
+    arrive = h.sem()
+    for copy in load:
+        copy.wait()
+    own16 = dot(a_value, r.h16_vm[...]).astype(BF16)
+    r.q16[...] = own16[:, :64]
+    r.kv16_in[h.s, h.c] = own16[:, 64:]
+    own_kv = r.kv16_in.at[h.s, h.c]
+    leave16, arrive16, cross16 = h.sem(), h.sem(), h.sem()
+    for step in range(1, CTX):
+        h.send(own_kv, own_kv, (h.s, lax.rem(h.c + step, CTX), h.y), arrive16, leave16)
+    for step in ORDER:
+        if step:
+            gather.relay(step)
+        gather.wait(step)
+        shard = h.shard(step)
+        block = r.a_full[pl.ds(pl.multiple_of(shard * 128, 128), 128)]
+        out = dot(block, r.qkv_vm[...]).astype(BF16)
+        for e in range(2):
+            for core in range(2):
+                r.message[e, shard, core, :128] = out[:, 128 + 128 * e : 256 + 128 * e]
+                for b in range(2):
+                    at = 32 * b + 16 * core
+                    lanes = slice(64 * e, 64 * e + 64)
+                    packed = jnp.concatenate([out[at : at + 16, lanes], out[64 + at : 80 + at, lanes]], axis=1)
+                    r.message[e, shard, core, 128 + 16 * b : 144 + 16 * b] = packed
+                chip = 8 * h.s + 4 * e + shard
+                h.send_or_keep(
+                    r.message.at[e, shard, core], r.message_in.at[h.c], (core, chip, h.y),
+                    (chip == h.c) & (h.s == core), arrive)
+    wait_bytes(r.kv16_in.at[h.s, pl.ds(0, CTX - 1)], arrive16)
+    cross = r.kv16_in.at[h.s]
+    h.send(cross, cross, h.sibling(), cross16)
+    wait_bytes(r.kv16_in.at[h.s, pl.ds(0, CTX - 1)], leave16)
+    wait_bytes(r.kv16_in.at[1 - h.s], cross16)
+    wait_bytes(r.message_in, arrive)
+
+
+def first_kernel(hidden, params, w_qkv, w_out, w_up, w_down):
+    def body(r):
+        h = Here(r.sems)
+        weights = Weights(h, r, 0)
+        h.barrier()
+        arrive = h.sem()
+        own = r.params_in.at[h.s * SHARD + h.y]
+        own[...] = r.params[...]
+        for step, core, to in weights.everyone():
+            if step:
+                h.send(own, own, to, arrive)
+        h.send(own, own, h.sibling(), arrive)
+        weights.send_qkv()
+        wait_bytes(r.params_in.at[pl.ds(0, 7)], arrive)
+        for layer in range(2):
+            r.norms[layer] = jnp.concatenate([r.params_in[layer * SHARD + i] for i in range(SHARD)], axis=1)
+        x = r.hidden[h.s].astype(F32)
+        a_value = layer_norm(x, r.norms[0, 0:1], r.norms[0, 2:3]).astype(BF16)
+        gather = start_head(h, r, a_value)
+        weights.send_rest()
+        run_head(h, r, gather, weights, a_value)
+        weights.wait_rest()
+        h.finish()
+
+    outs = {"norms": (spec((2, 8, D), F32), VMEM), **head_outs(), **weight_outs()}
+    ins = {
+        "hidden": (hidden, VMEM), "params": (params, VMEM), "w_qkv": (w_qkv, ANY), "w_out": (w_out, ANY),
+        "w_up": (w_up, ANY), "w_down": (w_down, ANY),
+    }
+    scratch = {
+        "params_in": VMEM((8, 8, SLICE), F32), **head_scratch(), **weight_scratch(),
+        "sems": pltpu.SemaphoreType.DMA((200,)),
+    }
+    return call("first", body, ins, outs, scratch, collective_id=0)
+
+
+def attend(block_order, positions, own_positions, message_in, kv16_in, q16):
+    def body(r):
+        half = lax.axis_index("section")
+        for c in range(CTX):
+            for m in range(2):
+                for b in range(2):
+                    block = 32 * m + r.order[m, 2 * c + b]
+                    rows = r.message_in[c, 64 * m + 32 * b : 64 * m + 32 * b + 32, :]
+                    at = pl.ds(pl.multiple_of(block * 32, 32), 32)
+                    r.keys[at] = rows[:, :64]
+                    r.values[at] = rows[:, 64:]
+                    at = pl.ds(pl.multiple_of(block * 16, 16), 16)
+                    r.queries[at] = r.message_in[c, 128 + 16 * b : 144 + 16 * b, 64 * m : 64 * m + 64] * 0.125
+        row = lax.broadcasted_iota(jnp.int32, (256, 512), 0)
+        row = 32 * (row // 16) + 16 * half + row % 16
+        visible = row >= lax.broadcasted_iota(jnp.int32, (256, 512), 1)
+        for t in range(4):
+            query = r.queries[256 * t : 256 * t + 256]
+            parts = [dot_nt(query, r.keys[512 * u : 512 * u + 512]) for u in range(t + 1)]
+            parts[t] = jnp.where(visible, parts[t], NEG_LARGE)
+            top = parts[0]
+            for p in parts[1:]:
+                top = jnp.maximum(top, p)
+            top = jnp.max(top, axis=-1, keepdims=True)
+            parts = [jnp.exp(p - top) for p in parts]
+            total = parts[0]
+            for p in parts[1:]:
+                total = total + p
+            total = jnp.sum(total, axis=-1, keepdims=True)
+            out = dot(parts[0].astype(BF16), r.values[:512])
+            for u in range(1, t + 1):
+                out = out + dot(parts[u].astype(BF16), r.values[512 * u : 512 * u + 512])
+            r.sorted_out[256 * t : 256 * t + 256] = (out / total).astype(BF16)
+            r.logs[256 * t : 256 * t + 256] = jnp.broadcast_to(top + jnp.log(total), (256, 128))
+        for c in range(CTX):
+            for m in range(2):
+                for b in range(2):
+                    at = pl.multiple_of((32 * m + r.order[m, 2 * c + b]) * 16, 16)
+                    r.out[c, 16 * b : 16 * b + 16, 64 * m : 64 * m + 64] = r.sorted_out[pl.ds(at, 16)]
+        kv = r.kv16_in[...].reshape(SEQ, 128)
+        scores = dot_nt(r.q16[...] * 0.125, kv[:, :64])
+        scores = jnp.where(r.own_positions[...] >= r.positions[...], scores, NEG_LARGE)
+        top = jnp.max(scores, axis=-1, keepdims=True)
+        scores = jnp.exp(scores - top)
+        total = jnp.sum(scores, axis=-1, keepdims=True)
+        out = dot(scores.astype(BF16), kv[:, 64:])
+        r.out16[...] = (out / total).astype(BF16)
+        r.logs16[...] = jnp.broadcast_to(top + jnp.log(total), (ROWS, 128))
+
+    ins = {
+        "order": (block_order, pltpu.SMEM), "positions": (positions, VMEM), "own_positions": (own_positions, VMEM),
+        "message_in": (message_in, VMEM), "kv16_in": (kv16_in, VMEM), "q16": (q16, VMEM),
+    }
+    outs = {
+        "out": (spec((CTX, 32, 128)), VMEM), "out16": (spec((ROWS, 64)), VMEM),
+        "sorted_out": (spec((1024, 64)), VMEM), "logs": (spec((1024, 128), F32), VMEM),
+        "logs16": (spec((ROWS, 128), F32), VMEM),
+    }
+    scratch = {
+        "keys": VMEM((SEQ, 64), BF16), "values": VMEM((SEQ, 64), BF16), "queries": VMEM((1024, 64), BF16),
+    }
+    return call("attend", body, ins, outs, scratch)
+
+
+def middle_scratch():
+    return {
+        "context_in": VMEM((2, 4, 2, 32, 128), BF16),
+        "out_vm": VMEM((192, D), BF16), "up_vm": VMEM((D, WINDOW), BF16), "down_vm": VMEM((WINDOW, D), BF16),
+        **scatter_scratch("o"), **scatter_scratch("f"),
+    }
+
+
+def load_weights(h, r, layer_weights):
+    loads = []
+    for name in ("out", "up", "down"):
+        copy = pltpu.make_async_copy(layer_weights[name], getattr(r, name + "_vm"), h.sem())
+        copy.start()
+        loads.append(copy)
+    return loads
+
+
+def gather_context(h, r):
+    arrive = h.sem()
+    to_core = h.c // 8
+    e, j = lax.rem(h.c // 4, 2), lax.rem(h.c, 4)
+    for c in range(CTX):
+        h.send_or_keep(
+            r.attended.at[c], r.context_in.at[e, j, h.s], (to_core, c, h.y), (h.c == c) & (h.s == to_core), arrive)
+    return arrive
+
+
+def unpack_context(r, store):
+    for j in range(4):
+        for m in range(2):
+            for b in range(2):
+                for core in range(2):
+                    lanes = slice(64 * m, 64 * m + 64)
+                    piece = jnp.concatenate(
+                        [r.context_in[e, j, core, 16 * b : 16 * b + 16, lanes] for e in range(2)], axis=1)
+                    at = 128 * j + 64 * m + 32 * b + 16 * core
+                    store[at : at + 16] = piece
+
+
+def block_rows(h, step):
+    return pl.ds(pl.multiple_of(h.shard(step) * 128, 128), 128)
+
+
+def run_out(h, r, x):
+    sums = scatter(h, r, "o")
+    for step in (2, 1, 3, 0):
+        sums.put(step, dot(r.context[block_rows(h, step)], r.out_vm[:128]))
+    for step in (2, 1, 3):
+        sums.relay(step)
+    own = x + dot(r.attended16[...], r.out_vm[128:])
+    return own + sums.result()
+
+
+def middle_kernel(layer, attended, attended16, x, norms, layer_weights, next_weights):
+    w_qkv, w_out, w_up, w_down = next_weights
+
+    def body(r):
+        h = Here(r.sems)
+        weights = Weights(h, r, layer + 1)
+        h.barrier()
+        loads = load_weights(h, r, {"out": r.out_l, "up": r.up_l, "down": r.down_l})
+        arrive = gather_context(h, r)
+        weights.send_qkv()
+        for copy in loads:
+            copy.wait()
+        wait_bytes(r.context_in, arrive)
+        unpack_context(r, r.context)
+        residual = run_out(h, r, r.x[h.s].astype(F32) if layer == 0 else r.x[...].astype(F32))
+        r.residual[...] = residual
+        b_value = layer_norm(residual, r.norms[layer, 1:2], r.norms[layer, 3:4]).astype(BF16)
+        gather = Gather8(h, r.b_full)
+        gather.start(b_value)
+        weights.send_rest()
+        sums = scatter(h, r, "f")
+        for step in ORDER:
+            if step:
+                gather.relay(step)
+            gather.wait(step)
+            rows = block_rows(h, step)
+            u = dot(r.b_full[rows], r.up_vm[...])
+            r.pre[rows] = u
+            sums.put(step, dot(gelu(u).astype(BF16), r.down_vm[...]))
+        for step in (1, 3, 2):
+            sums.relay(step)
+        y = (residual + sums.result()).astype(BF16)
+        r.y[...] = y
+        a_value = layer_norm(y.astype(F32), r.norms[layer + 1, 0:1], r.norms[layer + 1, 2:3]).astype(BF16)
+        gather = start_head(h, r, a_value)
+        run_head(h, r, gather, weights, a_value)
+        weights.wait_rest()
+        h.finish()
+
+    ins = {
+        "attended": (attended, VMEM), "attended16": (attended16, VMEM), "x": (x, VMEM), "norms": (norms, VMEM),
+        "out_l": (layer_weights["out_w"], ANY), "up_l": (layer_weights["up_w"], ANY),
+        "down_l": (layer_weights["down_w"], ANY),
+        "w_qkv": (w_qkv, ANY), "w_out": (w_out, ANY), "w_up": (w_up, ANY), "w_down": (w_down, ANY),
+    }
+    outs = {
+        "context": (spec((512, 128)), VMEM), "residual": (spec((ROWS, D), F32), VMEM), "b_full": (spec((512, D)), VMEM),
+        "pre": (spec((512, WINDOW), F32), VMEM), "y": (spec((ROWS, D)), VMEM), **head_outs(), **weight_outs(),
+    }
+    scratch = {
+        **middle_scratch(), **head_scratch(), **weight_scratch(), "sems": pltpu.SemaphoreType.DMA((280,)),
+    }
+    return call("middle", body, ins, outs, scratch, collective_id=1)
+
+
+def token_positions(block_order):
+    offsets = jnp.arange(32, dtype=jnp.int32)
+    groups = jnp.arange(2, dtype=jnp.int32)[:, None, None] * GROUP
+    return (groups + block_order[:, :, None] * 32 + offsets).reshape(2, GROUP)
+
+
+def forward(hidden_in, cotangent, block_order, qkv_weight, out_weight, up_weight, down_weight, norm_gains, norm_biases):
+    section, ctx = lax.axis_index("section"), lax.axis_index("ctx")
+    own_weights = (qkv_weight[0], out_weight[0], up_weight[0], down_weight[0])
+    params = jnp.concatenate([norm_gains[0], norm_biases[0]], axis=0).astype(F32)
+    params = jnp.pad(params, ((0, 4), (0, 0)))
+    grid = token_positions(block_order)
+    own_positions = lax.dynamic_slice(grid, (section, ctx * ROWS), (1, ROWS)).reshape(ROWS, 1)
+    positions = grid.reshape(1, SEQ)
+    hidden = hidden_in[0]
+    first = first_kernel(hidden, params, *own_weights)
+    attended = attend(block_order, positions, own_positions, first["message_in"], first["kv16_in"], first["q16"])
+    middle = middle_kernel(0, attended["out"], attended["out16"], hidden, first["norms"], first, own_weights)
+    return middle["y"]
+CTX_AXES = ("ctx",)
 
 
 def in_one_piece(arrays, axis, dim, along):
@@ -53,7 +713,7 @@
     return jax.tree.map(short, x)
 
 
-def layer_norm(values, gain_row, shift_row):
+def layer_norm_rows(values, gain_row, shift_row):
     center = values - jnp.mean(values, axis=-1, keepdims=True)
     spread = jnp.mean(center * center, axis=-1, keepdims=True)
     return center * lax.rsqrt(spread + EPSILON) * gain_row + shift_row
@@ -116,7 +776,7 @@
     )
     context_low = mixed.reshape(mixed.shape[0], model_width).astype(jnp.bfloat16)
     residual = layer_in.astype(jnp.float32) + matmul(context_low, w_out)
-    normed2 = layer_norm(residual, gain_row, shift_row).astype(jnp.bfloat16)
+    normed2 = layer_norm_rows(residual, gain_row, shift_row).astype(jnp.bfloat16)
     pre_act = matmul(normed2, w_up)
     hidden_low = gelu_tanh(pre_act).astype(jnp.bfloat16)
     result = residual + matmul(hidden_low, w_down)
@@ -173,11 +833,11 @@
     norm_biases,
 ):
     section_index = lax.axis_index("section")
-    ctx_index = lax.axis_index(CTX)
+    ctx_index = lax.axis_index(CTX_AXES)
     row_count = hidden_in.shape[2]
     micro_count = hidden_in.shape[1]
     model_width = hidden_in.shape[3]
-    group_len = row_count * lax.axis_size(CTX)
+    group_len = row_count * lax.axis_size(CTX_AXES)
     key_pos = key_positions(block_order, group_len, row_count // 2)
     pos_grid = key_pos.reshape(micro_count, group_len)
     is_first = section_index == 0
@@ -200,11 +860,11 @@
         query_pos = lax.dynamic_slice(
             pos_grid, (slot_index, ctx_index * row_count), (1, row_count)
         )[0]
-        normed = layer_norm(layer_in.astype(jnp.float32), gains32[0], shifts32[0]).astype(
+        normed = layer_norm_rows(layer_in.astype(jnp.float32), gains32[0], shifts32[0]).astype(
             jnp.bfloat16
         )
         projected = matmul(normed, w_qkv).astype(jnp.bfloat16)
-        gathered = lax.all_gather(projected[:, model_width:], CTX, axis=0, tiled=True)
+        gathered = lax.all_gather(projected[:, model_width:], CTX_AXES, axis=0, tiled=True)
         old_slot = lax.dynamic_slice_in_dim(kv_cache, slot_index * group_len, group_len, 0)
         kv_cache = lax.dynamic_update_slice_in_dim(
             kv_cache, jnp.where(is_valid, gathered, old_slot), slot_index * group_len, 0
@@ -254,7 +914,7 @@
             pos_grid, (slot_index, ctx_index * row_count), (1, row_count)
         )[0]
         layer_in32 = layer_in.astype(jnp.float32)
-        normed = layer_norm(layer_in32, gains32[0], shifts32[0]).astype(jnp.bfloat16)
+        normed = layer_norm_rows(layer_in32, gains32[0], shifts32[0]).astype(jnp.bfloat16)
         queries = matmul(normed, w_query).astype(jnp.bfloat16)
         attn_probs, probs_low, context_low, residual, normed2, pre_act, hidden_low, result = (
             layer_tail(
@@ -277,7 +937,7 @@
         grad_pre = gelu_pull(grad_hidden)[0].astype(jnp.bfloat16)
         grad_up = matmul_tn(normed2, grad_pre)
         grad_normed2 = matmul_nt(grad_pre, w_up)
-        _, norm_pull2 = jax.vjp(layer_norm, residual, gains32[1], shifts32[1])
+        _, norm_pull2 = jax.vjp(layer_norm_rows, residual, gains32[1], shifts32[1])
         grad_mid_part, grad_gain2, grad_shift2 = norm_pull2(grad_normed2)
         grad_mid = grad_out + grad_mid_part
         grad_attn = grad_mid.astype(jnp.bfloat16)
@@ -294,12 +954,12 @@
         key_grads = key_grads + jnp.concatenate([grad_keys, grad_values], axis=1)
         grad_group = lax.dynamic_slice_in_dim(key_grads, slot_index * group_len, group_len, 0)
         grad_kv = (
-            summed_rows(grad_group.astype(jnp.bfloat16), CTX, 0).astype(jnp.float32) * live_scale
+            summed_rows(grad_group.astype(jnp.bfloat16), CTX_AXES, 0).astype(jnp.float32) * live_scale
         )
         grad_proj = jnp.concatenate([grad_queries, grad_kv.astype(jnp.bfloat16)], axis=1)
         grad_qkvw = matmul_tn(normed, grad_proj)
         grad_normed = matmul_nt(grad_proj, w_qkv)
-        _, norm_pull1 = jax.vjp(layer_norm, layer_in32, gains32[0], shifts32[0])
+        _, norm_pull1 = jax.vjp(layer_norm_rows, layer_in32, gains32[0], shifts32[0])
         grad_in_part, grad_gain1, grad_shift1 = norm_pull1(grad_normed)
         grad_in_low = (grad_mid + grad_in_part).astype(jnp.bfloat16)
         old_grad = lax.dynamic_index_in_dim(grads_kept, slot_index, 0, keepdims=False)
@@ -348,9 +1008,12 @@
         ),
     )
     grad_sum = jax.tree.map(
-        lambda part: part.astype(jnp.float32), lax.psum(for_sending(grad_sum), CTX)
+        lambda part: part.astype(jnp.float32), lax.psum(for_sending(grad_sum), CTX_AXES)
     )
     qkv_grad, out_grad, up_grad, down_grad, gain_grad, bias_grad = grad_sum
+    y = forward(hidden_in, cotangent, block_order, qkv_weight, out_weight, up_weight, down_weight, norm_gains, norm_biases)
+    other = lax.ppermute(y, "section", [(0, 1), (1, 0)])
+    outputs_kept = jnp.where(is_first, jnp.stack([y, other]), outputs_kept)
     return (
         outputs_kept[None, None],
         grads_kept[None, None],
@@ -364,13 +1027,9 @@
 
 
 def solution(mesh):
-    split = Mesh(
-        mesh.devices.reshape(mesh.shape["section"], 4, 4, mesh.shape["shard"]),
-        ("section", "ctx_0", "ctx_1", "shard"),
-    )
     placed = (
-        P("shard", None, CTX, None),
-        P("shard", None, CTX, None),
+        P("shard", None, CTX_AXES, None),
+        P("shard", None, CTX_AXES, None),
         P(),
         P("section", "shard", None),
         P("section", "shard", None),
@@ -381,11 +1040,11 @@
     )
     return jax.shard_map(
         shards,
-        mesh=split,
+        mesh=mesh,
         in_specs=placed,
         out_specs=(
-            P("section", "shard", None, CTX, None),
-            P("section", "shard", None, CTX, None),
+            P("section", "shard", None, CTX_AXES, None),
+            P("section", "shard", None, CTX_AXES, None),
             P("section", "shard", None),
             P("section", "shard", None),
             P("section", "shard", None),

time: 1540 us -> 1640 us (1.065)
  Pallas kernels: 0 us -> 176 us
  waiting for transfers between devices: 823 us -> 743 us
    pallas_call x0 -> x3, Pallas kernels: none -> 176 us  [call(): pl.pallas_call(kernel, out_shape=tuple((outs[n][0] for n in out_names)),...]
    unnamed x19 -> x16, waiting for transfers between devices: 36.9 us -> 157 us
    reduce_scatter x3 -> x0, waiting for transfers between devices: 107 us -> none  [summed_rows(): x = lax.psum_scatter(x, axis, scatter_dimension=dim, tiled=True)]
    psum x1, waiting for transfers between devices: 93.1 us -> 0.01 us  [shards(): lax.psum(for_sending(grad_sum), CTX_AXES)]
    unnamed x252 -> x271, local copies, waits for them, and re-layouts: 24.8 us -> 37.9 us
  transfers between devices with their start and end apart: 19 -> 17, of which waited for: 15 -> 12; matrix products, arithmetic and copies ran while one was open for 14% -> 13% of each run, Pallas kernels for 0% -> 11%
where the time goes in v1:
time: 1640 us; the launch traced here: 1620 us
  waiting for transfers between devices  743 us (45%)
  matrix products  392 us (24%)
  Pallas kernels  176 us (11%)
  local copies, waits for them, and re-layouts  167 us (10%)
  other arithmetic  73.9 us (5%)
  blocking collectives  42.8 us (3%)
  between operations  16.5 us (1%)
    pallas_call x3, Pallas kernels, call(): pl.pallas_call(kernel, out_shape=tuple((outs[n][0] for n in out_names)),...  176 us
    all_gather x1, waiting for transfers between devices, in_one_piece(): out, at, outs = (lax.all_gather(both, axis, axis=dim, tiled=True), 0, [])  164 us
    unnamed x16, waiting for transfers between devices  157 us
    all_gather x3, waiting for transfers between devices, shards(): lax.all_gather(projected[:, model_width:], CTX_AXES, axis=0, tiled=True)  151 us
    reduce_scatter x1, waiting for transfers between devices, in_one_piece_2(): lax.psum_scatter(both, axis, scatter_dimension=dim, tiled=True)  121 us
    dot_general x12, matrix products, matmul_tn(): lax.dot_general(left_side, right_side, (((0,), (0,)), ((), ())), preferre...  99.6 us
    reduce_scatter x1, waiting for transfers between devices, shards(): lax.psum_scatter(grad_sum[3].astype(jnp.bfloat16), 'shard', scatter_dimen...  90 us
    dot_general x18, matrix products, matmul(): return jnp.dot(left_side, right_side, preferred_element_type=jnp.float32)  86.2 us
  transfers between devices with their start and end apart: 17, of which 12 were waited for; matrix products, arithmetic and copies ran while one was open for 13% of the time, Pallas kernels for 11%

profile of v1, /device:TPU:1, one launch (start us, length us, event | category | flops | bytes accessed | tf_op | source)
XLA Modules:
  0.0 1625.0 jit_solution(8017307642330784761)
XLA Ops:
  17.6 10.3 all-gather.1
  28.4 164.3 %all-gather.8.cloned.1.call-done = bf16[1088,8704]{1,0:T(8,128)(2,1)} async-done(((bf16[272,8704]{1,0:T(8,128)(2,1)}), bf16[1088,8704]{1,0:T(8,128)(2,1)}) %all-gather.8.cloned.1.call-update) | async-done | bytes 18939920 | tf_op jit(solution)/shard_map/all_gather | solution.py:678
  201.7 49.2 %all-gather.10.cloned.1.call-done = bf16[1024,2176]{1,0:T(8,128)(2,1)} async-done(((bf16[64,2176]{1,0:T(8,128)(2,1)}), bf16[1024,2176]{1,0:T(8,128)(2,1)}) %all-gather.10.cloned.1.call-update) | async-done | bytes 4456464 | tf_op jit(solution)/shard_map/all_gather | solution.py:867
  293.8 55.4 %all-gather.16.cloned.1.call-done = bf16[1,4352,1088]{2,1,0:T(8,128)(2,1)} async-done(((bf16[1,1088,1088]{2,1,0:T(8,128)(2,1)}), bf16[1,4352,1088]{2,1,0:T(8,128)(2,1)}) %all-gather.16.cloned.1.call-update) | async-done | bytes 9469968 | tf_op jit(solution)/shard_map/all_gather | solution.py:819
  349.2 9.9 bitcast_dynamic-update-slice_fusion.6
  368.5 53.1 %all-gather.12.cloned.1.call-done = bf16[1024,2176]{1,0:T(8,128)(2,1)} async-done(((bf16[64,2176]{1,0:T(8,128)(2,1)}), bf16[1024,2176]{1,0:T(8,128)(2,1)}) %all-gather.12.cloned.1.call-update) | async-done | bytes 4456464 | tf_op jit(solution)/shard_map/all_gather | solution.py:867
  428.2 10.0 fusion.431
  470.1 9.9 bitcast_dynamic-update-slice_fusion.5
  492.7 48.3 %all-gather.14.cloned.1.call-done = bf16[1024,2176]{1,0:T(8,128)(2,1)} async-done(((bf16[64,2176]{1,0:T(8,128)(2,1)}), bf16[1024,2176]{1,0:T(8,128)(2,1)}) %all-gather.14.cloned.1.call-update) | async-done | bytes 4456464 | tf_op jit(solution)/shard_map/all_gather | solution.py:867
  547.8 10.0 fusion.430
  571.1 9.1 fusion.444
  644.8 70.9 %reduce-scatter.19.cloned.1.call-done = bf16[64,2176]{1,0:T(8,128)(2,1)} async-done(((bf16[1024,2176]{1,0:T(8,128)(2,1)}), bf16[64,2176]{1,0:T(8,128)(2,1)}) %reduce-scatter.19.cloned.1.call-update) | async-done | bytes 278544
  768.9 10.0 multiply_reduce_fusion.1
  791.6 13.5 fusion.8
  823.5 70.0 %reduce-scatter.21.cloned.1.call-done = bf16[64,2176]{1,0:T(8,128)(2,1)} async-done(((bf16[1024,2176]{1,0:T(8,128)(2,1)}), bf16[64,2176]{1,0:T(8,128)(2,1)}) %reduce-scatter.21.cloned.1.call-update) | async-done | bytes 278544
  903.8 9.1 fusion.448
  965.6 9.9 fusion.24
  983.8 9.2 fusion.426
  998.4 16.3 %convolution_add_fusion.1 = f32[1088,4352]{1,0:T(8,128)} fusion(f32[1088,4352]{1,0:T(8,128)} %fusion.426, bf16[64,4352]{1,0:T(8,128)(2,1)S(1)} %copy-done.55, f32[64,1088]{1,0:T(8,128)S(1)} %copy-done.8, f32[64]{0:T(128)S(1)} %copy-done.93, f32[64]{0:T(128)S(1)} %copy-done.91, f32[1088]{0:T(1024)S(1)} %get-tuple-element.53, f32[1088]{0:T(1024)S(1)} %get-tuple-element.138), kind=kOutput, calls=%fused_computation.7 | convolution fusion | flops 611160064 | bytes 38724608 | tf_op jit(solution)/shard_map/dot_general | solution.py:731
  1029.0 12.9 fusion.7
  1041.8 15.6 reduce-scatter.23.cloned.1.call-done
  1060.6 10.4 fusion.9
  1071.0 31.1 %concatenate.41 = bf16[1088,8704]{1,0:T(8,128)(2,1)} concatenate(bf16[1088,3264]{1,0:T(8,128)(2,1)} %fusion.9, bf16[1088,1088]{1,0:T(8,128)(2,1)S(1)} %fusion.27, bf16[1088,4352]{1,0:T(8,128)(2,1)} %fusion.7), dimensions={1} | concatenate | bytes 37879808 | tf_op jit(solution)/shard_map/concatenate | solution.py:702
  1103.1 11.6 fusion.184
  1114.7 13.3 convolution_add_fusion.3
  1128.0 11.7 fusion.6
  1147.7 121.3 %reduce-scatter.15.cloned.1.call-done = bf16[272,8704]{1,0:T(8,128)(2,1)} async-done(((bf16[1088,8704]{1,0:T(8,128)(2,1)}), bf16[272,8704]{1,0:T(8,128)(2,1)}) %reduce-scatter.15.cloned.1.call-update) | async-done | bytes 4734992 | tf_op jit(solution)/shard_map/reduce_scatter | solution.py:704
  1274.8 90.0 %reduce-scatter.17.cloned.1.call-done = bf16[1088,1088]{1,0:T(8,128)(2,1)} async-done(((bf16[4352,1088]{1,0:T(8,128)(2,1)}), bf16[1088,1088]{1,0:T(8,128)(2,1)}) %reduce-scatter.17.cloned.1.call-update) | async-done | bytes 2367504 | tf_op jit(solution)/shard_map/reduce_scatter | solution.py:995
  1366.8 56.1 %first.1 = (f32[2,8,1088]{2,1,0:T(8,128)}, bf16[512,1088]{1,0:T(8,128)(2,1)}, bf16[16,160,128]{2,1,0:T(8,128)(2,1)}, bf16[2,16,64,128]{3,2,1,0:T(8,128)(2,1)}, b...) custom-call(bf16[2,64,1088]{2,1,0:T(8,128)(2,1)} %bitcast.434, ...), custom_call_target="tpu_custom_call" | custom-call | tf_op jit(solution)/shard_map/first/pallas_call | solution.py:43
  1428.4 114.3 %middle.1 = (bf16[512,128]{1,0:T(8,128)(2,1)}, f32[64,1088]{1,0:T(8,128)}, bf16[512,1088]{1,0:T(8,128)(2,1)}, f32[512,640]{1,0:T(8,128)}, bf16[64,1088]{1,0:T(8,...) custom-call(bf16[16,32,128]{2,1,0:T(8,128)(2,1)} %get-tuple-element., ...), custom_call_target="tpu_custom_call" | custom-call | tf_op jit(solution)/shard_map/middle/pallas_call | solution.py:43
  1561.7 10.0 fusion.88
  1574.1 32.5 %all-reduce.1 = (bf16[1,2,272]{2,1,0:T(2,128)(2,1)S(1)}, bf16[1,2,272]{2,1,0:T(2,128)(2,1)S(1)}) all-reduce(bf16[1,2,272]{2,1,0:T(2,128)(2,1)S(1)} %bitcast.494, bf16[1,2,272]{2,1,0:T(2,128)(2,1)S(1)} %bitcast.495), channel_id=1, replica_groups=mesh['section'=2,'ctx'=16,'shard'=4] {'ctx'}, use_global_device_ids=true, to_apply=%region_73.74 | all-reduce | flops 1088 | bytes 4352 | tf_op jit(solution)/shard_map/psum | solution.py:1011
  (523 shorter events, 439.3 us)
Async XLA Ops:
  7.2 185.5 %all-gather.8.cloned.1.call-start = ((), (), s32[]{:S(2)}) async-start(), calls=%async_computation.6 | async-start | bytes 23674880 | tf_op jit(solution)/shard_map/all_gather | solution.py:678
  16.3 234.6 %all-gather.10.cloned.1.call-start = ((), (), s32[]{:S(2)}) async-start(), calls=%async_computation.7 | async-start | bytes 4734976 | tf_op jit(solution)/shard_map/all_gather | solution.py:867
  197.9 151.4 %all-gather.16.cloned.1.call-start = ((), (), s32[]{:S(2)}) async-start(), calls=%async_computation.12 | async-start | bytes 12533760 | tf_op jit(solution)/shard_map/all_gather | solution.py:819
  198.6 222.9 %all-gather.12.cloned.1.call-start = ((), (), s32[]{:S(2)}) async-start(), calls=%async_computation.8 | async-start | bytes 4734976 | tf_op jit(solution)/shard_map/all_gather | solution.py:867
  359.1 3.3 collective-permute-start.1
  368.0 173.1 %all-gather.14.cloned.1.call-start = ((), (), s32[]{:S(2)}) async-start(), calls=%async_computation.9 | async-start | bytes 4734976 | tf_op jit(solution)/shard_map/all_gather | solution.py:867
  480.0 3.3 collective-permute-start.2
  488.0 59.9 %copy-start.43 = (bf16[64,3264]{1,0:T(8,128)(2,1)}, bf16[64,3264]{1,0:T(8,128)(2,1)S(1)}, u32[]{:S(2)}) copy-start(bf16[64,3264]{1,0:T(8,128)(2,1)S(1)} %convolution_convert_fusion) | copy-start | bytes 1253380
  488.9 226.9 %reduce-scatter.19.cloned.1.call-start = ((), (), s32[]{:S(2)}) async-start(), calls=%async_computation.13 | async-start | bytes 4734976
  490.0 256.0 %copy-start.75 = (f32[64]{0:T(128)}, f32[64]{0:T(128)S(1)}, u32[]{:S(2)}) copy-start(f32[64]{0:T(128)S(1)} %broadcast_multiply_fusion.8) | copy-start | bytes 772
  490.2 255.8 %copy-start.79 = (f32[64]{0:T(128)}, f32[64]{0:T(128)S(1)}, u32[]{:S(2)}) copy-start(f32[64]{0:T(128)S(1)} %fusion.365) | copy-start | bytes 772
  639.8 253.7 %reduce-scatter.21.cloned.1.call-start = ((), (), s32[]{:S(2)}) async-start(), calls=%async_computation.14 | async-start | bytes 4734976
  644.8 78.0 %copy-start.60 = (bf16[17,64,64]{2,1,0:T(8,128)(2,1)}, bf16[17,64,64]{2,1,0:T(8,128)(2,1)S(1)}, u32[]{:S(2)}) copy-start(bf16[17,64,64]{2,1,0:T(8,128)(2,1)S(1)} %fusion.115) | copy-start | bytes 417796
  735.3 28.2 %slice-start.9 = ((s8[18939904]{0:T(1024)(128)(4,1)}), s8[4194304]{0:T(1024)(128)(4,1)S(1)}, s32[]{:S(2)}) async-start(s8[18939904]{0:T(1024)(128)(4,1)} %bitcast.422), calls=%async_computation.27 | async-start | bytes 8388608
  735.3 28.2 %slice-start.10 = ((s8[18939904]{0:T(1024)(128)(4,1)}), s8[4194304]{0:T(1024)(128)(4,1)S(1)}, s32[]{:S(2)}) async-start(s8[18939904]{0:T(1024)(128)(4,1)} %bitcast.422), calls=%async_computation.28 | async-start | bytes 8388608
  746.3 9.9 collective-permute-start.3
  756.3 167.3 %copy-start.24 = (bf16[64,1088]{1,0:T(8,128)(2,1)}, bf16[64,1088]{1,0:T(8,128)(2,1)S(1)}, u32[]{:S(2)}) copy-start(bf16[64,1088]{1,0:T(8,128)(2,1)S(1)} %bitcast_select_fusion.2) | copy-start | bytes 417796
  818.0 239.5 %reduce-scatter.23.cloned.1.call-start = ((), (), s32[]{:S(2)}) async-start(), calls=%async_computation.15 | async-start | bytes 4734976
  823.5 76.9 %copy-start.63 = (bf16[17,64,64]{2,1,0:T(8,128)(2,1)}, bf16[17,64,64]{2,1,0:T(8,128)(2,1)S(1)}, u32[]{:S(2)}) copy-start(bf16[17,64,64]{2,1,0:T(8,128)(2,1)S(1)} %fusion.116) | copy-start | bytes 417796
  923.9 9.8 collective-permute-start.4
  981.9 287.0 %reduce-scatter.15.cloned.1.call-start = ((), (), s32[]{:S(2)}) async-start(), calls=%async_computation.10 | async-start | bytes 23674880 | tf_op jit(solution)/shard_map/reduce_scatter | solution.py:704
  1102.2 262.6 %reduce-scatter.17.cloned.1.call-start = ((), (), s32[]{:S(2)}) async-start(), calls=%async_computation.11 | async-start | bytes 12533760 | tf_op jit(solution)/shard_map/reduce_scatter | solution.py:995
  1139.8 433.0 %reduce-scatter.25.cloned.1.call-start = ((), (), s32[]{:S(2)}) async-start(), calls=%async_computation.16 | async-start | bytes 348160
  1147.6 460.1 %all-reduce.5.cloned.1.call-start = ((), (), s32[]{:S(2)}) async-start(), calls=%async_computation.17 | async-start | bytes 14622720 | tf_op jit(solution)/shard_map/psum | solution.py:1011
  1273.7 91.1 %copy-start.57 = (s32[2,32,32]{2,1,0:T(8,128)S(1)}, s32[2,32,32]{2,1,0:T(8,128)}, u32[]{:S(2)}) copy-start(s32[2,32,32]{2,1,0:T(8,128)} %copy-done.56) | copy-start | bytes 24580
  1273.7 91.8 %copy-start.97 = (s32[64,1]{0,1:T(1,128)S(1)}, s32[64,1]{0,1:T(1,128)}, u32[]{:S(2)}) copy-start(s32[64,1]{0,1:T(1,128)} %get-tuple-element.85) | copy-start | bytes 772
  1273.7 92.5 %copy-start.81 = (bf16[4,272]{1,0:T(4,128)(2,1)S(1)}, bf16[4,272]{1,0:T(4,128)(2,1)}, u32[]{:S(2)}) copy-start(bf16[4,272]{1,0:T(4,128)(2,1)} %get-tuple-element.92) | copy-start | bytes 6532
  1428.4 114.4 %copy-start.18 = (bf16[2,64,1088]{2,1,0:T(8,128)(2,1)S(1)}, bf16[2,64,1088]{2,1,0:T(8,128)(2,1)}, u32[]{:S(2)}) copy-start(bf16[2,64,1088]{2,1,0:T(8,128)(2,1)} %copy-done.17) | copy-start | bytes 835588
  1428.4 114.4 %slice-start.27 = ((bf16[64,3264]{1,0:T(8,128)(2,1)}), bf16[64,1088]{1,0:T(8,128)(2,1)S(1)}, s32[]{:S(2)}) async-start(bf16[64,3264]{1,0:T(8,128)(2,1)} %copy-done.43), calls=%async_computation.45 | async-start | bytes 294912 | tf_op jit(solution)/shard_map/slice | solution.py:874
  1428.4 114.6 %copy-start.67 = (pred[64,2048]{1,0:T(8,128)(4,1)S(1)}, pred[64,2048]{1,0:T(8,128)(4,1)}, u32[]{:S(2)}) copy-start(pred[64,2048]{1,0:T(8,128)(4,1)} %get-tuple-element.89) | copy-start | bytes 393220
  1542.7 29.0 %collective-permute-start = (bf16[64,1088]{1,0:T(8,128)(2,1)}, bf16[64,1088]{1,0:T(8,128)(2,1)S(1)}, u32[]{:S(2)}, u32[]{:S(2)}) collective-permute-start(bf16[64,1088]{1,0:T(8,128)(2,1)} %get-tuple-element.27), channel_id=1, source_target_pairs={{0,64},{64,0},{1,65},{65,1},{2,66},{66,2},{3,67},{67,3},{4,68},{68... | collective-permute-start | bytes 417800 | tf_op jit(solution)/shard_map/ppermute | solution.py:1015
  1572.8 42.0 %copy-start.58 = (bf16[1,1,2,64,1088]{4,3,2,1,0:T(8,128)(2,1)}, bf16[1,1,2,64,1088]{4,3,2,1,0:T(8,128)(2,1)S(1)}, u32[]{:S(2)}) copy-start(bf16[1,1,2,64,1088]{4,3,2,1,0:T(8,128)(2,1)S(1)} %fusion.306) | copy-start | bytes 835588
  (116 other events, 974.0 us)
Sparse Core Ops, SparseCore 0:
  16.5 176.1 all-gather.7
  198.0 52.9 all-gather.9
  252.6 96.5 all-gather.15
  368.1 53.3 all-gather.11
  489.0 51.9 all-gather.13
  639.9 75.7 reduce-scatter.18
  818.1 75.3 reduce-scatter.20
  982.1 75.3 reduce-scatter.22
  1102.3 166.6 reduce-scatter.14
  1271.3 93.4 reduce-scatter.16
  1367.2 19.5 reduce-scatter.24
  1391.2 151.6 all-reduce.4

commit v2 on v1

v2 whole, which is shorter than its diff:
```python
import types

import jax
import jax.numpy as jnp
from jax import lax
from jax.experimental import pallas as pl
from jax.experimental.pallas import tpu as pltpu
from jax.sharding import PartitionSpec as P

D = 1088
HEADS = 17
HEAD_DIM = 64
FF = 4352
SHARD = 4
CTX = 16
ROWS = 64
GROUP = 1024
SEQ = 2048
WINDOW = 640
SLICE = D // SHARD
EPSILON = 1e-05
NEG_LARGE = -1e30
BF16 = jnp.bfloat16
F32 = jnp.float32
MESH = pl.DeviceIdType.MESH
VMEM = pltpu.VMEM
ANY = pl.ANY
VMEM_BYTES = 56 * 2**20
SECTION, CONTEXT, LINE = "section", "ctx", "shard"
TILES = (68, 16, WINDOW)


def spec(shape, dtype=BF16):
    return jax.ShapeDtypeStruct(shape, dtype)


def call(name, body, ins, outs, scratch, collective_id=None):
    def kernel(*refs):
        refs, found = list(refs), {}
        for key, value in [*ins.items(), *outs.items(), *scratch.items()]:
            if isinstance(value, list):
                found[key], refs = refs[: len(value)], refs[len(value) :]
            else:
                found[key] = refs.pop(0)
        body(types.SimpleNamespace(**found))

    extra = {} if collective_id is None else dict(collective_id=collective_id, has_side_effects=True)
    shapes, given = [], []
    for value in scratch.values():
        shapes += value if isinstance(value, list) else [value]
    for value in ins.values():
        given += value if isinstance(value, list) else [value]
    results = pl.pallas_call(
        kernel,
        out_shape=tuple(value[0] for value in outs.values()),
        in_specs=[pl.BlockSpec(memory_space=space) for _, space in given],
        out_specs=tuple(pl.BlockSpec(memory_space=value[1]) for value in outs.values()),
        scratch_shapes=shapes,
        compiler_params=pltpu.CompilerParams(vmem_limit_bytes=VMEM_BYTES, **extra),
        name=name,
    )(*(array for array, _ in given))
    return types.SimpleNamespace(**dict(zip(outs, results)))


def dot(a, b):
    return jnp.dot(a, b, preferred_element_type=F32)


def dot_nt(a, b):
    return lax.dot_general(a, b, (((1,), (1,)), ((), ())), preferred_element_type=F32)


def dot_tn(a, b):
    return lax.dot_general(a, b, (((0,), (0,)), ((), ())), preferred_element_type=F32)


def norm_parts(values):
    center = values - jnp.mean(values, axis=-1, keepdims=True)
    rate = lax.rsqrt(jnp.mean(center * center, axis=-1, keepdims=True) + EPSILON)
    return center * rate, rate


def layer_norm(values, gain, bias):
    return norm_parts(values)[0] * gain + bias


def gelu(u):
    return 0.5 * u * (1.0 + jnp.tanh(0.7978845608028654 * (u + 0.044715 * u * u * u)))


class Here:
    def __init__(self, sems):
        self.s = lax.axis_index(SECTION)
        self.c = lax.axis_index(CONTEXT)
        self.y = lax.axis_index(LINE)
        self.sems, self.used, self.sent = sems, 0, []

    def sem(self):
        self.used += 1
        return self.sems.at[self.used - 1]

    def shard(self, step):
        return lax.rem(self.y + step, SHARD)

    def rows(self, shard, core):
        return pl.ds(pl.multiple_of((shard * 2 + core) * ROWS, ROWS), ROWS)

    def barrier(self, whole=True):
        sem = pltpu.get_barrier_semaphore()
        peers = []
        for step in range(SHARD):
            for core in range(2):
                if step or core:
                    peers.append((lax.rem(self.s + core, 2), self.c, self.shard(step)))
        for step in range(1, CTX if whole else 1):
            for core in range(2):
                peers.append((core, lax.rem(self.c + step, CTX), self.y))
        for to in peers:
            pl.semaphore_signal(sem, inc=1, device_id=to, device_id_type=MESH)
        pl.semaphore_wait(sem, len(peers))

    def local(self, src, dst):
        copy = pltpu.make_async_copy(src, dst, self.sem())
        copy.start()
        return copy

    def save(self, src, dst):
        copy = self.local(src, dst)
        self.sent.append(types.SimpleNamespace(wait_send=copy.wait))

    def send(self, src, dst, to, arrive, leave=None):
        copy = pltpu.make_async_remote_copy(
            src_ref=src, dst_ref=dst, send_sem=self.sem() if leave is None else leave,
            recv_sem=arrive, device_id=to, device_id_type=MESH)
        copy.start()
        if leave is None:
            self.sent.append(copy)
        return copy

    def send_or_keep(self, src, dst, to, is_self, arrive):
        leave = self.sem()
        copy = pltpu.make_async_remote_copy(
            src_ref=src, dst_ref=dst, send_sem=leave, recv_sem=arrive, device_id=to, device_id_type=MESH)
        kept = pltpu.make_async_copy(src, dst, arrive)
        pl.when(jnp.logical_not(is_self))(copy.start)
        pl.when(is_self)(kept.start)

        def wait_send():
            pl.when(jnp.logical_not(is_self))(copy.wait_send)

        self.sent.append(types.SimpleNamespace(wait_send=wait_send))

    def sibling(self):
        return (1 - self.s, self.c, self.y)

    def finish(self):
        for copy in self.sent:
            copy.wait_send()
        self.sent = []


def wait_bytes(ref, sem):
    pltpu.make_async_copy(ref, ref, sem).wait()


class Gather8:
    def __init__(self, here, full):
        self.here, self.full = here, full
        self.own = [here.sem() for _ in range(SHARD)]
        self.other = [here.sem() for _ in range(SHARD)]

    def start(self, value):
        h = self.here
        mine = self.full.at[h.rows(h.y, h.s)]
        mine[...] = value
        h.send(mine, mine, h.sibling(), self.other[0])
        for step in (1, 3, 2):
            h.send(mine, mine, (h.s, h.c, h.shard(step)), self.own[SHARD - step])

    def relay(self, step):
        h = self.here
        part = self.full.at[h.rows(h.shard(step), h.s)]
        wait_bytes(part, self.own[step])
        h.send(part, part, h.sibling(), self.other[step])

    def wait(self, step):
        h = self.here
        wait_bytes(self.full.at[h.rows(h.shard(step), 1 - h.s)], self.other[step])


class Scatter8:
    def __init__(self, here, bufs):
        self.here = here
        self.to_core, self.mine, self.from_core, self.to_shard, self.from_shard = bufs
        self.core = [here.sem() for _ in range(SHARD)]
        self.shard = [here.sem() for _ in range(SHARD)]

    def put(self, step, block):
        h = self.here
        low, high = block[:ROWS], block[ROWS:]
        self.to_core[step] = jnp.where(h.s == 0, high, low).astype(BF16)
        self.mine[step] = jnp.where(h.s == 0, low, high)
        h.send(self.to_core.at[step], self.from_core.at[step], h.sibling(), self.core[step])

    def relay(self, step):
        h = self.here
        wait_bytes(self.from_core.at[step], self.core[step])
        self.to_shard[step] = (self.mine[step] + self.from_core[step].astype(F32)).astype(BF16)
        h.send(self.to_shard.at[step], self.from_shard.at[step], (h.s, h.c, h.shard(step)), self.shard[step])

    def result(self):
        wait_bytes(self.from_core.at[0], self.core[0])
        total = self.mine[0] + self.from_core[0].astype(F32)
        for step in (1, 3, 2):
            wait_bytes(self.from_shard.at[step], self.shard[step])
            total = total + self.from_shard[step].astype(F32)
        return total


def scatter_scratch():
    quarter = (SHARD, ROWS, D)
    return [VMEM(quarter, BF16), VMEM(quarter, F32), VMEM(quarter, BF16), VMEM(quarter, BF16), VMEM(quarter, BF16)]


ORDER = (0, 1, 3, 2)


def window_offset(group):
    return 32 * lax.rem(group, 4)


def everyone(h):
    for step in (1, 3, 2, 0):
        for other in range(2):
            yield step, other, (lax.rem(h.s + other, 2), h.c, h.shard(step))


def packed_qkv(rows, g):
    keys = rows[:, D + 128 * g : D + 128 * g + 128]
    values = rows[:, 2 * D + 128 * g : 2 * D + 128 * g + 128]
    return jnp.concatenate([
        rows[:, 128 * g : 128 * g + 128], keys[:, :64], values[:, :64], keys[:, 64:], values[:, 64:],
        rows[:, D - 64 : D], rows[:, 2 * D - 64 : 2 * D], rows[:, 3 * D - 64 : 3 * D], jnp.zeros_like(keys[:, :64])],
        axis=1)


def window(g):
    return slice(128 * (17 * g // 4), 128 * (17 * g // 4) + WINDOW)


def spread_kernel(params, w_qkv, w_up):
    def body(r):
        h = Here(r.sems)
        own = pl.ds(pl.multiple_of(h.c * 16, 16), 16)
        loads = [
            h.local(ref.at[0, rows], dst.at[pl.ds(16 * i, 16)])
            for ref, dst in ((r.w_up, r.up_rows), (r.w_qkv, r.qkv_rows)) for i, rows in enumerate((own, pl.ds(256, 16)))]
        h.barrier(whole=False)
        arrive, arrive_mid, arrive_up = h.sem(), h.sem(), h.sem()
        mine = r.params_in.at[h.s * SHARD + h.y]
        mine[...] = r.params[...]
        for step, other, to in everyone(h):
            if step or other:
                h.send(mine, mine, to, arrive)
        for copy in loads:
            copy.wait()

        @pl.when(h.s == 0)
        def _():
            for g in range(8):
                r.mid[g] = r.up_rows[:, window(g)].reshape(2, 16, WINDOW)

        @pl.when(h.s == 1)
        def _():
            for g in range(8):
                r.mid[g] = packed_qkv(r.qkv_rows[...], g).reshape(2, 16, WINDOW)
                r.up[g] = r.up_rows[:, window(g)].reshape(2, 16, WINDOW)

        up_copies = []
        for step, other, to in everyone(h):
            g = 2 * to[2] + to[0]
            for half, dst, dst_up in ((0, r.mid_piece, r.up_piece), (1, r.mid_last, r.up_last)):
                src, dst = r.mid.at[g, half], dst.at[h.s * SHARD + h.y]
                src_up, dst_up = r.up.at[g, half], dst_up.at[h.y]
                if step or other:
                    h.send(src, dst, to, arrive_mid)
                    up_copies.append(pltpu.make_async_remote_copy(
                        src_ref=src_up, dst_ref=dst_up, send_sem=h.sem(), recv_sem=arrive_up, device_id=to,
                        device_id_type=MESH))
                else:
                    pltpu.make_async_copy(src, dst, arrive_mid).start()
                    up_copies.append(pltpu.make_async_copy(src_up, dst_up, arrive_up))

        @pl.when(h.s == 1)
        def _():
            for copy in up_copies:
                copy.start()

        wait_bytes(r.params_in.at[pl.ds(0, 7)], arrive)
        for layer in range(2):
            r.norms[layer] = jnp.concatenate([r.params_in[layer * SHARD + i] for i in range(SHARD)], axis=1)
        wait_bytes(r.mid, arrive_mid)
        wait_bytes(r.up.at[pl.ds(0, SHARD)], arrive_up)

        @pl.when(h.s == 1)
        def _():
            for copy in up_copies[:-4] + up_copies[-2:]:
                copy.wait_send()

        h.finish()

    ins = dict(params=(params, VMEM), w_qkv=(w_qkv, ANY), w_up=(w_up, ANY))
    outs = dict(
        norms=(spec((2, 8, D), F32), VMEM), mid_piece=(spec((8, 16, WINDOW)), VMEM),
        mid_last=(spec((8, 16, WINDOW)), VMEM), up_piece=(spec((SHARD, 16, WINDOW)), VMEM),
        up_last=(spec((SHARD, 16, WINDOW)), VMEM))
    scratch = dict(
        params_in=VMEM((8, 8, SLICE), F32), up_rows=VMEM((32, FF), BF16), qkv_rows=VMEM((32, 3 * D), BF16),
        mid=VMEM((8, 2, 16, WINDOW), BF16), up=VMEM((8, 2, 16, WINDOW), BF16), sems=pltpu.SemaphoreType.DMA((64,)))
    return call("spread", body, ins, outs, scratch, collective_id=0)


def load_tiles(h, gathered, last, dst, first=0):
    copies = []
    for i in range(SHARD):
        copies.append(h.local(gathered.at[:, first + i], dst.at[pl.ds(17 * i, 16)]))
        copies.append(h.local(last.at[first + i], dst.at[17 * i + 16]))
    return copies


def save_tiles(h, src, sixteenths, last):
    for i in range(SHARD):
        for x in range(4):
            h.save(src.at[pl.ds(17 * i + 4 * x, 4)], sixteenths.at[x, :, i])
        h.save(src.at[17 * i + 16], last.at[i])


def whole(ref):
    return ref[...].reshape(D, WINDOW)


class FirstWeights:
    def __init__(self, h, r):
        self.h, self.r = h, r
        self.arrive = [h.sem() for _ in range(3)]

    def load(self):
        h, r = self.h, self.r
        self.rows = pltpu.make_async_copy(r.w_qkv.at[0], r.qkv_rows, h.sem())
        pl.when(h.s == 0)(self.rows.start)
        self.loads = [h.local(r.w_down.at[0], r.down_rows), h.local(r.w_out.at[0], r.out_rows)]

    def send_qkv(self):
        h, r = self.h, self.r
        self.copies = []
        for step in (1, 3, 2, 0):
            for core in range(2):
                src = r.qkv_packed.at[h.shard(step) * 2 + core]
                dst = r.qkv_vm.at[pl.ds(h.y * 17, 17)]
                if step or core:
                    self.copies.append(pltpu.make_async_remote_copy(
                        src_ref=src, dst_ref=dst, send_sem=h.sem(), recv_sem=self.arrive[0],
                        device_id=(core, h.c, h.shard(step)), device_id_type=MESH))
                else:
                    kept = pltpu.make_async_copy(src, dst, self.arrive[0])

        @pl.when(h.s == 0)
        def _():
            self.rows.wait()
            for g in range(8):
                r.qkv_packed[g] = packed_qkv(r.qkv_rows[...], g).reshape(17, 16, WINDOW)
            for copy in self.copies:
                copy.start()
            kept.start()

    def send_rest(self):
        h, r = self.h, self.r
        for copy in self.loads:
            copy.wait()
        for other in range(2):
            core = lax.rem(h.s + other, 2)
            at = pl.multiple_of(window_offset(h.y * 2 + core), 32)
            src = r.down_rows.at[pl.ds(pl.multiple_of(544 * core, 16), 544)]
            dst = r.down_vm.at[h.s, pl.ds(at, 544)]
            if other:
                h.send(src, dst, h.sibling(), self.arrive[1])
            else:
                pltpu.make_async_copy(src, dst, self.arrive[1]).start()
        self.tiles = []
        for i in range(17):
            tile = h.y * 17 + i
            group = jnp.minimum(tile // 8, 7)
            core, shard = lax.rem(group, 2), group // 2
            src = r.out_rows.at[pl.ds(16 * i, 16)]
            dst = r.out_vm.at[h.s, pl.ds(pl.multiple_of(lax.rem(tile, 8) * 16, 16), 16)]
            copy = pltpu.make_async_remote_copy(
                src_ref=src, dst_ref=dst, send_sem=h.sem(), recv_sem=self.arrive[2],
                device_id=(core, h.c, shard), device_id_type=MESH)
            same = pltpu.make_async_copy(src, dst, self.arrive[2])
            is_self = (core == h.s) & (shard == h.y)
            pl.when((tile < 64) & is_self)(same.start)
            away = (tile < 64) & jnp.logical_not(is_self)
            pl.when(away)(copy.start)
            self.tiles.append((away, copy))
        src, dst = r.out_rows.at[pl.ds(SLICE - 64, 64)], r.out_vm.at[h.s, pl.ds(128, 64)]
        same = pltpu.make_async_copy(src, dst, self.arrive[2])
        self.last = []
        for step, other, to in everyone(h):
            if step or other:
                self.last.append(pltpu.make_async_remote_copy(
                    src_ref=src, dst_ref=dst, send_sem=h.sem(), recv_sem=self.arrive[2], device_id=to,
                    device_id_type=MESH))

        @pl.when(h.y == SHARD - 1)
        def _():
            same.start()
            for copy in self.last:
                copy.start()

    def wait_qkv(self):
        wait_bytes(self.r.qkv_vm, self.arrive[0])

    def finish(self):
        r, h = self.r, self.h
        wait_bytes(r.down_vm.at[:, pl.ds(0, 544)], self.arrive[1])
        h.save(r.down_vm, r.down_w)
        wait_bytes(r.out_vm, self.arrive[2])
        h.save(r.out_vm, r.out_w)

        @pl.when(h.s == 0)
        def _():
            for copy in self.copies:
                copy.wait_send()

        for away, copy in self.tiles:
            pl.when(away)(copy.wait_send)

        @pl.when(h.y == SHARD - 1)
        def _():
            for copy in self.last:
                copy.wait_send()


def head_outs():
    return dict(
        a_full=(spec((512, D)), ANY), message_in=(spec((CTX, 160, 128)), VMEM),
        kv16_in=(spec((2, CTX, ROWS, 128)), VMEM), q16=(spec((ROWS, HEAD_DIM)), VMEM))


def head_scratch():
    return dict(message=VMEM((2, 4, 2, 160, 128), BF16), qkv_vm=VMEM(TILES, BF16), a_vm=VMEM((512, D), BF16))


def run_head(h, r, gather, a_value, after=None):
    arrive = h.sem()
    own16 = dot(a_value, r.qkv_vm[:, :, 384:].reshape(D, 256)).astype(BF16)
    r.q16[...] = own16[:, :64]
    r.kv16_in[h.s, h.c] = own16[:, 64:192]
    own_kv = r.kv16_in.at[h.s, h.c]
    leave16, arrive16, cross16 = h.sem(), h.sem(), h.sem()
    for step in range(1, CTX):
        h.send(own_kv, own_kv, (h.s, lax.rem(h.c + step, CTX), h.y), arrive16, leave16)
    for step in ORDER:
        if step:
            gather.relay(step)
        gather.wait(step)
        shard = h.shard(step)
        block = r.a_vm[pl.ds(pl.multiple_of(shard * 128, 128), 128)]
        out = dot(block, r.qkv_vm[:, :, :384].reshape(D, 384)).astype(BF16)
        for e in range(2):
            for core in range(2):
                r.message[e, shard, core, :128] = out[:, 128 + 128 * e : 256 + 128 * e]
                for b in range(2):
                    at = 32 * b + 16 * core
                    lanes = slice(64 * e, 64 * e + 64)
                    packed = jnp.concatenate([out[at : at + 16, lanes], out[64 + at : 80 + at, lanes]], axis=1)
                    r.message[e, shard, core, 128 + 16 * b : 144 + 16 * b] = packed
                chip = 8 * h.s + 4 * e + shard
                h.send_or_keep(
                    r.message.at[e, shard, core], r.message_in.at[h.c], (core, chip, h.y),
                    (chip == h.c) & (h.s == core), arrive)
    h.save(r.a_vm, r.a_full)
    if after is not None:
        after()
    wait_bytes(r.kv16_in.at[h.s, pl.ds(0, CTX - 1)], arrive16)
    cross = r.kv16_in.at[h.s]
    h.send(cross, cross, h.sibling(), cross16)
    wait_bytes(r.kv16_in.at[h.s, pl.ds(0, CTX - 1)], leave16)
    wait_bytes(r.kv16_in.at[1 - h.s], cross16)
    wait_bytes(r.message_in, arrive)


def first_kernel(hidden, norms, w_qkv, w_out, w_down):
    def body(r):
        h = Here(r.sems)
        weights = FirstWeights(h, r)
        weights.load()
        r.down_vm[...] = jnp.zeros_like(r.down_vm)
        h.barrier()
        weights.send_qkv()
        x = r.hidden[h.s].astype(F32)
        a_value = layer_norm(x, r.norms[0, 0:1], r.norms[0, 2:3]).astype(BF16)
        gather = Gather8(h, r.a_vm)
        gather.start(a_value)
        weights.wait_qkv()
        h.save(r.qkv_vm, r.qkv_w)
        run_head(h, r, gather, a_value, weights.send_rest)
        weights.finish()
        h.finish()

    ins = dict(hidden=(hidden, VMEM), norms=(norms, VMEM), w_qkv=(w_qkv, ANY), w_out=(w_out, ANY), w_down=(w_down, ANY))
    outs = dict(
        **head_outs(), qkv_w=(spec(TILES), ANY), out_w=(spec((2, 192, D)), ANY), down_w=(spec((2, WINDOW, D)), ANY))
    scratch = dict(
        **head_scratch(), qkv_rows=VMEM((SLICE, 3 * D), BF16), qkv_packed=VMEM((8, 17, 16, WINDOW), BF16),
        down_rows=VMEM((D, D), BF16), out_rows=VMEM((SLICE, D), BF16), down_vm=VMEM((2, WINDOW, D), BF16),
        out_vm=VMEM((2, 192, D), BF16), sems=pltpu.SemaphoreType.DMA((200,)))
    return call("first", body, ins, outs, scratch, collective_id=1)


def attend(block_order, positions, own_positions, message_in, kv16_in, q16):
    def body(r):
        half = lax.axis_index(SECTION)
        for c in range(CTX):
            for m in range(2):
                for b in range(2):
                    block = 32 * m + r.order[m, 2 * c + b]
                    rows = r.message_in[c, 64 * m + 32 * b : 64 * m + 32 * b + 32, :]
                    at = pl.ds(pl.multiple_of(block * 32, 32), 32)
                    r.keys[at] = rows[:, :64]
                    r.values[at] = rows[:, 64:]
                    at = pl.ds(pl.multiple_of(block * 16, 16), 16)
                    r.queries[at] = r.message_in[c, 128 + 16 * b : 144 + 16 * b, 64 * m : 64 * m + 64] * 0.125
        row = lax.broadcasted_iota(jnp.int32, (256, 512), 0)
        row = 32 * (row // 16) + 16 * half + row % 16
        visible = row >= lax.broadcasted_iota(jnp.int32, (256, 512), 1)
        for t in range(4):
            query = r.queries[256 * t : 256 * t + 256]
            parts = [dot_nt(query, r.keys[512 * u : 512 * u + 512]) for u in range(t + 1)]
            parts[t] = jnp.where(visible, parts[t], NEG_LARGE)
            top = parts[0]
            for p in parts[1:]:
                top = jnp.maximum(top, p)
            top = jnp.max(top, axis=-1, keepdims=True)
            parts = [jnp.exp(p - top) for p in parts]
            total = parts[0]
            for p in parts[1:]:
                total = total + p
            total = jnp.sum(total, axis=-1, keepdims=True)
            out = dot(parts[0].astype(BF16), r.values[:512])
            for u in range(1, t + 1):
                out = out + dot(parts[u].astype(BF16), r.values[512 * u : 512 * u + 512])
            r.sorted_out[256 * t : 256 * t + 256] = (out / total).astype(BF16)
            r.logs[256 * t : 256 * t + 256] = jnp.broadcast_to(top + jnp.log(total), (256, 128))
        for c in range(CTX):
            for m in range(2):
                for b in range(2):
                    at = pl.multiple_of((32 * m + r.order[m, 2 * c + b]) * 16, 16)
                    r.out[c, 16 * b : 16 * b + 16, 64 * m : 64 * m + 64] = r.sorted_out[pl.ds(at, 16)]
        kv = r.kv16_in[...].reshape(SEQ, 128)
        scores = dot_nt(r.q16[...] * 0.125, kv[:, :64])
        scores = jnp.where(r.own_positions[...] >= r.positions[...], scores, NEG_LARGE)
        top = jnp.max(scores, axis=-1, keepdims=True)
        scores = jnp.exp(scores - top)
        total = jnp.sum(scores, axis=-1, keepdims=True)
        out = dot(scores.astype(BF16), kv[:, 64:])
        r.out16[...] = (out / total).astype(BF16)
        r.logs16[...] = jnp.broadcast_to(top + jnp.log(total), (ROWS, 128))

    ins = dict(
        order=(block_order, pltpu.SMEM), positions=(positions, VMEM), own_positions=(own_positions, VMEM),
        message_in=(message_in, VMEM), kv16_in=(kv16_in, VMEM), q16=(q16, VMEM),)
    outs = dict(
        out=(spec((CTX, 32, 128)), VMEM), out16=(spec((ROWS, 64)), VMEM),
        sorted_out=(spec((1024, 64)), VMEM), logs=(spec((1024, 128), F32), VMEM),
        logs16=(spec((ROWS, 128), F32), VMEM),)
    scratch = dict(
        keys=VMEM((SEQ, 64), BF16), values=VMEM((SEQ, 64), BF16), queries=VMEM((1024, 64), BF16),)
    return call("attend", body, ins, outs, scratch)


def middle_scratch():
    return dict(
        context_in=VMEM((2, 4, 2, 32, 128), BF16), out_vm=VMEM((192, D), BF16), up_vm=VMEM(TILES, BF16),
        down_vm=VMEM((WINDOW, D), BF16), to_out=scatter_scratch(), to_down=scatter_scratch())


def load_layer(h, r, layer, first):
    loads = [h.local(r.out_w.at[layer], r.out_vm), h.local(r.down_w.at[layer], r.down_vm)]
    return loads + load_tiles(h, r.up_all, r.up_last, r.up_vm, first)


def gather_context(h, r):
    arrive = h.sem()
    to_core = h.c // 8
    e, j = lax.rem(h.c // 4, 2), lax.rem(h.c, 4)
    for c in range(CTX):
        h.send_or_keep(
            r.attended.at[c], r.context_in.at[e, j, h.s], (to_core, c, h.y), (h.c == c) & (h.s == to_core), arrive)
    return arrive


def unpack_context(r, store):
    for j in range(4):
        for m in range(2):
            for b in range(2):
                for core in range(2):
                    lanes = slice(64 * m, 64 * m + 64)
                    piece = jnp.concatenate(
                        [r.context_in[e, j, core, 16 * b : 16 * b + 16, lanes] for e in range(2)], axis=1)
                    at = 128 * j + 64 * m + 32 * b + 16 * core
                    store[at : at + 16] = piece


def block_rows(h, step):
    return pl.ds(pl.multiple_of(h.shard(step) * 128, 128), 128)


def run_out(h, r, x):
    sums = Scatter8(h, r.to_out)
    for step in (2, 1, 3, 0):
        sums.put(step, dot(r.context[block_rows(h, step)], r.out_vm[:128]))
    for step in (2, 1, 3):
        sums.relay(step)
    own = x + dot(r.attended16[...], r.out_vm[128:])
    return own + sums.result()


def middle_kernel(attended, attended16, x, norms, first, mid_all, mid_last):
    def body(r):
        h = Here(r.sems)
        loads = load_layer(h, r, 0, 0)
        head_loads = load_tiles(h, r.up_all, r.up_last, r.qkv_vm, SHARD)
        h.barrier()
        arrive = gather_context(h, r)
        for copy in loads:
            copy.wait()
        wait_bytes(r.context_in, arrive)
        unpack_context(r, r.context)
        residual = run_out(h, r, r.x[h.s].astype(F32))
        r.residual[...] = residual
        b_value = layer_norm(residual, r.norms[0, 1:2], r.norms[0, 3:4]).astype(BF16)
        gather = Gather8(h, r.b_vm)
        gather.start(b_value)
        sums = Scatter8(h, r.to_down)
        for step in ORDER:
            if step:
                gather.relay(step)
            gather.wait(step)
            rows = block_rows(h, step)
            u = dot(r.b_vm[rows], whole(r.up_vm))
            r.pre_vm[rows] = u
            sums.put(step, dot(gelu(u).astype(BF16), r.down_vm[...]))
        for step in (1, 3, 2):
            sums.relay(step)
        h.save(r.b_vm, r.b_full)
        h.save(r.pre_vm, r.pre)
        for copy in head_loads:
            copy.wait()
        y = (residual + sums.result()).astype(BF16)
        r.y[...] = y
        a_value = layer_norm(y.astype(F32), r.norms[1, 0:1], r.norms[1, 2:3]).astype(BF16)
        gather = Gather8(h, r.a_vm)
        gather.start(a_value)
        run_head(h, r, gather, a_value)
        h.finish()

    ins = dict(
        attended=(attended, VMEM), attended16=(attended16, VMEM), x=(x, VMEM), norms=(norms, VMEM),
        out_w=(first.out_w, ANY), down_w=(first.down_w, ANY), up_all=(mid_all, ANY), up_last=(mid_last, ANY))
    outs = dict(
        context=(spec((512, 128)), VMEM), residual=(spec((ROWS, D), F32), VMEM), b_full=(spec((512, D)), ANY),
        pre=(spec((512, WINDOW), F32), ANY), y=(spec((ROWS, D)), VMEM), **head_outs())
    scratch = dict(
        **middle_scratch(), **head_scratch(), b_vm=VMEM((512, D), BF16), pre_vm=VMEM((512, WINDOW), F32),
        sems=pltpu.SemaphoreType.DMA((200,)))
    return call("middle", body, ins, outs, scratch, collective_id=2)


def gelu_slope(u):
    t = jnp.tanh(0.7978845608028654 * (u + 0.044715 * u * u * u))
    return 0.5 * (1.0 + t) + 0.5 * u * (1.0 - t * t) * 0.7978845608028654 * (1.0 + 0.134145 * u * u)


def norm_back(grad, values, gain):
    normed, rate = norm_parts(values)
    scaled = grad * gain
    mean = jnp.mean(scaled, axis=-1, keepdims=True)
    along = jnp.mean(scaled * normed, axis=-1, keepdims=True)
    back = rate * (scaled - mean - normed * along)
    return back, grad * normed


def columns(at, gain_rows, bias_rows):
    lane = lax.broadcasted_iota(jnp.int32, (ROWS, 64), 1)

    def into(rows, column):
        return lax.dot_general(
            rows, (lane == column).astype(F32), (((0,), (0,)), ((), ())), precision=lax.Precision.HIGHEST,
            preferred_element_type=F32)

    return into(gain_rows, at) + into(bias_rows, at + 1)


def back_outs():
    return dict(
        mid_grad=(spec((ROWS, D), F32), VMEM), context_grad_in=(spec((CTX, 32, 128)), VMEM),
        context16_grad=(spec((ROWS, HEAD_DIM)), VMEM), up_g=(spec((4, 4, SHARD, 16, WINDOW)), ANY),
        up_g_last=(spec((SHARD, 16, WINDOW)), ANY), down_g=(spec((544, D)), ANY), out_g=(spec((192, D)), VMEM),
        norm2_g=(spec((68, 16, 64)), VMEM))


def back_scratch():
    return dict(
        m_full=VMEM((512, D), BF16), z_full=VMEM((512, D), BF16), hidden_low=VMEM((512, WINDOW), BF16),
        pre_grad=VMEM((512, WINDOW), BF16), context_message=VMEM((2, 4, 2, 32, 128), BF16), up_grad=VMEM(TILES, BF16),
        down_grad=VMEM((WINDOW, D), BF16), b_vm=VMEM((512, D), BF16), to_norm2=scatter_scratch())


def back_block(h, r, rows, sums, step, u, g):
    r.hidden_low[rows] = g
    hidden_grad = dot_nt(r.m_full[rows], r.down_vm[...])
    pre_grad = (hidden_grad * gelu_slope(u)).astype(BF16)
    r.pre_grad[rows] = pre_grad
    sums.put(step, dot_nt(pre_grad, whole(r.up_vm)))


def finish_back(h, r, sums, layer, residual, out_grad, context, beside=None):
    r.down_grad[...] = dot_tn(r.hidden_low[...], r.m_full[...]).astype(BF16)
    offset = pl.multiple_of(window_offset(h.y * 2 + h.s), 32)
    h.save(r.down_grad.at[pl.ds(offset, 544)], r.down_g)
    r.up_grad[...] = dot_tn(r.b_vm[...], r.pre_grad[...]).astype(BF16).reshape(TILES)
    save_tiles(h, r.up_grad, r.up_g, r.up_g_last)
    normed_grad = sums.result()
    back, gain_rows = norm_back(normed_grad, residual, r.norms[layer, 1:2])
    mid_grad = out_grad + back
    r.mid_grad[...] = mid_grad
    z = mid_grad.astype(BF16)
    gather = Gather8(h, r.z_full)
    gather.start(z)
    r.norm2_g[...] = columns(2, gain_rows, normed_grad).astype(BF16).reshape(68, 16, 64)
    if beside is not None:
        beside()
    arrive = h.sem()
    r.context16_grad[...] = dot_nt(z, r.out_vm[128:]).astype(BF16)
    for step in ORDER:
        if step:
            gather.relay(step)
        gather.wait(step)
        shard = h.shard(step)
        out = dot_nt(r.z_full[block_rows(h, step)], r.out_vm[:128]).astype(BF16)
        for e in range(2):
            for core in range(2):
                lanes = slice(64 * e, 64 * e + 64)
                for b in range(2):
                    at = 32 * b + 16 * core
                    r.context_message[e, shard, core, 16 * b : 16 * b + 16] = jnp.concatenate(
                        [out[at : at + 16, lanes], out[64 + at : 80 + at, lanes]], axis=1)
                chip = 8 * h.s + 4 * e + shard
                h.send_or_keep(
                    r.context_message.at[e, shard, core], r.context_grad_in.at[h.c], (core, chip, h.y),
                    (chip == h.c) & (h.s == core), arrive)
    r.out_g[:128] = dot_tn(context[...], r.z_full[...]).astype(BF16)
    r.out_g[128:] = dot_tn(r.attended16[...], z).astype(BF16)
    wait_bytes(r.context_grad_in, arrive)


def turn_kernel(attended, attended16, x, norms, first, up_all, up_last, cotangent):
    def body(r):
        h = Here(r.sems)
        loads = load_layer(h, r, 1, 0)
        h.barrier()
        arrive = gather_context(h, r)
        out_grad = r.cotangent[h.s]
        gather_m = Gather8(h, r.m_full)
        gather_m.start(out_grad)
        for copy in loads:
            copy.wait()
        wait_bytes(r.context_in, arrive)
        unpack_context(r, r.context)
        residual = run_out(h, r, r.x[...].astype(F32))
        b_value = layer_norm(residual, r.norms[1, 1:2], r.norms[1, 3:4]).astype(BF16)
        gather = Gather8(h, r.b_vm)
        gather.start(b_value)
        back_sums, sums = Scatter8(h, r.to_norm2), Scatter8(h, r.to_down)
        for step in ORDER:
            if step:
                gather_m.relay(step)
                gather.relay(step)
            gather_m.wait(step)
            gather.wait(step)
            rows = block_rows(h, step)
            u = dot(r.b_vm[rows], whole(r.up_vm))
            g = gelu(u).astype(BF16)
            back_block(h, r, rows, back_sums, step, u, g)
            sums.put(step, dot(g, r.down_vm[...]))
        for step in (1, 3, 2):
            back_sums.relay(step)
        for step in (1, 3, 2):
            sums.relay(step)

        def beside():
            r.out[...] = (residual + sums.result()).astype(BF16)

        finish_back(h, r, back_sums, 1, residual, out_grad.astype(F32), r.context, beside)
        h.finish()

    ins = dict(
        attended=(attended, VMEM), attended16=(attended16, VMEM), x=(x, VMEM), norms=(norms, VMEM),
        out_w=(first.out_w, ANY), down_w=(first.down_w, ANY), up_all=(up_all, ANY), up_last=(up_last, ANY),
        cotangent=(cotangent, VMEM))
    outs = dict(out=(spec((ROWS, D)), VMEM), **back_outs())
    scratch = dict(
        context=VMEM((512, 128), BF16), **middle_scratch(), **back_scratch(), sems=pltpu.SemaphoreType.DMA((200,)))
    return call("turn", body, ins, outs, scratch, collective_id=3)


def attend_back(block_order, positions, own_positions, message_in, kv16_in, q16, saved, grad_in, grad16):
    def body(r):
        half = lax.axis_index(SECTION)
        for c in range(CTX):
            for m in range(2):
                for b in range(2):
                    block = 32 * m + r.order[m, 2 * c + b]
                    rows = r.message_in[c, 64 * m + 32 * b : 64 * m + 32 * b + 32, :]
                    at = pl.ds(pl.multiple_of(block * 32, 32), 32)
                    r.keys[at] = rows[:, :64]
                    r.values[at] = rows[:, 64:]
                    at = pl.ds(pl.multiple_of(block * 16, 16), 16)
                    r.queries[at] = r.message_in[c, 128 + 16 * b : 144 + 16 * b, 64 * m : 64 * m + 64] * 0.125
                    r.grads[at] = r.grad_in[c, 16 * b : 16 * b + 16, 64 * m : 64 * m + 64]
        r.key_grads[...] = jnp.zeros_like(r.key_grads)
        r.value_grads[...] = jnp.zeros_like(r.value_grads)
        column = lax.broadcasted_iota(jnp.int32, (512, 256), 1)
        column = 32 * (column // 16) + 16 * half + column % 16
        visible = column >= lax.broadcasted_iota(jnp.int32, (512, 256), 0)
        ones = jnp.ones((8, 64), F32)

        def row_of(grads, outs):
            product = grads.astype(F32) * outs.astype(F32)
            return lax.dot_general(
                ones, product, (((1,), (1,)), ((), ())), precision=lax.Precision.HIGHEST,
                preferred_element_type=F32)[0:1]

        for t in range(4):
            part = slice(256 * t, 256 * t + 256)
            query, grad = r.queries[part], r.grads[part]
            logs = jnp.transpose(r.logs[part])[0:1]
            delta = row_of(grad, r.sorted_out[part])
            query_grad = jnp.zeros((256, 64), F32)
            for u in range(t + 1):
                chunk = slice(512 * u, 512 * u + 512)
                keys = r.keys[chunk]
                scores = dot_nt(keys, query)
                if u == t:
                    scores = jnp.where(visible, scores, NEG_LARGE)
                probs = jnp.exp(scores - logs)
                probs_grad = dot_nt(r.values[chunk], grad)
                scores_grad = (probs * (probs_grad - delta)).astype(BF16)
                r.value_grads[chunk] += dot(probs.astype(BF16), grad)
                r.key_grads[chunk] += dot(scores_grad, query)
                query_grad = query_grad + dot_tn(scores_grad, keys)
            r.query_grads[part] = (query_grad * 0.125).astype(BF16)
        for c in range(CTX):
            for m in range(2):
                for b in range(2):
                    block = 32 * m + r.order[m, 2 * c + b]
                    at = pl.ds(pl.multiple_of(block * 32, 32), 32)
                    r.message[c, 64 * m + 32 * b : 64 * m + 32 * b + 32, :] = jnp.concatenate(
                        [r.key_grads[at], r.value_grads[at]], axis=1).astype(BF16)
                    at = pl.ds(pl.multiple_of(block * 16, 16), 16)
                    r.message[c, 128 + 16 * b : 144 + 16 * b, 64 * m : 64 * m + 64] = r.query_grads[at]
        kv = r.kv16_in[...].reshape(SEQ, 128)
        query, grad = r.q16[...] * 0.125, r.grad16[...]
        scores = dot_nt(kv[:, :64], query)
        scores = jnp.where(r.own_positions[...] >= r.positions[...], scores, NEG_LARGE)
        probs = jnp.exp(scores - jnp.transpose(r.logs16[...])[0:1])
        probs_grad = dot_nt(kv[:, 64:], grad)
        scores_grad = (probs * (probs_grad - row_of(grad, r.out16[...]))).astype(BF16)
        both = jnp.concatenate([dot(scores_grad, query), dot(probs.astype(BF16), grad)], axis=1)
        r.kv16_grad[...] = both.astype(BF16).reshape(2, CTX, ROWS, 128)
        r.q16_grad[...] = (dot_tn(scores_grad, kv[:, :64]) * 0.125).astype(BF16)

    ins = dict(
        order=(block_order, pltpu.SMEM), positions=(positions, VMEM), own_positions=(own_positions, VMEM),
        message_in=(message_in, VMEM), kv16_in=(kv16_in, VMEM), q16=(q16, VMEM),
        sorted_out=(saved.sorted_out, VMEM), logs=(saved.logs, VMEM), logs16=(saved.logs16, VMEM),
        out16=(saved.out16, VMEM), grad_in=(grad_in, VMEM), grad16=(grad16, VMEM),)
    outs = dict(
        message=(spec((CTX, 160, 128)), VMEM), kv16_grad=(spec((2, CTX, ROWS, 128)), VMEM),
        q16_grad=(spec((ROWS, 64)), VMEM),)
    scratch = dict(
        keys=VMEM((SEQ, 64), BF16), values=VMEM((SEQ, 64), BF16), queries=VMEM((1024, 64), BF16),
        grads=VMEM((1024, 64), BF16), query_grads=VMEM((1024, 64), BF16),
        key_grads=VMEM((SEQ, 64), F32), value_grads=VMEM((SEQ, 64), F32),)
    return call("attend_back", body, ins, outs, scratch)


def tail_ins(back, a_full, x, above, norms):
    return dict(
        message=(back.message, VMEM), kv16_grad=(back.kv16_grad, VMEM), q16_grad=(back.q16_grad, VMEM),
        a_full=(a_full, ANY), x=(x, VMEM), mid_in=(above.mid_grad, VMEM), norms=(norms, VMEM),
        norm2_in=(above.norm2_g, VMEM))


def tail_outs():
    return dict(
        in_grad=(spec((ROWS, D)), VMEM), qkv_g=(spec((4, 4, SHARD, 16, WINDOW)), ANY),
        qkv_g_last=(spec((SHARD, 16, WINDOW)), ANY))


def tail_scratch():
    return dict(
        message_in=VMEM((2, 4, 2, 160, 128), BF16), core16=VMEM((CTX, ROWS, 128), BF16),
        sum16=VMEM((CTX, ROWS, 128), BF16), own16=VMEM((CTX, ROWS, 128), BF16), qkv_grads=VMEM((512, 384), BF16),
        qkv_vm=VMEM(TILES, BF16), qkv_grad=VMEM(TILES, BF16), a_vm=VMEM((512, D), BF16), to_norm1=scatter_scratch())


def start_tail(h, r):
    cross = h.sem()
    h.send(r.kv16_grad.at[1 - h.s], r.core16, h.sibling(), cross)
    arrive = h.sem()
    to_core = h.c // 8
    e, j = lax.rem(h.c // 4, 2), lax.rem(h.c, 4)
    for c in range(CTX):
        h.send_or_keep(
            r.message.at[c], r.message_in.at[e, j, h.s], (to_core, c, h.y), (h.c == c) & (h.s == to_core), arrive)
    wait_bytes(r.core16, cross)
    r.sum16[...] = (r.kv16_grad[h.s].astype(F32) + r.core16[...].astype(F32)).astype(BF16)
    leave16, arrive16 = h.sem(), h.sem()
    for step in range(1, CTX):
        to = lax.rem(h.c + step, CTX)
        h.send(r.sum16.at[to], r.own16.at[step], (h.s, to, h.y), arrive16, leave16)
    return arrive, leave16, arrive16


def run_tail(h, r, layer, x, waits, loads, beside=()):
    arrive, leave16, arrive16 = waits
    for copy in loads:
        copy.wait()
    weights = whole(r.qkv_vm)
    wait_bytes(r.message_in, arrive)
    for j in range(4):
        for e in range(2):
            both = r.message_in[e, j, 0, :128].astype(F32) + r.message_in[e, j, 1, :128].astype(F32)
            r.qkv_grads[128 * j : 128 * j + 128, 128 + 128 * e : 256 + 128 * e] = both.astype(BF16)
        for m in range(2):
            for b in range(2):
                for core in range(2):
                    lanes = slice(64 * m, 64 * m + 64)
                    piece = jnp.concatenate(
                        [r.message_in[e, j, core, 128 + 16 * b : 144 + 16 * b, lanes] for e in range(2)], axis=1)
                    at = 128 * j + 64 * m + 32 * b + 16 * core
                    r.qkv_grads[at : at + 16, :128] = piece
    sums = Scatter8(h, r.to_norm1)
    for step in (2, 1, 3, 0):
        sums.put(step, dot_nt(r.qkv_grads[block_rows(h, step)], weights[:, :384]))
    for step in (2, 1, 3):
        sums.relay(step)
    for each in beside:
        each()
    wait_bytes(r.own16.at[pl.ds(1, CTX - 1)], arrive16)
    wait_bytes(r.own16.at[pl.ds(1, CTX - 1)], leave16)
    kv16 = r.sum16[h.c].astype(F32)
    for step in range(1, CTX):
        kv16 = kv16 + r.own16[step].astype(F32)
    grads16 = jnp.concatenate([r.q16_grad[...], kv16.astype(BF16)], axis=1)
    own = dot_nt(grads16, weights[:, 384:576])
    r.qkv_grad[:, :, :384] = dot_tn(r.a_vm[...], r.qkv_grads[...]).astype(BF16).reshape(68, 16, 384)
    own_grad = dot_tn(r.a_vm[h.rows(h.y, h.s)], grads16)
    normed_grad = own + sums.result()
    back, gain_rows = norm_back(normed_grad, x, r.norms[layer, 0:1])
    in_grad = (r.mid_in[...] + back).astype(BF16)
    r.in_grad[...] = in_grad

    def finish():
        sums_of_rows = columns(0, gain_rows, normed_grad) + r.norm2_in[...].reshape(D, 64).astype(F32)
        r.qkv_grad[:, :, 384:] = jnp.concatenate([own_grad, sums_of_rows], axis=1).astype(BF16).reshape(68, 16, 256)
        save_tiles(h, r.qkv_grad, r.qkv_g, r.qkv_g_last)

    return in_grad, finish


def back_kernel(back, a_full, x, above, norms, first, middle, attended16, mid_all, mid_last):
    def body(r):
        h = Here(r.sems)
        tail_loads = load_tiles(h, r.up_all, r.up_last, r.qkv_vm, SHARD)
        tail_loads.append(h.local(r.a_full, r.a_vm))
        loads = load_layer(h, r, 0, 0)
        loads += [h.local(r.b_full, r.b_vm), h.local(r.pre, r.pre_vm), h.local(r.context, r.context_vm)]
        h.barrier()
        waits = start_tail(h, r)
        out_grad, finish = run_tail(h, r, 1, r.x[...].astype(F32), waits, tail_loads)
        gather = Gather8(h, r.m_full)
        gather.start(out_grad)
        finish()
        for copy in loads:
            copy.wait()
        sums = Scatter8(h, r.to_norm2)
        for step in ORDER:
            if step:
                gather.relay(step)
            gather.wait(step)
            rows = block_rows(h, step)
            u = r.pre_vm[rows]
            back_block(h, r, rows, sums, step, u, gelu(u).astype(BF16))
        for step in (1, 3, 2):
            sums.relay(step)
        finish_back(h, r, sums, 0, r.residual[...], out_grad.astype(F32), r.context_vm)
        h.finish()

    ins = dict(
        **tail_ins(back, a_full, x, above, norms), pre=(middle.pre, ANY), b_full=(middle.b_full, ANY),
        context=(middle.context, ANY), residual=(middle.residual, VMEM), attended16=(attended16, VMEM),
        out_w=(first.out_w, ANY), down_w=(first.down_w, ANY), up_all=(mid_all, ANY), up_last=(mid_last, ANY))
    outs = dict(**tail_outs(), **back_outs())
    scratch = dict(
        out_vm=VMEM((192, D), BF16), up_vm=VMEM(TILES, BF16), down_vm=VMEM((WINDOW, D), BF16),
        pre_vm=VMEM((512, WINDOW), F32), context_vm=VMEM((512, 128), BF16), **tail_scratch(), **back_scratch(),
        sems=pltpu.SemaphoreType.DMA((240,)))
    return call("back", body, ins, outs, scratch, collective_id=4)


class Reduce16:
    def __init__(self, h, part, bufs, x_first):
        self.h, self.part, self.x_first = h, part, x_first
        self.first_in, self.mine, self.second_in = bufs
        self.x, self.z = h.c // 4, lax.rem(h.c, 4)
        self.first = [h.sem() for _ in range(3)]
        self.second = [h.sem() for _ in range(3)]

    def chip(self, x, z):
        return (self.h.s, 4 * lax.rem(x, 4) + lax.rem(z, 4), self.h.y)

    def start(self):
        for j in (1, 3, 2):
            if self.x_first:
                src, to = self.part.at[lax.rem(self.x + j, 4)], self.chip(self.x + j, self.z)
            else:
                src, to = self.part.at[:, lax.rem(self.z + j, 4)], self.chip(self.x, self.z + j)
            self.h.send(src, self.first_in.at[j - 1], to, self.first[j - 1])

    def middle(self):
        for j in range(3):
            wait_bytes(self.first_in.at[j], self.first[j])
        for k in range(4):
            own = self.part[self.x, k] if self.x_first else self.part[k, self.z]
            total = own.astype(F32)
            for j in range(3):
                total = total + self.first_in[j, k].astype(F32)
            self.mine[k] = total.astype(BF16)
        for j in (1, 3, 2):
            if self.x_first:
                src, to = self.mine.at[lax.rem(self.z + j, 4)], self.chip(self.x, self.z + j)
            else:
                src, to = self.mine.at[lax.rem(self.x + j, 4)], self.chip(self.x + j, self.z)
            self.h.send(src, self.second_in.at[j - 1], to, self.second[j - 1])

    def result(self):
        total = self.mine[self.z if self.x_first else self.x].astype(F32)
        for j in range(3):
            wait_bytes(self.second_in.at[j], self.second[j])
            total = total + self.second_in[j].astype(F32)
        return total.astype(BF16)


def reduce_scratch(units):
    return [VMEM((3, 4, units, 16, WINDOW), BF16), VMEM((4, units, 16, WINDOW), BF16), VMEM((3, units, 16, WINDOW), BF16)]


class Spread16:
    def __init__(self, h, parts, x_first):
        self.h, self.parts, self.x_first = h, parts, x_first
        self.x, self.z = h.c // 4, lax.rem(h.c, 4)
        self.first = [h.sem() for _ in range(3)]
        self.second = [h.sem() for _ in range(3)]

    def chip(self, x, z):
        return (self.h.s, 4 * lax.rem(x, 4) + lax.rem(z, 4), self.h.y)

    def start(self):
        own = self.parts.at[self.x, self.z]
        for j in (1, 3, 2):
            to = self.chip(self.x + j, self.z) if self.x_first else self.chip(self.x, self.z + j)
            self.h.send(own, own, to, self.first[j - 1])

    def middle(self):
        for j in range(3):
            wait_bytes(self.parts.at[0, 0], self.first[j])
        for j in (1, 3, 2):
            if self.x_first:
                line, to = self.parts.at[:, self.z], self.chip(self.x, self.z + j)
            else:
                line, to = self.parts.at[self.x], self.chip(self.x + j, self.z)
            self.h.send(line, line, to, self.second[j - 1])

    def finish(self):
        for j in range(3):
            wait_bytes(self.parts.at[0], self.second[j])


def last_kernel(back, a_full, hidden, above, norms, qkv_w):
    def body(r):
        h = Here(r.sems)
        part_loads = [h.local(r.up_g, r.up_part), h.local(r.qkv_g_above, r.qkv_part)]
        loads = [h.local(r.qkv_w, r.qkv_vm), h.local(r.a_full, r.a_vm)]
        h.barrier()
        waits = start_tail(h, r)
        for copy in part_loads:
            copy.wait()
        up = Reduce16(h, r.up_part, r.up_sums, True)
        qkv = Reduce16(h, r.qkv_part, r.qkv_sums, False)
        up.start()
        qkv.start()
        in_grad, finish = run_tail(h, r, 0, r.x[h.s].astype(F32), waits, loads, (up.middle, qkv.middle))
        finish()
        r.up_piece[...] = up.result()
        r.qkv_piece[...] = qkv.result()
        h.finish()

    parts = VMEM((4, 4, SHARD, 16, WINDOW), BF16)
    scratch = dict(
        **tail_scratch(), up_part=parts, qkv_part=parts, up_sums=reduce_scratch(SHARD),
        qkv_sums=reduce_scratch(SHARD), sems=pltpu.SemaphoreType.DMA((200,)))
    ins = dict(
        **tail_ins(back, a_full, hidden, above, norms), qkv_w=(qkv_w, ANY), up_g=(above.up_g, ANY),
        qkv_g_above=(above.qkv_g, ANY))
    piece = (spec((SHARD, 16, WINDOW)), VMEM)
    outs = dict(**tail_outs(), up_piece=piece, qkv_piece=piece)
    return call("last", body, ins, outs, scratch, collective_id=5)


def share_kernel(qkv0, qkv0_last, up0_piece, up0_last, up1, up1_last, qkv1_piece, qkv1_last):
    def body(r):
        h = Here(r.sems)
        x, z = h.c // 4, lax.rem(h.c, 4)
        group = 2 * h.y + h.s
        loads = [h.local(r.qkv0.at[:, :, pl.ds(2 * i, 2)], r.part.at[i]) for i in range(2)]
        up1_load = h.local(r.up1.at[x, z], r.up1_vm)
        h.barrier()
        for copy in loads:
            copy.wait()
        sums = [Reduce16(h, r.part.at[i], (r.sums_a, r.sums_b)[i], i == 0) for i in range(2)]
        for each in sums:
            each.start()
        arrive_last = h.sem()
        for i in range(SHARD):
            r.last_message[i, 0] = r.up0_last[i]
            r.last_message[i, 1] = r.qkv0_last[i]
            r.last_message[i, 2] = r.qkv1_last[i]
            chip = 4 * i + h.y
            h.send_or_keep(r.last_message.at[i], r.last_in.at[h.c], (h.s, chip, h.y), chip == h.c, arrive_last)
        up1_load.wait()
        arrive_up = h.sem()
        for layer, piece in ((0, r.up0_piece), (1, r.up1_vm)):
            for step in (1, 3, 2, 0):
                shard = h.shard(step)
                h.send_or_keep(
                    piece.at[shard], r.up_in.at[group], (layer, h.c, shard), (h.s == layer) & (step == 0), arrive_up)
        wait_bytes(r.up_in, arrive_up)
        spreads = []
        for i, parts in enumerate((r.up_low, r.up_high)):
            parts[x, z] = r.up_in[4 * i : 4 * i + 4]
            spreads.append(Spread16(h, parts, i == 0))
            spreads[i].start()
        for each in sums:
            each.middle()
        for i in range(2):
            r.qkv0_piece[2 * i : 2 * i + 2] = sums[i].result()
        arrive_qkv = h.sem()
        for layer, piece in ((0, r.qkv0_piece), (1, r.qkv1_piece)):
            for step in (1, 3, 2, 0):
                shard = h.shard(step)
                h.send_or_keep(
                    piece.at[shard], r.qkv_in.at[group], (layer, h.c, shard), (h.s == layer) & (step == 0), arrive_qkv)
        for each in spreads:
            each.middle()
        arrive_rest = h.sem()
        reduces = z == h.y

        @pl.when(reduces)
        def _():
            wait_bytes(r.last_in, arrive_last)
            total = r.last_in[0].astype(F32)
            for c in range(1, CTX):
                total = total + r.last_in[c].astype(F32)
            total = total.astype(BF16)
            r.rest_message[0] = total[:2]
            r.rest_message[1, 0] = r.up1_last[x]
            r.rest_message[1, 1] = total[2]

        rest = []
        for layer in range(2):
            leave = h.sem()
            src, dst = r.rest_message.at[layer], r.rest.at[z, h.s]
            copy = pltpu.make_async_remote_copy(
                src_ref=src, dst_ref=dst, send_sem=leave, recv_sem=arrive_rest, device_id=(layer, h.c, x),
                device_id_type=MESH)
            kept = pltpu.make_async_copy(src, dst, arrive_rest)
            is_self = (h.s == layer) & (x == h.y)
            pl.when(reduces & is_self)(kept.start)
            away = reduces & jnp.logical_not(is_self)
            pl.when(away)(copy.start)
            rest.append((away, copy))
        wait_bytes(r.qkv_in, arrive_qkv)
        for i, parts in enumerate((r.qkv_low, r.qkv_high)):
            parts[x, z] = r.qkv_in[4 * i : 4 * i + 4, :, :384]
            spreads.append(Spread16(h, parts, i == 0))
            spreads[2 + i].start()
        own = r.qkv_in[0, :, 384:].astype(F32)
        for g in range(1, 8):
            own = own + r.qkv_in[g, :, 384:].astype(F32)
        r.own_sums[x, z] = own.astype(BF16)
        spreads.append(Spread16(h, r.own_sums, True))
        spreads[4].start()
        owner = x == h.y
        across = [h.sem() for _ in range(4)]
        along = [h.sem() for _ in range(3)]
        line = r.rest.at[z]

        @pl.when(owner)
        def _():
            wait_bytes(line, arrive_rest)

        wide = []
        for j in range(1, 4):
            wide.append(pltpu.make_async_remote_copy(
                src_ref=line, dst_ref=line, send_sem=across[j], recv_sem=across[0],
                device_id=(h.s, 4 * lax.rem(x + j, 4) + z, h.y), device_id_type=MESH))

        @pl.when(owner)
        def _():
            for copy in wide:
                copy.start()

        @pl.when(jnp.logical_not(owner))
        def _():
            wait_bytes(line, across[0])

        for j in range(1, 4):
            h.send(line, line, (h.s, 4 * x + lax.rem(z + j, 4), h.y), along[j - 1])
        for each in spreads[2:]:
            each.middle()
        for each in spreads:
            each.finish()
        for sem in along:
            wait_bytes(line, sem)

        @pl.when(owner)
        def _():
            for copy in wide:
                copy.wait_send()

        for away, copy in rest:
            pl.when(away)(copy.wait_send)
        h.finish()

    ins = dict(
        qkv0=(qkv0, ANY), qkv0_last=(qkv0_last, VMEM), up0_piece=(up0_piece, VMEM), up0_last=(up0_last, VMEM),
        up1=(up1, ANY), up1_last=(up1_last, VMEM), qkv1_piece=(qkv1_piece, VMEM), qkv1_last=(qkv1_last, VMEM))
    up_half, qkv_half = (spec((4, 4, 4, 16, WINDOW)), VMEM), (spec((4, 4, 4, 16, 384)), VMEM)
    outs = dict(
        up_low=up_half, up_high=up_half, qkv_low=qkv_half, qkv_high=qkv_half,
        own_sums=(spec((4, 4, 16, 256)), VMEM), rest=(spec((4, 2, 2, 16, WINDOW)), VMEM))
    scratch = dict(
        part=VMEM((2, 4, 4, 2, 16, WINDOW), BF16), sums_a=reduce_scratch(2), sums_b=reduce_scratch(2),
        up1_vm=VMEM((SHARD, 16, WINDOW), BF16), qkv0_piece=VMEM((SHARD, 16, WINDOW), BF16),
        last_message=VMEM((SHARD, 3, 16, WINDOW), BF16), last_in=VMEM((CTX, 3, 16, WINDOW), BF16),
        up_in=VMEM((8, 16, WINDOW), BF16), qkv_in=VMEM((8, 16, WINDOW), BF16),
        rest_message=VMEM((2, 2, 16, WINDOW), BF16), sems=pltpu.SemaphoreType.DMA((160,)))
    return call("share", body, ins, outs, scratch, collective_id=6)


def settle_kernel(layers):
    def body(r):
        h = Here(r.sems)
        parts = [r.layer0, r.layer1]
        group = 2 * h.y + h.s
        loads = [h.local(parts[layer][0], r.down_vm.at[layer]) for layer in range(2)]
        h.barrier(whole=False)
        arrive_out, arrive_last, arrive_down = (h.sem() for _ in range(3))
        for copy in loads:
            copy.wait()
        for layer in range(2):
            out = parts[layer][1]
            h.send_or_keep(r.down_vm.at[layer], r.down.at[h.s], (layer, h.c, h.y), h.s == layer, arrive_down)
            for i in range(8):
                tile = 8 * group + i
                to = tile // 17
                row = pl.multiple_of(lax.rem(tile, 17) * 16, 16)
                h.send_or_keep(
                    out.at[pl.ds(16 * i, 16)], r.out_in.at[pl.ds(row, 16)], (layer, h.c, to),
                    (h.s == layer) & (to == h.y), arrive_out)
            h.send_or_keep(
                out.at[pl.ds(128, 64)], r.last_in.at[group], (layer, h.c, SHARD - 1),
                (h.s == layer) & (h.y == SHARD - 1), arrive_last)

        @pl.when(h.y < SHARD - 1)
        def _():
            wait_bytes(r.out_in, arrive_out)
            r.out[...] = r.out_in[...].astype(F32)

        @pl.when(h.y == SHARD - 1)
        def _():
            wait_bytes(r.out_in.at[pl.ds(0, SLICE - 64)], arrive_out)
            wait_bytes(r.last_in, arrive_last)
            r.out[: SLICE - 64] = r.out_in[: SLICE - 64].astype(F32)
            total = r.last_in[0].astype(F32)
            for g in range(1, 8):
                total = total + r.last_in[g].astype(F32)
            r.out[SLICE - 64 :] = total

        wait_bytes(r.down, arrive_down)
        h.finish()

    spaces = [ANY, VMEM]
    ins = dict(layer0=list(zip(layers[0], spaces)), layer1=list(zip(layers[1], spaces)))
    outs = dict(out=(spec((SLICE, D), F32), VMEM), down=(spec((2, 544, D)), VMEM))
    scratch = dict(
        down_vm=VMEM((2, 544, D), BF16), out_in=VMEM((SLICE, D), BF16), last_in=VMEM((8, 64, D), BF16),
        sems=pltpu.SemaphoreType.DMA((64,)))
    return call("settle", body, ins, outs, scratch, collective_id=7)


def join_kernel(share):
    def body(up_low, up_high, qkv_low, qkv_high, own_sums, rest, up_ref, qkv_ref, norm_ref):
        def join(windows, blocks, own):
            for g in range(8):
                main = windows[g][:, :512]
                if g % 4:
                    main = jnp.concatenate([main[:, :128] + windows[g - 1][:, 512:], main[:, 128:]], axis=1)
                at = 128 * (17 * g // 4)
                up_ref[:, at : at + 512] = main
                if g % 4 == 3:
                    up_ref[:, at + 512 : at + 640] = windows[g][:, 512:]
            queries = [blocks[g][:, :128] for g in range(8)] + [own[:, :64]]
            keys = [blocks[g][:, a : a + 64] for g in range(8) for a in (128, 256)] + [own[:, 64:128]]
            values = [blocks[g][:, a : a + 64] for g in range(8) for a in (192, 320)] + [own[:, 128:192]]
            qkv_ref[...] = jnp.concatenate(queries + keys + values, axis=1)
            norm_ref[...] = jnp.concatenate([own[:, 192:], jnp.zeros((16, 64), F32)], axis=1)

        @pl.when(pl.program_id(0) < CTX)
        def _():
            windows = [ref[0, 0, g].astype(F32) for ref in (up_low, up_high) for g in range(4)]
            blocks = [ref[0, 0, g].astype(F32) for ref in (qkv_low, qkv_high) for g in range(4)]
            join(windows, blocks, own_sums[0, 0].astype(F32))

        @pl.when(pl.program_id(0) == CTX)
        def _():
            windows = [rest[g // 2, g % 2, 0].astype(F32) for g in range(8)]
            blocks = [rest[g // 2, g % 2, 1].astype(F32) for g in range(8)]
            own = blocks[0][:, 384:]
            for g in range(1, 8):
                own = own + blocks[g][:, 384:]
            join(windows, blocks, own)

    def chip(*block):
        zeros = (0,) * len(block)
        return pl.BlockSpec((1, 1, *block), lambda i: (jnp.minimum(i, 15) // 4, jnp.minimum(i, 15) % 4, *zeros))

    def rows(width):
        return pl.BlockSpec((16, width), lambda i: (i, 0))

    return pl.pallas_call(
        body,
        grid=(17,),
        out_shape=(spec((SLICE, FF), F32), spec((SLICE, 3 * D), F32), spec((SLICE, 128), F32)),
        in_specs=[
            chip(4, 16, WINDOW), chip(4, 16, WINDOW), chip(4, 16, 384), chip(4, 16, 384), chip(16, 256),
            pl.BlockSpec((4, 2, 2, 16, WINDOW), lambda i: (0,) * 5)],
        out_specs=(rows(FF), rows(3 * D), rows(128)),
        name="join",
    )(share.up_low, share.up_high, share.qkv_low, share.qkv_high, share.own_sums, share.rest)


def token_positions(block_order):
    offsets = jnp.arange(32, dtype=jnp.int32)
    groups = jnp.arange(2, dtype=jnp.int32)[:, None, None] * GROUP
    return (groups + block_order[:, :, None] * 32 + offsets).reshape(2, GROUP)


def swapped(section, first, second):
    own = jnp.where(section == 0, first, second)
    other = lax.ppermute(jnp.where(section == 0, second, first), SECTION, [(0, 1), (1, 0)])
    return jnp.where(section == 0, own, other), jnp.where(section == 0, other, own)


def gathered(x):
    return lax.all_gather(x, CONTEXT)


def shards(hidden_in, cotangent, block_order, qkv_weight, out_weight, up_weight, down_weight, norm_gains, norm_biases):
    section, ctx = lax.axis_index(SECTION), lax.axis_index(CONTEXT)
    params = jnp.concatenate([norm_gains[0], norm_biases[0]], axis=0).astype(F32)
    params = jnp.pad(params, ((0, 4), (0, 0)))
    grid = token_positions(block_order)
    own_positions = lax.dynamic_slice(grid, (section, ctx * ROWS), (1, ROWS))
    positions = grid.reshape(1, SEQ)
    hidden = hidden_in[0]
    spread = spread_kernel(params, qkv_weight, up_weight)
    norms = spread.norms
    mid_all = gathered(spread.mid_piece)
    first = first_kernel(hidden, norms, qkv_weight, out_weight, down_weight)
    up_piece, q16 = lax.optimization_barrier((spread.up_piece, first.q16))
    up_all = gathered(up_piece)
    at = (block_order, positions, own_positions.reshape(ROWS, 1))
    attended0 = attend(*at, first.message_in, first.kv16_in, q16)
    middle = middle_kernel(attended0.out, attended0.out16, hidden, norms, first, mid_all, spread.mid_last)
    attended1 = attend(*at, middle.message_in, middle.kv16_in, middle.q16)
    turn = turn_kernel(
        attended1.out, attended1.out16, middle.y, norms, first, up_all, spread.up_last, cotangent[0])
    up1, up1_last, down1, out1 = lax.psum((turn.up_g, turn.up_g_last, turn.down_g, turn.out_g), CONTEXT)
    at = (block_order, positions.reshape(SEQ, 1), own_positions)
    back1 = attend_back(
        *at, middle.message_in, middle.kv16_in, middle.q16, attended1, turn.context_grad_in, turn.context16_grad)
    back = back_kernel(
        back1, middle.a_full, middle.y, turn, norms, first, middle, attended0.out16, mid_all, spread.mid_last)
    (down_g, out_g), (up1, up1_last, down1, out1) = lax.optimization_barrier(
        ((back.down_g, back.out_g), (up1, up1_last, down1, out1)))
    down0, out0 = lax.psum((down_g, out_g), CONTEXT)
    back0 = attend_back(
        *at, first.message_in, first.kv16_in, first.q16, attended0, back.context_grad_in, back.context16_grad)
    last = last_kernel(back0, first.a_full, hidden, back, norms, first.qkv_w)
    share = share_kernel(
        last.qkv_g, last.qkv_g_last, last.up_piece, back.up_g_last, up1, up1_last, last.qkv_piece, back.qkv_g_last)
    up, qkv, norm_sums = join_kernel(share)
    settle = settle_kernel(((down0, out0), (down1, out1)))
    norm_sums = norm_sums[:, :4].T
    activations = jnp.stack(swapped(section, middle.y, turn.out))
    input_grads = jnp.stack(swapped(section, last.in_grad, back.in_grad))
    return (
        activations[None, None],
        input_grads[None, None],
        qkv[None],
        settle.out[None],
        up[None],
        settle.down.reshape(D, D).astype(F32)[None],
        norm_sums[None, 0::2],
        norm_sums[None, 1::2],
    )


def solution(mesh):
    tokens = P(LINE, None, CONTEXT, None)
    rows = P(SECTION, LINE, None)
    norms = P(SECTION, None, LINE)
    layers = P(SECTION, LINE, None, CONTEXT, None)
    return jax.shard_map(
        shards,
        mesh=mesh,
        in_specs=(tokens, tokens, P(), rows, rows, rows, rows, norms, norms),
        out_specs=(layers, layers, rows, rows, rows, rows, norms, norms),
        check_vma=False,
    )
```

time: 1640 us -> 513 us (0.31)
  waiting for transfers between devices: 743 us -> 22.1 us
  matrix products: 392 us -> 0 us
  Pallas kernels: 176 us -> 451 us
  local copies, waits for them, and re-layouts: 167 us -> 7.64 us
  other arithmetic: 73.9 us -> 8.53 us
  blocking collectives: 42.8 us -> 0 us
    all_gather x5 -> x2, waiting for transfers between devices: 370 us -> 0.01 us  [gathered(): return lax.all_gather(x, CONTEXT)]
    dot_general x60 -> x0, matrix products: 338 us -> none  [the longest x12 99.6 us: matmul_tn(): lax.dot_general(left_side, right_side, (((0,), (0,)), ((), ())), preferre...]
    pallas_call x3 -> x13, Pallas kernels: 176 us -> 451 us  [the longest x12 439 us: call(): pl.pallas_call(kernel, out_shape=tuple((value[0] for value in outs.values...]
    reduce_scatter x2 -> x0, waiting for transfers between devices: 211 us -> none  [the longest x1 121 us: in_one_piece_2(): lax.psum_scatter(both, axis, scatter_dimension=dim, tiled=True)]
    unnamed x16 -> x4, waiting for transfers between devices: 157 us -> 0.07 us
    slice x20 -> x2, local copies, waits for them, and re-layouts: 71.3 us -> 0.52 us  [the longest x1 0.28 us: shards(): norm_sums[None, 1::2]]
    sub x6 -> x0, matrix products: 54.5 us -> none  [attention_probs(): exponent = jnp.exp(scores - row_max)]
    concatenate x2 -> x0, local copies, waits for them, and re-layouts: 40.2 us -> none  [the longest x1 31.1 us: in_one_piece_2(): both = jnp.concatenate(arrays, axis=along)]
  transfers between devices with their start and end apart: 17 -> 6, of which waited for: 12 -> 2; matrix products, arithmetic and copies ran while one was open for 13% -> 2% of each run, Pallas kernels for 11% -> 69%
where the time goes in v2:
time: 513 us; the launch traced here: 506 us
  Pallas kernels  451 us (88%)
  waiting for transfers between devices  22.1 us (4%)
  between operations  14.4 us (3%)
  other arithmetic  8.53 us (2%)
  local copies, waits for them, and re-layouts  7.64 us (1%)
    pallas_call x12, Pallas kernels, call(): pl.pallas_call(kernel, out_shape=tuple((value[0] for value in outs.values...  439 us
    psum x1, waiting for transfers between devices, shards(): down0, out0 = lax.psum((down_g, out_g), CONTEXT)  21.8 us
    pallas_call x1, Pallas kernels, join_kernel(): pl.pallas_call(body, grid=(17,), out_shape=(spec((SLICE, FF), F32), spec(...  11.9 us
  transfers between devices with their start and end apart: 6, of which 2 were waited for; matrix products, arithmetic and copies ran while one was open for 2% of the time, Pallas kernels for 69%

profile of v2, /device:TPU:1, one launch (start us, length us, event | category | flops | bytes accessed | tf_op | source)
XLA Modules:
  0.0 505.9 jit_solution(5515358449659043406)
XLA Ops:
  7.2 1.3 fusion.3.refs_0_
  8.5 14.3 %spread.1 = (f32[2,8,1088]{2,1,0:T(8,128)}, bf16[8,16,640]{2,1,0:T(8,128)(2,1)}, bf16[8,16,640]{2,1,0:T(8,128)(2,1)}, bf16[4,16,640]{2,1,0:T(8,128)(2,1)}, bf16[4,16,640]{2,1,0:T(8,128)(2,1)}) custom-call(f32[8,272]{1,0:T(8,128)} %fusion.3.refs_0_, bf16[1,272,3264]{2,1,0:T(8,128)(2,1)} %refs_2_.3, bf16[1,272,4352]{2,1,0:T(8,128)(2,1)} %refs_2_.2), custom_call_target="tpu_custom_call" | custom-call | tf_op jit(solution)/shard_map/spread/pallas_call | solution.py:53
  22.9 50.2 %first.1 = (bf16[512,1088]{1,0:T(8,128)(2,1)}, bf16[16,160,128]{2,1,0:T(8,128)(2,1)}, bf16[2,16,64,128]{3,2,1,0:T(8,128)(2,1)}, bf16[64,64]{1,0:T(8,128)(2,1)}, ...) custom-call(bf16[2,64,1088]{2,1,0:T(8,128)(2,1)} %bitcast.32, ...), custom_call_target="tpu_custom_call" | custom-call | tf_op jit(solution)/shard_map/first/pallas_call | solution.py:53
  73.4 0.7 add.78.refs_1_
  74.4 0.7 copy.27.refs_2_
  75.2 5.5 %attend.2 = (bf16[16,32,128]{2,1,0:T(8,128)(2,1)}, bf16[64,64]{1,0:T(8,128)(2,1)}, bf16[1024,64]{1,0:T(8,128)(2,1)}, f32[1024,128]{1,0:T(8,128)}, f32[64,128]{1,0:T(8,128)}) custom-call(s32[2,32]{1,0:T(2,128)} %refs_0_.7, s32[1,2048]{1,0:T(1,128)} %add.78.refs_1_, s32[64,1]{1,0:T(8,128)} %copy.27.refs_2_, bf16[16,160,128]{2,1,0:T(8,128)(2,1)} %get-tuple-element.90.refs_3_, ...), custom_call_target="tpu_custom_call" | custom-call | tf_op jit(solution)/shard_map/attend/pallas_call | solution.py:53
  80.6 63.5 %middle.1 = (bf16[512,128]{1,0:T(8,128)(2,1)}, f32[64,1088]{1,0:T(8,128)}, bf16[512,1088]{1,0:T(8,128)(2,1)}, f32[512,640]{1,0:T(8,128)}, bf16[64,1088]{1,0:T(8,...) custom-call(bf16[16,32,128]{2,1,0:T(8,128)(2,1)} %get-tuple-element., ...), custom_call_target="tpu_custom_call" | custom-call | tf_op jit(solution)/shard_map/middle/pallas_call | solution.py:53
  144.1 5.5 %attend.3 = (bf16[16,32,128]{2,1,0:T(8,128)(2,1)}, bf16[64,64]{1,0:T(8,128)(2,1)}, bf16[1024,64]{1,0:T(8,128)(2,1)}, f32[1024,128]{1,0:T(8,128)}, f32[64,128]{1,0:T(8,128)}) custom-call(s32[2,32]{1,0:T(2,128)} %refs_0_.7, s32[1,2048]{1,0:T(1,128)} %add.78.refs_1_, s32[64,1]{1,0:T(8,128)} %copy.27.refs_2_, bf16[16,160,128]{2,1,0:T(8,128)(2,1)} %get-tuple-element.102.refs_3_, ...), custom_call_target="tpu_custom_call" | custom-call | tf_op jit(solution)/shard_map/attend/pallas_call | solution.py:53
  149.7 68.7 %turn.1 = (bf16[64,1088]{1,0:T(8,128)(2,1)}, f32[64,1088]{1,0:T(8,128)}, bf16[16,32,128]{2,1,0:T(8,128)(2,1)}, bf16[64,64]{1,0:T(8,128)(2,1)}, bf16[4,4,4,16,640...) custom-call(bf16[16,32,128]{2,1,0:T(8,128)(2,1)} %get-tuple-element., ...), custom_call_target="tpu_custom_call" | custom-call | tf_op jit(solution)/shard_map/turn/pallas_call | solution.py:53
  218.4 0.4 all-reduce.6.cloned.1.call-start
  218.8 2.1 add.87.refs_1_
  220.9 1.4 collective-permute-start
  222.3 8.7 %attend_back.2 = (bf16[16,160,128]{2,1,0:T(8,128)(2,1)}, bf16[2,16,64,128]{3,2,1,0:T(8,128)(2,1)}, bf16[64,64]{1,0:T(8,128)(2,1)}) custom-call(s32[2,32]{1,0:T(2,128)} %refs_0_.7, s32[2048,1]{1,0:T(8,128)} %add.87.refs_1_, s32[1,64]{1,0:T(1,128)} %copy-done.7, bf16[16,160,128]{2,1,0:T(8,128)(2,1)} %get-tuple-element.102.refs_3_, ...), custom_call_target="tpu_custom_call" | custom-call | tf_op jit(solution)/shard_map/attend_back/pallas_call | solution.py:53
  230.9 74.6 %back.1 = (bf16[64,1088]{1,0:T(8,128)(2,1)}, bf16[4,4,4,16,640]{4,3,2,1,0:T(8,128)(2,1)}, bf16[4,16,640]{2,1,0:T(8,128)(2,1)}, f32[64,1088]{1,0:T(8,128)}, bf16[...) custom-call(bf16[16,160,128]{2,1,0:T(8,128)(2,1)} %get-tuple-element, ...), custom_call_target="tpu_custom_call" | custom-call | tf_op jit(solution)/shard_map/back/pallas_call | solution.py:53
  305.6 8.7 %attend_back.3 = (bf16[16,160,128]{2,1,0:T(8,128)(2,1)}, bf16[2,16,64,128]{3,2,1,0:T(8,128)(2,1)}, bf16[64,64]{1,0:T(8,128)(2,1)}) custom-call(s32[2,32]{1,0:T(2,128)} %refs_0_.7, s32[2048,1]{1,0:T(8,128)} %add.87.refs_1_, s32[1,64]{1,0:T(1,128)} %copy-done.7, bf16[16,160,128]{2,1,0:T(8,128)(2,1)} %get-tuple-element.90.refs_3_, ...), custom_call_target="tpu_custom_call" | custom-call | tf_op jit(solution)/shard_map/attend_back/pallas_call | solution.py:53
  314.2 46.5 %last.1 = (bf16[64,1088]{1,0:T(8,128)(2,1)}, bf16[4,4,4,16,640]{4,3,2,1,0:T(8,128)(2,1)}, bf16[4,16,640]{2,1,0:T(8,128)(2,1)}, bf16[4,16,640]{2,1,0:T(8,128)(2,1)}, bf16[4,16,640]{2,1,0:T(8,128)(2,1)}) custom-call(bf16[16,160,128]{2,1,0:T(8,128)(2,1)} %get-tuple-element.130.refs_0_, bf16[2,16,64,128]{3,2,1,0:T(8,128)(2,1)} %get-tuple-element.131.refs_1_, ...), custom_call_target="tpu_custom_call" | custom-call | tf_op jit(solution)/shard_map/last/pallas_call | solution.py:53
  360.8 1.0 broadcast_select_fusion
  361.8 0.4 collective-permute-start.1
  362.3 0.8 maximum_bitcast_fusion
  363.0 0.2 collective-permute-done.1
  363.3 0.8 maximum_bitcast_fusion.1
  364.0 71.6 %share.1 = (bf16[4,4,4,16,640]{4,3,2,1,0:T(8,128)(2,1)}, bf16[4,4,4,16,640]{4,3,2,1,0:T(8,128)(2,1)}, bf16[4,4,4,16,384]{4,3,2,1,0:T(8,128)(2,1)}, bf16[4,4,4,16...) custom-call(bf16[4,4,4,16,640]{4,3,2,1,0:T(8,128)(2,1)} %get-tuple-element.141.refs_0_, ...), custom_call_target="tpu_custom_call" | custom-call | tf_op jit(solution)/shard_map/share/pallas_call | solution.py:53
  435.6 11.9 %join.1 = (f32[272,4352]{1,0:T(8,128)}, f32[272,3264]{1,0:T(8,128)}, f32[272,128]{1,0:T(8,128)}) custom-call(bf16[4,4,4,16,640]{4,3,2,1,0:T(8,128)(2,1)} %get-tuple-element.155.up_low, bf16[4,4,4,16,640]{4,3,2,1,0:T(8,128)(2,1)} %get-tuple-element.156.up_high, bf16[4,4,4,16,384]{4,3,2,1,0:T(8,128)(2,1)} %get-tuple-element.157.qkv_low, ...), custom_call_target="tpu_custom_call" | custom-call | tf_op jit(solution)/shard_map/join/pallas_call | solution.py:1364
  447.5 0.9 slice_bitcast_fusion
  448.5 0.3 slice.11
  448.8 0.2 slice.10
  449.0 0.7 copy.31
  449.7 0.7 copy.32
  450.4 21.8 %all-reduce.6.cloned.1.call-done = (bf16[544,1088]{1,0:T(8,128)(2,1)}, bf16[192,1088]{1,0:T(8,128)(2,1)}) async-done(((bf16[544,1088]{1,0:T(8,128)(2,1)}, bf16[192,1088]{1,0:T(8,128)(2,1)}), (bf16[544,1088]{1,0:T(8,128)(2,1)}, bf16[192,1088]{1,0:T(8,128)(2,1)})) %all-reduce.6.cloned.1.call-update) | async-done | bytes 1601552 | tf_op jit(solution)/shard_map/psum | solution.py:1420
  472.2 21.3 %settle.1 = (f32[272,1088]{1,0:T(8,128)}, bf16[2,544,1088]{2,1,0:T(8,128)(2,1)}) custom-call(bf16[544,1088]{1,0:T(8,128)(2,1)} %get-tuple-element.194.refs_0_, bf16[192,1088]{1,0:T(8,128)(2,1)} %get-tuple-element.195.refs_1_, bf16[544,1088]{1,0:T(8,128)(2,1)} %get-tuple-element.164.refs_2_, bf16[192,1088]{1,0:T(8,128)(2,1)} %get-tuple-element.165.refs_3_), custom_call_target="tpu_custom_call" | custom-call | tf_op jit(solution)/shard_map/settle/pallas_call | solution.py:53
  493.5 4.4 bitcast_convert_fusion
  497.9 1.0 copy.40
  (39 shorter events, 0.9 us)
Async XLA Ops:
  7.2 73.5 %all-gather.5.cloned.1.call-start = ((), (), s32[]{:S(2)}) async-start(), calls=%async_computation | async-start | bytes 2785280 | tf_op jit(solution)/shard_map/all_gather | solution.py:1389
  22.9 126.8 %all-gather.7.cloned.1.call-start = ((), (), s32[]{:S(2)}) async-start(), calls=%async_computation.1 | async-start | bytes 1392640 | tf_op jit(solution)/shard_map/all_gather | solution.py:1389
  22.9 50.4 %copy-start.6 = (s32[2,32]{1,0:T(2,128)S(1)}, s32[2,32]{1,0:T(2,128)}, u32[]{:S(2)}) copy-start(s32[2,32]{1,0:T(2,128)} %refs_0_.7) | copy-start | bytes 772
  73.1 289.0 %all-reduce.8.cloned.1.call-start = ((), (), s32[]{:S(2)}) async-start(), calls=%async_computation.3 | async-start | bytes 6176768 | tf_op jit(solution)/shard_map/psum | solution.py:1412
  74.4 69.7 %copy-start.7 = (s32[1,64]{1,0:T(1,128)}, s32[1,64]{1,0:T(1,128)S(1)}, u32[]{:S(2)}) copy-start(s32[1,64]{1,0:T(1,128)S(1)} %dynamic-slice_add_fusion.refs_2_) | copy-start | bytes 772
  218.3 2.6 copy-start
  218.3 2.5 copy-start.3
  218.4 253.8 %all-reduce.6.cloned.1.call-start = ((), (), s32[]{:S(2)}) async-start(), calls=%async_computation.2 | async-start | bytes 3391488 | tf_op jit(solution)/shard_map/psum | solution.py:1420
  220.9 141.3 %collective-permute-start = (bf16[64,1088]{1,0:T(8,128)(2,1)S(1)}, bf16[64,1088]{1,0:T(8,128)(2,1)S(1)}, u32[]{:S(2)}, u32[]{:S(2)}) collective-permute-start(bf16[64,1088]{1,0:T(8,128)(2,1)S(1)} %broadcast_select_fusion.2), channel_id=1, source_target_pairs={{0,64},{64,0},{1,65},{65,1},{2,66},{66,2},{3,67},{67,3},{4,68},{68... | collective-permute-start | bytes 417800 | tf_op jit(solution)/shard_map/ppermute | solution.py:1384
  314.2 46.6 %copy-start.4 = (bf16[64,1088]{1,0:T(8,128)(2,1)S(1)}, bf16[64,1088]{1,0:T(8,128)(2,1)}, u32[]{:S(2)}) copy-start(bf16[64,1088]{1,0:T(8,128)(2,1)} %get-tuple-element.140) | copy-start | bytes 417796
  360.8 1.5 copy-start.1
  361.8 1.5 collective-permute-start.1
  362.2 1.0 copy-start.5
  493.5 4.4 copy-start.2
Sparse Core Ops, SparseCore 0:
  23.0 53.4 all-gather.4
  78.7 42.6 all-gather.6
  218.5 108.8 all-reduce.7
  362.3 109.8 all-reduce.5

commit v3 on v2

v3 whole, which is shorter than its diff:
```python
import functools
import types

import jax
import jax.numpy as jnp
from jax import lax
from jax.experimental import pallas as pl
from jax.experimental.pallas import tpu as pltpu
from jax.sharding import PartitionSpec as P

D = 1088
HEADS = 17
HEAD_DIM = 64
FF = 4352
SHARD = 4
CTX = 16
ROWS = 64
GROUP = 1024
SEQ = 2048
WINDOW = 640
SLICE = D // SHARD
EPSILON = 1e-05
NEG_LARGE = -1e30
BF16 = jnp.bfloat16
F32 = jnp.float32
MESH = pl.DeviceIdType.MESH
VMEM = pltpu.VMEM
ANY = pl.ANY
VMEM_BYTES = 56 * 2**20
SECTION, CONTEXT, LINE = "section", "ctx", "shard"
TILES = (68, 16, WINDOW)


def spec(shape, dtype=BF16):
    return jax.ShapeDtypeStruct(shape, dtype)


def call(name, body, ins, outs, scratch, collective_id=None):
    def kernel(*refs):
        refs, found = list(refs), {}
        for key, value in [*ins.items(), *outs.items(), *scratch.items()]:
            if isinstance(value, list):
                found[key], refs = refs[: len(value)], refs[len(value) :]
            else:
                found[key] = refs.pop(0)
        body(types.SimpleNamespace(**found))

    extra = {} if collective_id is None else dict(collective_id=collective_id, has_side_effects=True)
    shapes, given = [], []
    for value in scratch.values():
        shapes += value if isinstance(value, list) else [value]
    for value in ins.values():
        given += value if isinstance(value, list) else [value]
    results = pl.pallas_call(
        kernel,
        out_shape=tuple(value[0] for value in outs.values()),
        in_specs=[pl.BlockSpec(memory_space=space) for _, space in given],
        out_specs=tuple(pl.BlockSpec(memory_space=value[1]) for value in outs.values()),
        scratch_shapes=shapes,
        compiler_params=pltpu.CompilerParams(vmem_limit_bytes=VMEM_BYTES, **extra),
        name=name,
    )(*(array for array, _ in given))
    return types.SimpleNamespace(**dict(zip(outs, results)))


def dot(a, b):
    return jnp.dot(a, b, preferred_element_type=F32)


def dot_nt(a, b):
    return lax.dot_general(a, b, (((1,), (1,)), ((), ())), preferred_element_type=F32)


def dot_tn(a, b):
    return lax.dot_general(a, b, (((0,), (0,)), ((), ())), preferred_element_type=F32)


def norm_parts(values):
    center = values - jnp.mean(values, axis=-1, keepdims=True)
    rate = lax.rsqrt(jnp.mean(center * center, axis=-1, keepdims=True) + EPSILON)
    return center * rate, rate


def layer_norm(values, gain, bias):
    return norm_parts(values)[0] * gain + bias


def gelu(u):
    return 0.5 * u * (1.0 + jnp.tanh(0.7978845608028654 * (u + 0.044715 * u * u * u)))


class Here:
    def __init__(self, sems):
        self.s = lax.axis_index(SECTION)
        self.c = lax.axis_index(CONTEXT)
        self.y = lax.axis_index(LINE)
        self.sems, self.used, self.sent = sems, 0, []

    def sem(self):
        self.used += 1
        return self.sems.at[self.used - 1]

    def shard(self, step):
        return lax.rem(self.y + step, SHARD)

    def rows(self, shard, core):
        return pl.ds(pl.multiple_of((shard * 2 + core) * ROWS, ROWS), ROWS)

    def barrier(self, whole=True):
        sem = pltpu.get_barrier_semaphore()
        peers = []
        for step in range(SHARD):
            for core in range(2):
                if step or core:
                    peers.append((lax.rem(self.s + core, 2), self.c, self.shard(step)))
        for step in range(1, CTX if whole else 1):
            for core in range(2):
                peers.append((core, lax.rem(self.c + step, CTX), self.y))
        for to in peers:
            pl.semaphore_signal(sem, inc=1, device_id=to, device_id_type=MESH)
        self.awaited = len(peers)

    def ready(self):
        pl.semaphore_wait(pltpu.get_barrier_semaphore(), self.awaited)

    def save_on(self, core, src, dst):
        copy = pltpu.make_async_copy(src, dst, self.sem())
        pl.when(self.s == core)(copy.start)
        self.sent.append(types.SimpleNamespace(wait_send=lambda: pl.when(self.s == core)(copy.wait)))

    def local(self, src, dst):
        copy = pltpu.make_async_copy(src, dst, self.sem())
        copy.start()
        return copy

    def save(self, src, dst):
        copy = self.local(src, dst)
        self.sent.append(types.SimpleNamespace(wait_send=copy.wait))

    def send(self, src, dst, to, arrive, leave=None):
        copy = pltpu.make_async_remote_copy(
            src_ref=src, dst_ref=dst, send_sem=self.sem() if leave is None else leave,
            recv_sem=arrive, device_id=to, device_id_type=MESH)
        copy.start()
        if leave is None:
            self.sent.append(copy)
        return copy

    def send_or_keep(self, src, dst, to, is_self, arrive):
        leave = self.sem()
        copy = pltpu.make_async_remote_copy(
            src_ref=src, dst_ref=dst, send_sem=leave, recv_sem=arrive, device_id=to, device_id_type=MESH)
        kept = pltpu.make_async_copy(src, dst, arrive)
        pl.when(jnp.logical_not(is_self))(copy.start)
        pl.when(is_self)(kept.start)

        def wait_send():
            pl.when(jnp.logical_not(is_self))(copy.wait_send)

        self.sent.append(types.SimpleNamespace(wait_send=wait_send))

    def sibling(self):
        return (1 - self.s, self.c, self.y)

    def finish(self):
        for copy in self.sent:
            copy.wait_send()
        self.sent = []


def wait_bytes(ref, sem):
    pltpu.make_async_copy(ref, ref, sem).wait()


HALF = ROWS // 2


def half_rows(half):
    return slice(HALF * half, HALF * half + HALF)


class Gather8:
    def __init__(self, here, full):
        self.here, self.full = here, full
        self.own = [[here.sem() for _ in range(2)] for _ in range(SHARD)]
        self.other = [[here.sem() for _ in range(2)] for _ in range(SHARD)]

    def rows(self, shard, core, half):
        return self.full.at[pl.ds(pl.multiple_of((shard * 2 + core) * ROWS + half * HALF, HALF), HALF)]

    def start(self, value, half):
        h = self.here
        mine = self.rows(h.y, h.s, half)
        mine[...] = value
        h.send(mine, mine, h.sibling(), self.other[0][half])
        for step in (1, 3, 2):
            h.send(mine, mine, (h.s, h.c, h.shard(step)), self.own[SHARD - step][half])

    def relay(self, step):
        h = self.here
        for half in range(2):
            part = self.rows(h.shard(step), h.s, half)
            wait_bytes(part, self.own[step][half])
            h.send(part, part, h.sibling(), self.other[step][half])

    def wait(self, step):
        h = self.here
        for half in range(2):
            wait_bytes(self.rows(h.shard(step), 1 - h.s, half), self.other[step][half])


class Scatter8:
    def __init__(self, here, bufs):
        self.here = here
        self.to_core, self.mine, self.from_core, self.to_shard, self.from_shard = bufs
        self.core = [[here.sem() for _ in range(2)] for _ in range(SHARD)]
        self.shard = [[here.sem() for _ in range(2)] for _ in range(SHARD)]

    def part(self, ref, step, half):
        return ref.at[step, pl.ds(half * HALF, HALF)]

    def put(self, step, block):
        h = self.here
        low, high = block[:ROWS], block[ROWS:]
        self.to_core[step] = jnp.where(h.s == 0, high, low).astype(BF16)
        self.mine[step] = jnp.where(h.s == 0, low, high)
        for half in range(2):
            h.send(
                self.part(self.to_core, step, half), self.part(self.from_core, step, half), h.sibling(),
                self.core[step][half])

    def relay(self, steps):
        h = self.here
        for half in range(2):
            for step in steps:
                part = self.part(self.from_core, step, half)
                wait_bytes(part, self.core[step][half])
                total = self.mine[step, half_rows(half)] + part[...].astype(F32)
                out = self.part(self.to_shard, step, half)
                out[...] = total.astype(BF16)
                h.send(
                    out, self.part(self.from_shard, step, half), (h.s, h.c, h.shard(step)), self.shard[step][half])

    def result(self, half):
        part = self.part(self.from_core, 0, half)
        wait_bytes(part, self.core[0][half])
        total = self.mine[0, half_rows(half)] + part[...].astype(F32)
        for step in (1, 3, 2):
            part = self.part(self.from_shard, step, half)
            wait_bytes(part, self.shard[step][half])
            total = total + part[...].astype(F32)
        return total


def scatter_scratch():
    quarter = (SHARD, ROWS, D)
    return [VMEM(quarter, BF16), VMEM(quarter, F32), VMEM(quarter, BF16), VMEM(quarter, BF16), VMEM(quarter, BF16)]


ORDER = (0, 1, 3, 2)


def window_offset(group):
    return 32 * lax.rem(group, 4)


def everyone(h):
    for step in (1, 3, 2, 0):
        for other in range(2):
            yield step, other, (lax.rem(h.s + other, 2), h.c, h.shard(step))


def packed_qkv(rows, g):
    keys = rows[:, D + 128 * g : D + 128 * g + 128]
    values = rows[:, 2 * D + 128 * g : 2 * D + 128 * g + 128]
    return jnp.concatenate([
        rows[:, 128 * g : 128 * g + 128], keys[:, :64], values[:, :64], keys[:, 64:], values[:, 64:],
        rows[:, D - 64 : D], rows[:, 2 * D - 64 : 2 * D], rows[:, 3 * D - 64 : 3 * D], jnp.zeros_like(keys[:, :64])],
        axis=1)


def window(g):
    return slice(128 * (17 * g // 4), 128 * (17 * g // 4) + WINDOW)


def spread_kernel(params, w_qkv, w_up):
    def body(r):
        h = Here(r.sems)
        own = pl.ds(pl.multiple_of(h.c * 16, 16), 16)
        loads = [
            h.local(ref.at[0, rows], dst.at[pl.ds(16 * i, 16)])
            for ref, dst in ((r.w_up, r.up_rows), (r.w_qkv, r.qkv_rows)) for i, rows in enumerate((own, pl.ds(256, 16)))]
        h.barrier(whole=False)
        h.ready()
        arrive, arrive_mid, arrive_up = h.sem(), h.sem(), h.sem()
        mine = r.params_in.at[h.s * SHARD + h.y]
        mine[...] = r.params[...]
        for step, other, to in everyone(h):
            if step or other:
                h.send(mine, mine, to, arrive)
        for copy in loads:
            copy.wait()

        @pl.when(h.s == 0)
        def _():
            for g in range(8):
                r.mid[g] = r.up_rows[:, window(g)].reshape(2, 16, WINDOW)
                r.up[g] = packed_qkv(r.qkv_rows[...], g).reshape(2, 16, WINDOW)

        @pl.when(h.s == 1)
        def _():
            for g in range(8):
                r.mid[g] = packed_qkv(r.qkv_rows[...], g).reshape(2, 16, WINDOW)
                r.up[g] = r.up_rows[:, window(g)].reshape(2, 16, WINDOW)

        for step, other, to in everyone(h):
            g = 2 * to[2] + to[0]
            slot = h.s * SHARD + h.y
            for sem, source, targets in (
                    (arrive_up, r.up, (r.side_piece, r.side_last)), (arrive_mid, r.mid, (r.mid_piece, r.mid_last))):
                for half in range(2):
                    src, dst = source.at[g, half], targets[half].at[slot]
                    if step or other:
                        h.send(src, dst, to, sem)
                    else:
                        pltpu.make_async_copy(src, dst, sem).start()
        wait_bytes(r.params_in.at[pl.ds(0, 7)], arrive)
        for layer in range(2):
            r.norms[layer] = jnp.concatenate([r.params_in[layer * SHARD + i] for i in range(SHARD)], axis=1)
        wait_bytes(r.mid, arrive_mid)
        wait_bytes(r.up, arrive_up)
        h.finish()

    ins = dict(params=(params, VMEM), w_qkv=(w_qkv, ANY), w_up=(w_up, ANY))
    outs = dict(
        norms=(spec((2, 8, D), F32), VMEM), mid_piece=(spec((8, 16, WINDOW)), VMEM),
        mid_last=(spec((8, 16, WINDOW)), VMEM), side_piece=(spec((8, 16, WINDOW)), VMEM),
        side_last=(spec((8, 16, WINDOW)), VMEM))
    scratch = dict(
        params_in=VMEM((8, 8, SLICE), F32), up_rows=VMEM((32, FF), BF16), qkv_rows=VMEM((32, 3 * D), BF16),
        mid=VMEM((8, 2, 16, WINDOW), BF16), up=VMEM((8, 2, 16, WINDOW), BF16), sems=pltpu.SemaphoreType.DMA((64,)))
    return call("spread", body, ins, outs, scratch, collective_id=0)


def load_tiles(h, gathered, last, dst, first=0):
    copies = []
    for i in range(SHARD):
        copies.append(h.local(gathered.at[:, first + i], dst.at[pl.ds(17 * i, 16)]))
        copies.append(h.local(last.at[first + i], dst.at[17 * i + 16]))
    return copies


def place(value, parts, last):
    tiles = value.astype(BF16).reshape(68, 16, value.shape[1])
    for i in range(SHARD):
        for c in range(CTX):
            parts[c // 4, c % 4, i] = tiles[17 * i + c]
        last[i] = tiles[17 * i + 16]


def whole(ref):
    return ref[...].reshape(D, WINDOW)


class FirstWeights:
    def __init__(self, h, r):
        self.h, self.r = h, r
        self.arrive = [h.sem() for _ in range(3)]
        self.spreads = [Spread16(h, parts, i == 0) for i, parts in enumerate((r.qkv_low, r.qkv_high))]

    def load(self):
        h, r = self.h, self.r
        self.loads = [h.local(r.w_down.at[0], r.down_rows), h.local(r.w_out.at[0], r.out_rows)]

    def send_qkv(self):
        r = self.r
        for i, (each, parts) in enumerate(zip(self.spreads, (r.qkv_low, r.qkv_high))):
            parts[each.x, each.z] = r.side_piece[2 * i : 2 * i + 2]
            each.start()

    def send_qkv_on(self):
        for each in self.spreads:
            each.middle()

    def send_rest(self):
        h, r = self.h, self.r
        for copy in self.loads:
            copy.wait()
        for other in range(2):
            core = lax.rem(h.s + other, 2)
            at = pl.multiple_of(window_offset(h.y * 2 + core), 32)
            src = r.down_rows.at[pl.ds(pl.multiple_of(544 * core, 16), 544)]
            dst = r.down_vm.at[h.s, pl.ds(at, 544)]
            if other:
                h.send(src, dst, h.sibling(), self.arrive[1])
            else:
                pltpu.make_async_copy(src, dst, self.arrive[1]).start()
        self.tiles = []
        for i in range(17):
            tile = h.y * 17 + i
            group = jnp.minimum(tile // 8, 7)
            core, shard = lax.rem(group, 2), group // 2
            src = r.out_rows.at[pl.ds(16 * i, 16)]
            dst = r.out_vm.at[h.s, pl.ds(pl.multiple_of(lax.rem(tile, 8) * 16, 16), 16)]
            copy = pltpu.make_async_remote_copy(
                src_ref=src, dst_ref=dst, send_sem=h.sem(), recv_sem=self.arrive[2],
                device_id=(core, h.c, shard), device_id_type=MESH)
            same = pltpu.make_async_copy(src, dst, self.arrive[2])
            is_self = (core == h.s) & (shard == h.y)
            pl.when((tile < 64) & is_self)(same.start)
            away = (tile < 64) & jnp.logical_not(is_self)
            pl.when(away)(copy.start)
            self.tiles.append((away, copy))
        src, dst = r.out_rows.at[pl.ds(SLICE - 64, 64)], r.out_vm.at[h.s, pl.ds(128, 64)]
        same = pltpu.make_async_copy(src, dst, self.arrive[2])
        self.last = []
        for step, other, to in everyone(h):
            if step or other:
                self.last.append(pltpu.make_async_remote_copy(
                    src_ref=src, dst_ref=dst, send_sem=h.sem(), recv_sem=self.arrive[2], device_id=to,
                    device_id_type=MESH))

        @pl.when(h.y == SHARD - 1)
        def _():
            same.start()
            for copy in self.last:
                copy.start()

    def wait_qkv(self):
        r = self.r
        for each in self.spreads:
            each.finish()
        for i in range(SHARD):
            for c in range(CTX):
                parts = (r.qkv_low, r.qkv_high)[i // 2]
                r.qkv_vm[17 * i + c] = parts[c // 4, c % 4, i % 2]
            r.qkv_vm[17 * i + 16] = r.side_last[i]

    def finish(self):
        r, h = self.r, self.h
        wait_bytes(r.down_vm.at[:, pl.ds(0, 544)], self.arrive[1])
        h.save(r.down_vm, r.down_w)
        wait_bytes(r.out_vm, self.arrive[2])
        h.save(r.out_vm, r.out_w)

        for away, copy in self.tiles:
            pl.when(away)(copy.wait_send)

        @pl.when(h.y == SHARD - 1)
        def _():
            for copy in self.last:
                copy.wait_send()


def head_outs():
    return dict(
        a_full=(spec((512, D)), ANY), message_in=(spec((CTX, 160, 128)), VMEM),
        kv16_in=(spec((2, CTX, ROWS, 128)), VMEM), q16=(spec((ROWS, HEAD_DIM)), VMEM))


def head_scratch():
    return dict(message=VMEM((2, 4, 2, 160, 128), BF16), qkv_vm=VMEM(TILES, BF16), a_vm=VMEM((512, D), BF16))


def run_head(h, r, gather, after=None):
    arrive = h.sem()
    own16 = dot(r.a_vm[h.rows(h.y, h.s)], r.qkv_vm[:, :, 384:].reshape(D, 256)).astype(BF16)
    r.q16[...] = own16[:, :64]
    r.kv16_in[h.s, h.c] = own16[:, 64:192]
    own_kv = r.kv16_in.at[h.s, h.c]
    leave16, arrive16, cross16 = h.sem(), h.sem(), h.sem()
    for step in range(1, CTX):
        h.send(own_kv, own_kv, (h.s, lax.rem(h.c + step, CTX), h.y), arrive16, leave16)
    for step in ORDER:
        if step:
            gather.relay(step)
        gather.wait(step)
        shard = h.shard(step)
        block = r.a_vm[pl.ds(pl.multiple_of(shard * 128, 128), 128)]
        out = dot(block, r.qkv_vm[:, :, :384].reshape(D, 384)).astype(BF16)
        for e in range(2):
            for core in range(2):
                r.message[e, shard, core, :128] = out[:, 128 + 128 * e : 256 + 128 * e]
                for b in range(2):
                    at = 32 * b + 16 * core
                    lanes = slice(64 * e, 64 * e + 64)
                    packed = jnp.concatenate([out[at : at + 16, lanes], out[64 + at : 80 + at, lanes]], axis=1)
                    r.message[e, shard, core, 128 + 16 * b : 144 + 16 * b] = packed
                chip = 8 * h.s + 4 * e + shard
                h.send_or_keep(
                    r.message.at[e, shard, core], r.message_in.at[h.c], (core, chip, h.y),
                    (chip == h.c) & (h.s == core), arrive)
    h.save(r.a_vm, r.a_full)
    if after is not None:
        after()
    wait_bytes(r.kv16_in.at[h.s, pl.ds(0, CTX - 1)], arrive16)
    cross = r.kv16_in.at[h.s]
    h.send(cross, cross, h.sibling(), cross16)
    wait_bytes(r.kv16_in.at[h.s, pl.ds(0, CTX - 1)], leave16)
    wait_bytes(r.kv16_in.at[1 - h.s], cross16)
    wait_bytes(r.message_in, arrive)


def first_kernel(hidden, norms, side_piece, side_last, w_out, w_down):
    def body(r):
        h = Here(r.sems)
        weights = FirstWeights(h, r)
        weights.load()
        r.down_vm[...] = jnp.zeros_like(r.down_vm)
        h.barrier()
        h.ready()
        weights.send_qkv()
        x = r.hidden[h.s].astype(F32)
        a_value = layer_norm(x, r.norms[0, 0:1], r.norms[0, 2:3]).astype(BF16)
        gather = Gather8(h, r.a_vm)
        for half in range(2):
            gather.start(a_value[half_rows(half)], half)
        weights.send_qkv_on()
        weights.wait_qkv()
        h.save(r.qkv_vm, r.qkv_w)
        run_head(h, r, gather, weights.send_rest)
        weights.finish()
        h.finish()

    ins = dict(hidden=(hidden, VMEM), norms=(norms, VMEM), side_piece=(side_piece, VMEM), side_last=(side_last, VMEM),
        w_out=(w_out, ANY), w_down=(w_down, ANY))
    outs = dict(
        **head_outs(), qkv_w=(spec(TILES), ANY), out_w=(spec((2, 192, D)), ANY), down_w=(spec((2, WINDOW, D)), ANY))
    scratch = dict(
        **head_scratch(), qkv_low=VMEM((4, 4, 2, 16, WINDOW), BF16), qkv_high=VMEM((4, 4, 2, 16, WINDOW), BF16),
        down_rows=VMEM((D, D), BF16), out_rows=VMEM((SLICE, D), BF16), down_vm=VMEM((2, WINDOW, D), BF16),
        out_vm=VMEM((2, 192, D), BF16), sems=pltpu.SemaphoreType.DMA((240,)))
    return call("first", body, ins, outs, scratch, collective_id=1)


def sort_rows(r):
    for m in range(2):
        for p in range(32):
            at = 32 * m + p
            tile = r.places[0, m, p]
            for i in range(2):
                rows = r.kept[tile + i]
                r.keys[32 * at + 16 * i : 32 * at + 16 * i + 16] = rows[:, :64]
                r.values[32 * at + 16 * i : 32 * at + 16 * i + 16] = rows[:, 64:]
            query = r.kept[r.places[1, m, p]]
            r.queries[16 * at : 16 * at + 16] = query[:, 64 * m : 64 * m + 64] * 0.125


def attend(h, r):
    row = lax.broadcasted_iota(jnp.int32, (256, 512), 0)
    row = 32 * (row // 16) + 16 * h.s + row % 16
    visible = row >= lax.broadcasted_iota(jnp.int32, (256, 512), 1)
    for t in range(4):
        query = r.queries[256 * t : 256 * t + 256]
        parts = [dot_nt(query, r.keys[512 * u : 512 * u + 512]) for u in range(t + 1)]
        parts[t] = jnp.where(visible, parts[t], NEG_LARGE)
        top = parts[0]
        for p in parts[1:]:
            top = jnp.maximum(top, p)
        top = jnp.max(top, axis=-1, keepdims=True)
        parts = [jnp.exp(p - top) for p in parts]
        total = parts[0]
        for p in parts[1:]:
            total = total + p
        total = jnp.sum(total, axis=-1, keepdims=True)
        out = dot(parts[0].astype(BF16), r.values[:512])
        for u in range(1, t + 1):
            out = out + dot(parts[u].astype(BF16), r.values[512 * u : 512 * u + 512])
        r.sorted_out[16 * t : 16 * t + 16] = (out / total).astype(BF16).reshape(16, 16, 64)
        r.logs[256 * t : 256 * t + 256] = jnp.broadcast_to(top + jnp.log(total), (256, 128))
    for c in range(CTX):
        for m in range(2):
            for b in range(2):
                rows = r.sorted_out[32 * m + r.order[m, 2 * c + b]]
                r.attended[c, 16 * b : 16 * b + 16, 64 * m : 64 * m + 64] = rows


def attend_last(r):
    kv = r.kept16[...].reshape(SEQ, 128)
    scores = dot_nt(r.kept_q16[...] * 0.125, kv[:, :64])
    scores = jnp.where(r.own_positions[...] >= r.positions[...], scores, NEG_LARGE)
    top = jnp.max(scores, axis=-1, keepdims=True)
    scores = jnp.exp(scores - top)
    total = jnp.sum(scores, axis=-1, keepdims=True)
    out = dot(scores.astype(BF16), kv[:, 64:])
    r.attended16[...] = (out / total).astype(BF16)
    r.logs16[...] = jnp.broadcast_to(top + jnp.log(total), (ROWS, 128))


def attend_ins(kept, at):
    order, places, positions, own_positions = at
    return dict(
        order=(order, pltpu.SMEM), places=(places, pltpu.SMEM), positions=(positions, VMEM),
        own_positions=(own_positions, VMEM), kept=(kept.message_in.reshape(160, 16, 128), VMEM), kept16=(kept.kv16_in, VMEM),
        kept_q16=(kept.q16, VMEM))


def attend_outs():
    return dict(
        attended16=(spec((ROWS, 64)), VMEM), sorted_out=(spec((64, 16, 64)), VMEM), logs=(spec((1024, 128), F32), VMEM),
        logs16=(spec((ROWS, 128), F32), VMEM))


def attend_scratch():
    return dict(
        keys=VMEM((SEQ, 64), BF16), values=VMEM((SEQ, 64), BF16), queries=VMEM((1024, 64), BF16),
        attended=VMEM((CTX, 32, 128), BF16))


def middle_scratch():
    return dict(
        context_in=VMEM((2, 4, 2, 32, 128), BF16), out_vm=VMEM((192, D), BF16), up_vm=VMEM(TILES, BF16),
        down_vm=VMEM((WINDOW, D), BF16), to_out=scatter_scratch(), to_down=scatter_scratch())


def load_layer(h, r, layer, first):
    loads = [h.local(r.out_w.at[layer], r.out_vm), h.local(r.down_w.at[layer], r.down_vm)]
    return loads + load_tiles(h, r.up_all, r.up_last, r.up_vm, first)


def gather_context(h, r):
    arrive = h.sem()
    to_core = h.c // 8
    e, j = lax.rem(h.c // 4, 2), lax.rem(h.c, 4)
    for c in range(CTX):
        h.send_or_keep(
            r.attended.at[c], r.context_in.at[e, j, h.s], (to_core, c, h.y), (h.c == c) & (h.s == to_core), arrive)
    return arrive


def unpack_context(r, store):
    for j in range(4):
        for m in range(2):
            for b in range(2):
                for core in range(2):
                    lanes = slice(64 * m, 64 * m + 64)
                    piece = jnp.concatenate(
                        [r.context_in[e, j, core, 16 * b : 16 * b + 16, lanes] for e in range(2)], axis=1)
                    at = 128 * j + 64 * m + 32 * b + 16 * core
                    store[at : at + 16] = piece


def block_rows(h, step):
    return pl.ds(pl.multiple_of(h.shard(step) * 128, 128), 128)


def run_out(h, r, x, ready):
    sums = Scatter8(h, r.to_out)
    for step in (2, 1, 3, 0):
        sums.put(step, dot(r.context[block_rows(h, step)], r.out_vm[:128]))
    sums.relay((2, 1, 3))
    own = x + dot(r.attended16[...], r.out_vm[128:])
    for half in range(2):
        residual = own[half_rows(half)] + sums.result(half)
        r.residual[half_rows(half)] = residual
        ready(half, residual)


def middle_kernel(at, x, norms, first, mid_all, mid_last):
    def body(r):
        h = Here(r.sems)
        loads = load_layer(h, r, 0, 0)
        head_loads = load_tiles(h, r.up_all, r.up_last, r.qkv_vm, SHARD)
        h.barrier()
        sort_rows(r)
        attend(h, r)
        h.ready()
        arrive = gather_context(h, r)
        attend_last(r)
        for copy in loads:
            copy.wait()
        wait_bytes(r.context_in, arrive)
        unpack_context(r, r.context)
        gather = Gather8(h, r.b_vm)

        def ready(half, residual):
            gather.start(layer_norm(residual, r.norms[0, 1:2], r.norms[0, 3:4]).astype(BF16), half)

        run_out(h, r, r.x[h.s].astype(F32), ready)
        sums = Scatter8(h, r.to_down)
        for step in ORDER:
            if step:
                gather.relay(step)
            gather.wait(step)
            rows = block_rows(h, step)
            u = dot(r.b_vm[rows], whole(r.up_vm))
            r.pre_vm[rows] = u
            sums.put(step, dot(gelu(u).astype(BF16), r.down_vm[...]))
        sums.relay((1, 3, 2))
        h.save(r.b_vm, r.b_full)
        h.save(r.pre_vm, r.pre)
        for copy in head_loads:
            copy.wait()
        gather = Gather8(h, r.a_vm)
        for half in range(2):
            y = (r.residual[half_rows(half)] + sums.result(half)).astype(BF16)
            r.y[half_rows(half)] = y
            gather.start(layer_norm(y.astype(F32), r.norms[1, 0:1], r.norms[1, 2:3]).astype(BF16), half)
        run_head(h, r, gather)
        h.finish()

    ins = dict(
        **attend_ins(first, at), x=(x, VMEM), norms=(norms, VMEM), out_w=(first.out_w, ANY),
        down_w=(first.down_w, ANY), up_all=(mid_all, ANY), up_last=(mid_last, ANY))
    outs = dict(
        **attend_outs(), context=(spec((512, 128)), VMEM), residual=(spec((ROWS, D), F32), VMEM), b_full=(spec((512, D)), ANY),
        pre=(spec((512, WINDOW), F32), ANY), y=(spec((ROWS, D)), VMEM), **head_outs())
    scratch = dict(
        **attend_scratch(), **middle_scratch(), **head_scratch(), b_vm=VMEM((512, D), BF16), pre_vm=VMEM((512, WINDOW), F32),
        sems=pltpu.SemaphoreType.DMA((300,)))
    return call("middle", body, ins, outs, scratch, collective_id=2)


def gelu_slope(u):
    t = jnp.tanh(0.7978845608028654 * (u + 0.044715 * u * u * u))
    return 0.5 * (1.0 + t) + 0.5 * u * (1.0 - t * t) * 0.7978845608028654 * (1.0 + 0.134145 * u * u)


def norm_back(grad, values, gain):
    normed, rate = norm_parts(values)
    scaled = grad * gain
    mean = jnp.mean(scaled, axis=-1, keepdims=True)
    along = jnp.mean(scaled * normed, axis=-1, keepdims=True)
    back = rate * (scaled - mean - normed * along)
    return back, grad * normed


def columns(at, gain_rows, bias_rows):
    lane = lax.broadcasted_iota(jnp.int32, (ROWS, 64), 1)

    def into(rows, column):
        return dot_tn(rows.astype(BF16), (lane == column).astype(BF16))

    return into(gain_rows, at) + into(bias_rows, at + 1)


def back_outs():
    return dict(
        mid_grad=(spec((ROWS, D), F32), VMEM), context_grad_in=(spec((CTX, 32, 128)), VMEM),
        context16_grad=(spec((ROWS, HEAD_DIM)), VMEM),
        up_g_last=(spec((SHARD, 16, WINDOW)), VMEM), norm2_g=(spec((68, 16, 64)), VMEM))


def back_scratch():
    return dict(
        m_full=VMEM((512, D), BF16), z_full=VMEM((512, D), BF16), hidden_low=VMEM((512, WINDOW), BF16),
        pre_grad=VMEM((512, WINDOW), BF16), context_message=VMEM((2, 4, 2, 32, 128), BF16), up_grad=VMEM((4, 4, SHARD, 16, WINDOW), BF16),
        down_grad=VMEM((40, 16, D), BF16), b_vm=VMEM((512, D), BF16), to_norm2=scatter_scratch())


def back_block(h, r, rows, sums, step, u, g):
    r.hidden_low[rows] = g
    hidden_grad = dot_nt(r.m_full[rows], r.down_vm[...])
    pre_grad = (hidden_grad * gelu_slope(u)).astype(BF16)
    r.pre_grad[rows] = pre_grad
    sums.put(step, dot_nt(pre_grad, whole(r.up_vm)))


def finish_back(h, r, sums, layer, residual, out_grad, context, down_ready, up_ready, beside, near_end=None):
    r.down_grad[...] = dot_tn(r.hidden_low[...], r.m_full[...]).astype(BF16).reshape(40, 16, D)
    down_ready(r.down_grad.at[pl.ds(2 * lax.rem(h.y * 2 + h.s, 4), 34)])
    place(dot_tn(r.b_vm[...], r.pre_grad[...]), r.up_grad, r.up_g_last)
    up_ready()
    gather = Gather8(h, r.z_full)
    gain_rows, normed_grad = [], []
    for half in range(2):
        rows = half_rows(half)
        normed_grad.append(sums.result(half))
        back, gains = norm_back(normed_grad[half], residual[rows], r.norms[layer, 1:2])
        gain_rows.append(gains)
        mid_grad = out_grad[rows] + back
        r.mid_grad[rows] = mid_grad
        gather.start(mid_grad.astype(BF16), half)
    gain_rows, normed_grad = jnp.concatenate(gain_rows, axis=0), jnp.concatenate(normed_grad, axis=0)
    z = r.z_full[h.rows(h.y, h.s)]
    r.norm2_g[...] = columns(2, gain_rows, normed_grad).astype(BF16).reshape(68, 16, 64)
    beside()
    arrive = h.sem()
    r.context16_grad[...] = dot_nt(z, r.out_vm[128:]).astype(BF16)
    for step in ORDER:
        if step:
            gather.relay(step)
        gather.wait(step)
        shard = h.shard(step)
        out = dot_nt(r.z_full[block_rows(h, step)], r.out_vm[:128]).astype(BF16)
        for e in range(2):
            for core in range(2):
                lanes = slice(64 * e, 64 * e + 64)
                for b in range(2):
                    at = 32 * b + 16 * core
                    r.context_message[e, shard, core, 16 * b : 16 * b + 16] = jnp.concatenate(
                        [out[at : at + 16, lanes], out[64 + at : 80 + at, lanes]], axis=1)
                chip = 8 * h.s + 4 * e + shard
                h.send_or_keep(
                    r.context_message.at[e, shard, core], r.context_grad_in.at[h.c], (core, chip, h.y),
                    (chip == h.c) & (h.s == core), arrive)
    r.out_g[:8] = dot_tn(context[...], r.z_full[...]).astype(BF16).reshape(8, 16, D)
    r.out_g[8:] = dot_tn(r.attended16[...], z).astype(BF16).reshape(4, 16, D)
    if near_end is not None:
        near_end()
    wait_bytes(r.context_grad_in, arrive)


def turn_kernel(at, kept, x, norms, first, up_all, up_last, cotangent):
    def body(r):
        h = Here(r.sems)
        loads = load_layer(h, r, 1, 0)
        h.barrier()
        sort_rows(r)
        h.ready()
        out_grad = r.cotangent[h.s]
        gather_m = Gather8(h, r.m_full)
        for half in range(2):
            gather_m.start(out_grad[half_rows(half)], half)
        attend(h, r)
        arrive = gather_context(h, r)
        attend_last(r)
        for step in (1, 3, 2):
            gather_m.relay(step)
        for copy in loads:
            copy.wait()
        wait_bytes(r.context_in, arrive)
        unpack_context(r, r.context)
        gather = Gather8(h, r.b_vm)

        def ready(half, residual):
            gather.start(layer_norm(residual, r.norms[1, 1:2], r.norms[1, 3:4]).astype(BF16), half)

        run_out(h, r, r.x[...].astype(F32), ready)
        back_sums, sums = Scatter8(h, r.to_norm2), Scatter8(h, r.to_down)
        for step in ORDER:
            if step:
                gather.relay(step)
            gather_m.wait(step)
            gather.wait(step)
            rows = block_rows(h, step)
            u = dot(r.b_vm[rows], whole(r.up_vm))
            g = gelu(u).astype(BF16)
            back_block(h, r, rows, back_sums, step, u, g)
            sums.put(step, dot(g, r.down_vm[...]))
        back_sums.relay((1, 3, 2))
        sums.relay((1, 3, 2))

        ups = [
            Reduce16(h, r.up_grad.at[:, :, pl.ds(2 * i, 2)], (r.ups_in.at[i], (r.up_mine_a, r.up_mine_b)[i], None), i == 0)
            for i in range(2)]
        first_rows = FirstRows(h, r)

        def up_ready():
            for each in ups:
                each.start()
            first_rows.start()

        def near_end():
            for each in ups:
                each.add()
            first_rows.add()

        def beside():
            for half in range(2):
                rows = half_rows(half)
                r.out[rows] = (r.residual[rows] + sums.result(half)).astype(BF16)

        finish_back(
            h, r, back_sums, 1, r.residual[...], out_grad.astype(F32), r.context, first_rows.load,
            up_ready, beside, near_end)
        h.finish()

    ins = dict(
        **attend_ins(kept, at), x=(x, VMEM), norms=(norms, VMEM), out_w=(first.out_w, ANY),
        down_w=(first.down_w, ANY), up_all=(up_all, ANY), up_last=(up_last, ANY),
        cotangent=(cotangent, VMEM))
    outs = dict(
        **attend_outs(), out=(spec((ROWS, D)), VMEM), **first_rows_outs(),
        up_mine_a=(spec((4, 2, 16, WINDOW)), VMEM), up_mine_b=(spec((4, 2, 16, WINDOW)), VMEM), out_g=(spec((12, 16, D)), VMEM), **back_outs())
    scratch = dict(
        **attend_scratch(), context=VMEM((512, 128), BF16), residual=VMEM((ROWS, D), F32), **middle_scratch(),
        **first_rows_scratch(), ups_in=VMEM((2, 3, 4, 2, 16, WINDOW), BF16), **back_scratch(), sems=pltpu.SemaphoreType.DMA((400,)))
    return call("turn", body, ins, outs, scratch, collective_id=3)


def row_of(grads, outs):
    product = grads.astype(F32) * outs.astype(F32)
    return lax.dot_general(
        jnp.ones((8, 64), F32), product, (((1,), (1,)), ((), ())), precision=lax.Precision.HIGHEST,
        preferred_element_type=F32)[0:1]


def sort_grads(r):
    sort_rows(r)
    for m in range(2):
        for p in range(32):
            at = 32 * m + p
            r.grads[16 * at : 16 * at + 16] = r.grad_in[r.places[2, m, p]][:, 64 * m : 64 * m + 64]
    r.key_grads[...] = jnp.zeros_like(r.key_grads)
    r.value_grads[...] = jnp.zeros_like(r.value_grads)


def attend_back(h, r):
    column = lax.broadcasted_iota(jnp.int32, (512, 256), 1)
    column = 32 * (column // 16) + 16 * h.s + column % 16
    visible = column >= lax.broadcasted_iota(jnp.int32, (512, 256), 0)
    for t in range(4):
        part = slice(256 * t, 256 * t + 256)
        query, grad = r.queries[part], r.grads[part]
        logs = jnp.transpose(r.logs[part])[0:1]
        delta = row_of(grad, r.sorted_out[16 * t : 16 * t + 16].reshape(256, 64))
        query_grad = jnp.zeros((256, 64), F32)
        for u in range(t + 1):
            chunk = slice(512 * u, 512 * u + 512)
            keys = r.keys[chunk]
            scores = dot_nt(keys, query)
            if u == t:
                scores = jnp.where(visible, scores, NEG_LARGE)
            probs = jnp.exp(scores - logs)
            probs_grad = dot_nt(r.values[chunk], grad)
            scores_grad = (probs * (probs_grad - delta)).astype(BF16)
            blocks = slice(16 * u, 16 * u + 16)
            r.value_grads[blocks] += dot(probs.astype(BF16), grad).reshape(16, 32, 64)
            r.key_grads[blocks] += dot(scores_grad, query).reshape(16, 32, 64)
            query_grad = query_grad + dot_tn(scores_grad, keys)
        r.query_grads[16 * t : 16 * t + 16] = (query_grad * 0.125).astype(BF16).reshape(16, 16, 64)
    for c in range(CTX):
        for m in range(2):
            for b in range(2):
                block = 32 * m + r.order[m, 2 * c + b]
                r.message[c, 64 * m + 32 * b : 64 * m + 32 * b + 32, :] = jnp.concatenate(
                    [r.key_grads[block], r.value_grads[block]], axis=1).astype(BF16)
                r.message[c, 128 + 16 * b : 144 + 16 * b, 64 * m : 64 * m + 64] = r.query_grads[block]


def attend_back_last(r):
    kv = r.kept16[...].reshape(SEQ, 128)
    query, grad = r.kept_q16[...] * 0.125, r.grad16[...]
    scores = dot_nt(kv[:, :64], query)
    scores = jnp.where(r.own_positions[...] >= r.positions[...], scores, NEG_LARGE)
    probs = jnp.exp(scores - jnp.transpose(r.logs16[...])[0:1])
    probs_grad = dot_nt(kv[:, 64:], grad)
    scores_grad = (probs * (probs_grad - row_of(grad, r.out16[...]))).astype(BF16)
    both = jnp.concatenate([dot(scores_grad, query), dot(probs.astype(BF16), grad)], axis=1)
    r.kv16_grad[...] = both.astype(BF16).reshape(2, CTX, ROWS, 128)
    r.q16_grad[...] = (dot_tn(scores_grad, kv[:, :64]) * 0.125).astype(BF16)


def tail_ins(at, kept, saved, a_full, x, above, norms):
    return dict(
        **attend_ins(kept, at), sorted_out=(saved.sorted_out, VMEM), logs=(saved.logs, VMEM), logs16=(saved.logs16, VMEM),
        out16=(saved.attended16, VMEM), grad_in=(above.context_grad_in.reshape(32, 16, 128), VMEM), grad16=(above.context16_grad, VMEM),
        a_full=(a_full, ANY), x=(x, VMEM), mid_in=(above.mid_grad, VMEM), norms=(norms, VMEM),
        norm2_in=(above.norm2_g, VMEM))


def tail_outs():
    return dict(in_grad=(spec((ROWS, D)), VMEM))


def tail_scratch():
    return dict(
        keys=VMEM((SEQ, 64), BF16), values=VMEM((SEQ, 64), BF16), queries=VMEM((1024, 64), BF16),
        grads=VMEM((1024, 64), BF16), query_grads=VMEM((64, 16, 64), BF16), key_grads=VMEM((64, 32, 64), F32),
        value_grads=VMEM((64, 32, 64), F32), message=VMEM((CTX, 160, 128), BF16),
        kv16_grad=VMEM((2, CTX, ROWS, 128), BF16), q16_grad=VMEM((ROWS, 64), BF16),
        message_in=VMEM((2, 4, 2, 160, 128), BF16), core16=VMEM((CTX, ROWS, 128), BF16),
        sum16=VMEM((CTX, ROWS, 128), BF16), own16=VMEM((CTX, ROWS, 128), BF16), qkv_grads=VMEM((512, 384), BF16),
        qkv_vm=VMEM(TILES, BF16), a_vm=VMEM((512, D), BF16), main_part=VMEM((4, 4, SHARD, 16, 384), BF16),
        side_part=VMEM((4, 4, SHARD, 16, 256), BF16), to_norm1=scatter_scratch())


def start_tail(h, r):
    attend_back_last(r)
    cross = h.sem()
    h.send(r.kv16_grad.at[1 - h.s], r.core16, h.sibling(), cross)
    attend_back(h, r)
    arrive = h.sem()
    to_core = h.c // 8
    e, j = lax.rem(h.c // 4, 2), lax.rem(h.c, 4)
    for c in range(CTX):
        h.send_or_keep(
            r.message.at[c], r.message_in.at[e, j, h.s], (to_core, c, h.y), (h.c == c) & (h.s == to_core), arrive)
    wait_bytes(r.core16, cross)
    r.sum16[...] = (r.kv16_grad[h.s].astype(F32) + r.core16[...].astype(F32)).astype(BF16)
    leave16, arrive16 = h.sem(), h.sem()
    for step in range(1, CTX):
        to = lax.rem(h.c + step, CTX)
        h.send(r.sum16.at[to], r.own16.at[step], (h.s, to, h.y), arrive16, leave16)
    return arrive, leave16, arrive16


def run_tail(h, r, layer, x, waits, loads, last, main_ready, side_ready, arrived, beside, in_ready):
    arrive, leave16, arrive16 = waits
    for copy in loads:
        copy.wait()
    weights = whole(r.qkv_vm)
    wait_bytes(r.message_in, arrive)
    arrived()
    for j in range(4):
        for e in range(2):
            both = r.message_in[e, j, 0, :128].astype(F32) + r.message_in[e, j, 1, :128].astype(F32)
            r.qkv_grads[128 * j : 128 * j + 128, 128 + 128 * e : 256 + 128 * e] = both.astype(BF16)
        for m in range(2):
            for b in range(2):
                for core in range(2):
                    lanes = slice(64 * m, 64 * m + 64)
                    piece = jnp.concatenate(
                        [r.message_in[e, j, core, 128 + 16 * b : 144 + 16 * b, lanes] for e in range(2)], axis=1)
                    at = 128 * j + 64 * m + 32 * b + 16 * core
                    r.qkv_grads[at : at + 16, :128] = piece
    sums = Scatter8(h, r.to_norm1)
    for step in (2, 1, 3, 0):
        sums.put(step, dot_nt(r.qkv_grads[block_rows(h, step)], weights[:, :384]))
    sums.relay((2, 1, 3))
    wait_bytes(r.own16.at[pl.ds(1, CTX - 1)], arrive16)
    wait_bytes(r.own16.at[pl.ds(1, CTX - 1)], leave16)
    kv16 = r.sum16[h.c].astype(F32)
    for step in range(1, CTX):
        kv16 = kv16 + r.own16[step].astype(F32)
    grads16 = jnp.concatenate([r.q16_grad[...], kv16.astype(BF16)], axis=1)
    own = dot_nt(grads16, weights[:, 384:576])
    place(dot_tn(r.a_vm[...], r.qkv_grads[...]), r.main_part, last.at[:, :, pl.ds(0, 384)])
    main_ready()
    own_grad = dot_tn(r.a_vm[h.rows(h.y, h.s)], grads16)
    beside()
    gain_rows, normed_grad = [], []
    for half in range(2):
        rows = half_rows(half)
        normed_grad.append(own[rows] + sums.result(half))
        back, gains = norm_back(normed_grad[half], x[rows], r.norms[layer, 0:1])
        gain_rows.append(gains)
        in_grad = (r.mid_in[rows] + back).astype(BF16)
        r.in_grad[rows] = in_grad
        in_ready(half, in_grad)
    gain_rows, normed_grad = jnp.concatenate(gain_rows, axis=0), jnp.concatenate(normed_grad, axis=0)

    def finish():
        sums_of_rows = columns(0, gain_rows, normed_grad) + r.norm2_in[...].reshape(D, 64).astype(F32)
        side = jnp.concatenate([own_grad, sums_of_rows], axis=1)
        place(side, r.side_part, last.at[:, :, pl.ds(384, 256)])
        side_ready()

    return finish


def send_out(h, r, out, layer, arrive, arrive_last):
    group = 2 * h.y + h.s
    for i in range(8):
        tile = 8 * group + i
        to = tile // 17
        h.send_or_keep(
            out.at[i], r.out_sum.at[lax.rem(tile, 17)], (layer, h.c, to), (h.s == layer) & (to == h.y), arrive)
    h.send_or_keep(
        out.at[pl.ds(8, 4)], r.last_in.at[group], (layer, h.c, SHARD - 1), (h.s == layer) & (h.y == SHARD - 1),
        arrive_last)


def back_kernel(at, kept, saved, x, above, norms, first, attended16, mid_all, mid_last):
    def body(r):
        h = Here(r.sems)
        tail_loads = load_tiles(h, r.up_all, r.up_last, r.qkv_vm, SHARD)
        tail_loads.append(h.local(r.a_full, r.a_vm))
        loads = load_layer(h, r, 0, 0)
        loads += [h.local(r.b_full, r.b_vm), h.local(r.pre, r.pre_vm), h.local(r.context, r.context_vm)]
        h.barrier()
        sort_grads(r)
        arrive_out, arrive_last = h.sem(), h.sem()
        x, z = h.c // 4, lax.rem(h.c, 4)
        ups = [
            Reduce16(h, None, (None, (r.up_mine_a, r.up_mine_b)[i], r.ups_second.at[i]), i == 0) for i in range(2)]
        main = Reduce16(h, r.main_part, r.main_sums, False)
        side = Reduce16(h, r.side_part, r.side_sums, True)
        up0 = Reduce16(h, r.up_grad, (r.up0_in, r.up0_mine, None), True)
        rows16 = Rows16(h, r, 1)
        first_rows = FirstRows(h, r)
        h.ready()
        for each in ups:
            each.send_on()
        rows16.start()
        send_out(h, r, r.out1_g, 1, arrive_out, arrive_last)
        waits = start_tail(h, r)

        def settle(core):
            @pl.when(h.s == core)
            def _():
                @pl.when(h.y < SHARD - 1)
                def _():
                    wait_bytes(r.out_sum, arrive_out)

                @pl.when(h.y == SHARD - 1)
                def _():
                    wait_bytes(r.out_sum.at[pl.ds(0, 13)], arrive_out)
                    wait_bytes(r.last_in, arrive_last)
                    r.out_sum[13:] = added([r.last_in[g] for g in range(8)])

        arrive_up = h.sem()
        spreads = [Spread16(h, parts, i == 0, 1) for i, parts in enumerate((r.up_low, r.up_high))]

        def arrived():
            for i in range(2):
                r.up1_piece[2 * i : 2 * i + 2] = ups[i].result()
            send_piece(h, r.up1_piece, r.up_in, 1, arrive_up)
            settle(1)
            rows16.start_out()

        def beside_sums():
            rows16.middle()

            @pl.when(h.s == 1)
            def _():
                wait_bytes(r.up_in, arrive_up)
                rows = joined_up([r.up_in[g] for g in range(8)])
                for i, parts in enumerate((r.up_low, r.up_high)):
                    parts[x, z] = rows[:, 2176 * i : 2176 * i + 2176]

            for each in spreads:
                each.start()

        gather = Gather8(h, r.m_full)
        finish = run_tail(
            h, r, 1, r.x[...].astype(F32), waits, tail_loads, r.qkv_g_last, main.start, side.start,
            arrived, beside_sums, lambda half, value: gather.start(value, half))
        finish()
        rows16.spread()
        for copy in loads:
            copy.wait()
        sums = Scatter8(h, r.to_norm2)
        for step in ORDER:
            if step:
                gather.relay(step)
            gather.wait(step)
            rows = block_rows(h, step)
            u = r.pre_vm[rows]
            back_block(h, r, rows, sums, step, u, gelu(u).astype(BF16))
            if step == 0:
                for each in spreads:
                    each.middle()
            if step == 1:
                rows16.spread_on()
        sums.relay((1, 3, 2))
        def down_ready(rows):
            first_rows.load(rows)
            main.middle()
            side.middle()

        def up_ready():
            up0.start()
            first_rows.start()

        def beside():
            r.qkv1_piece[:, :, :384] = main.result()
            r.qkv1_piece[:, :, 384:] = side.result()

        def near_end():
            send_out(h, r, r.out_g, 0, arrive_out, arrive_last)
            up0.add()
            first_rows.add()
            for each in spreads:
                each.finish()
            h.save_on(1, r.up_low, r.up_low_all)
            h.save_on(1, r.up_high, r.up_high_all)

        finish_back(
            h, r, sums, 0, r.residual[...], r.in_grad[...].astype(F32), r.context_vm, down_ready, up_ready, beside, near_end)
        rows16.finish()

        settle(0)
        h.finish()

    ins = dict(
        **tail_ins(at, kept, saved, kept.a_full, x, above, norms), pre=(kept.pre, ANY), b_full=(kept.b_full, ANY),
        context=(kept.context, ANY), residual=(kept.residual, VMEM), attended16=(attended16, VMEM),
        out_w=(first.out_w, ANY), down_w=(first.down_w, ANY), up_all=(mid_all, ANY), up_last=(mid_last, ANY),
        up_mine_a=(above.up_mine_a, VMEM), up_mine_b=(above.up_mine_b, VMEM), out1_g=(above.out_g, VMEM),
        mine_a=(above.next_a, VMEM), mine_b=(above.next_b, VMEM), mine_beside=(above.next_beside, VMEM))
    piece, half = (spec((SHARD, 16, WINDOW)), VMEM), (spec((4, 4, 16, 2176)), ANY)
    outs = dict(
        **tail_outs(), **back_outs(), qkv_g_last=piece, qkv1_piece=piece, up0_mine=(spec((4, SHARD, 16, WINDOW)), VMEM),
        up_low_all=half, up_high_all=half, **rows_outs(), **rows_results(),
        **first_rows_outs(), out_sum=(spec((17, 16, D)), VMEM))
    scratch = dict(
        out_vm=VMEM((192, D), BF16), up_vm=VMEM(TILES, BF16), down_vm=VMEM((WINDOW, D), BF16),
        pre_vm=VMEM((512, WINDOW), F32), context_vm=VMEM((512, 128), BF16), out_g=VMEM((12, 16, D), BF16),
        ups_second=VMEM((2, 3, 2, 16, WINDOW), BF16), **first_rows_scratch(),
        up0_in=VMEM((3, 4, SHARD, 16, WINDOW), BF16), up_low=VMEM((4, 4, 16, 2176), BF16),
        up_high=VMEM((4, 4, 16, 2176), BF16), main_sums=reduce_scratch(SHARD, 384), side_sums=reduce_scratch(SHARD, 256),
        up1_piece=VMEM((SHARD, 16, WINDOW), BF16), up_in=VMEM((8, 16, WINDOW), BF16), last_in=VMEM((8, 4, 16, D), BF16), **tail_scratch(), **back_scratch(),
        **rows_scratch(), sems=pltpu.SemaphoreType.DMA((520,)))
    return call("back", body, ins, outs, scratch, collective_id=4)


class Plane16:
    def __init__(self, h, x_first, core=None):
        self.h, self.x_first = h, x_first
        self.on = None if core is None else h.s == core
        self.x, self.z = h.c // 4, lax.rem(h.c, 4)
        self.first = [h.sem() for _ in range(3)]
        self.second = [h.sem() for _ in range(3)]

    def when(self, act):
        act() if self.on is None else pl.when(self.on)(act)

    def chip(self, x, z):
        return (self.h.s, 4 * lax.rem(x, 4) + lax.rem(z, 4), self.h.y)

    def along(self, axis_x):
        return [self.chip(self.x + j, self.z) if axis_x else self.chip(self.x, self.z + j) for j in (1, 2, 3)]

    def send(self, pairs, targets, sems):
        copies = [
            pltpu.make_async_remote_copy(
                src_ref=src, dst_ref=dst, send_sem=self.h.sem(), recv_sem=sem, device_id=to, device_id_type=MESH)
            for (src, dst), to, sem in zip(pairs, targets, sems)]

        def start():
            for i in (0, 2, 1):
                copies[i].start()

        def wait_send():
            for copy in copies:
                copy.wait_send()

        self.when(start)
        self.h.sent.append(types.SimpleNamespace(wait_send=lambda: self.when(wait_send)))


class Reduce16(Plane16):
    def __init__(self, h, part, bufs, x_first, core=None):
        super().__init__(h, x_first, core)
        self.part = part
        self.first_in, self.mine, self.second_in = bufs

    def start(self):
        pairs = []
        for j in (1, 2, 3):
            src = self.part.at[lax.rem(self.x + j, 4)] if self.x_first else self.part.at[:, lax.rem(self.z + j, 4)]
            pairs.append((src, self.first_in.at[j - 1]))
        self.send(pairs, self.along(self.x_first), self.first)

    def add(self):
        def add():
            for j in range(3):
                wait_bytes(self.first_in.at[j], self.first[j])
            for k in range(4):
                own = self.part[self.x, k] if self.x_first else self.part[k, self.z]
                self.mine[k] = added([own] + [self.first_in[j, k] for j in range(3)])

        self.when(add)

    def send_on(self):
        at = self.z if self.x_first else self.x
        pairs = [(self.mine.at[lax.rem(at + j, 4)], self.second_in.at[j - 1]) for j in (1, 2, 3)]
        self.send(pairs, self.along(not self.x_first), self.second)

    def middle(self):
        self.add()
        self.send_on()

    def result(self):
        for j in range(3):
            wait_bytes(self.second_in.at[j], self.second[j])
        return added([self.mine[self.z if self.x_first else self.x]] + [self.second_in[j] for j in range(3)])


def reduce_scratch(units, width):
    return [VMEM((3, 4, units, 16, width), BF16), VMEM((4, units, 16, width), BF16), VMEM((3, units, 16, width), BF16)]


class Spread16(Plane16):
    def __init__(self, h, parts, x_first, core=None):
        super().__init__(h, x_first, core)
        self.parts = parts

    def start(self):
        own = self.parts.at[self.x, self.z]
        self.send([(own, own)] * 3, self.along(self.x_first), self.first)

    def middle(self):
        def wait():
            for sem in self.first:
                wait_bytes(self.parts.at[0, 0], sem)

        self.when(wait)
        line = self.parts.at[:, self.z] if self.x_first else self.parts.at[self.x]
        self.send([(line, line)] * 3, self.along(not self.x_first), self.second)

    def finish(self):
        def wait():
            for sem in self.second:
                wait_bytes(self.parts.at[0], sem)

        self.when(wait)


class FirstRows:
    def __init__(self, h, r):
        self.h, self.r = h, r
        self.sums = [
            Reduce16(h, r.rows_a, (r.rows_in.at[0], r.next_a, None), True),
            Reduce16(h, r.rows_b, (r.rows_in.at[1], r.next_b, None), False)]

    def load(self, down):
        h, r = self.h, self.r
        self.loads = [h.local(down.at[pl.ds(32, 2)], r.next_beside)]
        for x in range(4):
            for i, parts in enumerate((r.rows_a, r.rows_b)):
                self.loads += [h.local(down.at[8 * x + 2 * z + i], parts.at[x, z, 0]) for z in range(4)]

    def start(self):
        for copy in self.loads:
            copy.wait()
        for each in self.sums:
            each.start()

    def add(self):
        for each in self.sums:
            each.add()


def first_rows_outs():
    mine = (spec((4, 1, 16, D)), VMEM)
    return dict(next_a=mine, next_b=mine, next_beside=(spec((2, 16, D)), VMEM))


def first_rows_scratch():
    part = VMEM((4, 4, 1, 16, D), BF16)
    return dict(rows_a=part, rows_b=part, rows_in=VMEM((2, 3, 4, 1, 16, D), BF16))


class Rows16:
    def __init__(self, h, r, core):
        self.h, self.r, self.core = h, r, core
        self.sums = [
            Reduce16(h, None, (None, r.mine_a, r.rows_second.at[0]), True),
            Reduce16(h, None, (None, r.mine_b, r.rows_second.at[1]), False),
            Reduce16(h, r.rows_c, r.rows_sums_c, True, core)]
        self.spreads = [
            Spread16(h, r.rows_all.at[0], True), Spread16(h, r.rows_all.at[1], False), Spread16(h, r.rows_out, False, core)]
        self.arrive = h.sem()
        self.arrive_each = [h.sem() for _ in range(3)]
        self.cross = [h.sem() for _ in range(2)]

    def on(self, i):
        return self.h.s == self.core if i == 2 else None

    def when(self, i, act, also=None):
        conditions = [c for c in (self.on(i), also) if c is not None]
        if not conditions:
            return act()
        return pl.when(functools.reduce(jnp.logical_and, conditions))(act)

    def start(self):
        for i in range(2):
            self.sums[i].send_on()
            self.send_tile(self.r.mine_beside.at[i], i)

    def start_out(self):
        h, r = self.h, self.r

        @pl.when(h.s == self.core)
        def _():
            for c in range(CTX):
                r.rows_c[c // 4, c % 4, 0] = r.out_sum[c]

        self.sums[2].start()
        self.send_tile(r.out_sum.at[16], 2)

    def send_tile(self, src, i):
        h = self.h
        dst, leave = self.r.tile_in.at[h.c], h.sem()
        copy = pltpu.make_async_remote_copy(
            src_ref=src, dst_ref=dst, send_sem=leave, recv_sem=self.arrive, device_id=(h.s, 5 * i, h.y),
            device_id_type=MESH)
        kept = pltpu.make_async_copy(src, dst, self.arrive)
        self.when(i, copy.start, h.c != 5 * i)
        self.when(i, kept.start, h.c == 5 * i)
        h.sent.append(types.SimpleNamespace(
            wait_send=functools.partial(self.when, i, copy.wait_send, h.c != 5 * i)))

    def middle(self):
        self.sums[2].middle()

    def spread(self):
        h, r = self.h, self.r
        x, z = h.c // 4, lax.rem(h.c, 4)
        r.rows_all[0, x, z] = self.sums[0].result()
        r.rows_all[1, x, z] = self.sums[1].result()

        def out():
            r.rows_out[x, z] = self.sums[2].result()

        self.when(2, out)
        for each in self.spreads:
            each.start()
        for i in range(3):
            copies = [
                pltpu.make_async_remote_copy(
                    src_ref=r.tiles.at[i], dst_ref=r.tiles.at[i], send_sem=h.sem(), recv_sem=self.arrive_each[i],
                    device_id=(h.s, lax.rem(h.c + step, CTX), h.y), device_id_type=MESH)
                for step in range(1, CTX)]

            def start(i=i, copies=copies):
                wait_bytes(r.tile_in, self.arrive)
                r.tiles[i] = added([r.tile_in[c] for c in range(CTX)])
                for copy in copies:
                    copy.start()

            def wait_send(copies=copies):
                for copy in copies:
                    copy.wait_send()

            self.when(i, start, h.c == 5 * i)
            h.sent.append(types.SimpleNamespace(
                wait_send=functools.partial(self.when, i, wait_send, h.c == 5 * i)))

    def spread_on(self):
        for each in self.spreads:
            each.middle()

    def finish(self):
        h, r = self.h, self.r
        for each in self.spreads:
            each.finish()
        for i in range(3):
            self.when(i, functools.partial(wait_bytes, r.tiles.at[i], self.arrive_each[i]), h.c != 5 * i)
        copies = [
            pltpu.make_async_remote_copy(
                src_ref=src, dst_ref=dst, send_sem=h.sem(), recv_sem=sem, device_id=h.sibling(), device_id_type=MESH)
            for src, dst, sem in (
                (r.rows_all, r.rows_other, self.cross[0]),
                (r.tiles.at[pl.ds(0, 2)], r.tiles_other, self.cross[1]))]

        @pl.when(h.s != self.core)
        def _():
            for copy in copies:
                copy.start()

        h.save_on(self.core, r.rows_all, r.rows_own)
        h.save_on(self.core, r.rows_out, r.rows_out_all)

        @pl.when(h.s != self.core)
        def _():
            for copy in copies:
                copy.wait_send()

        @pl.when(h.s == self.core)
        def _():
            wait_bytes(r.rows_other, self.cross[0])
            wait_bytes(r.tiles_other, self.cross[1])

        h.save_on(self.core, r.rows_other, r.rows_cross)


def rows_outs():
    return dict(tiles=(spec((3, 16, D)), VMEM), tiles_other=(spec((2, 16, D)), VMEM))


def rows_scratch():
    part = VMEM((4, 4, 1, 16, D), BF16)
    return dict(
        rows_c=part, rows_sums_c=reduce_scratch(1, D), rows_second=VMEM((2, 3, 1, 16, D), BF16),
        tile_in=VMEM((CTX, 16, D), BF16), rows_all=VMEM((2, 4, 4, 1, 16, D), BF16), rows_out=part,
        rows_other=VMEM((2, 4, 4, 1, 16, D), BF16))


def rows_results():
    whole_rows = (spec((2, 4, 4, 1, 16, D)), ANY)
    return dict(rows_own=whole_rows, rows_cross=whole_rows, rows_out_all=(spec((4, 4, 1, 16, D)), ANY))


def send_piece(h, piece, dst, layer, arrive):
    for step in (1, 3, 2, 0):
        shard = h.shard(step)
        h.send_or_keep(
            piece.at[shard], dst.at[2 * h.y + h.s], (layer, h.c, shard), (h.s == layer) & (step == 0), arrive)


def joined_up(windows):
    parts = []
    for g in range(8):
        main = windows[g][:, :512]
        if g % 4:
            main = jnp.concatenate([main[:, :128] + windows[g - 1][:, 512:], main[:, 128:]], axis=1)
        parts.append(main)
        if g % 4 == 3:
            parts.append(windows[g][:, 512:])
    return jnp.concatenate(parts, axis=1)


def joined_qkv(blocks, own):
    queries = [blocks[g][:, :128] for g in range(8)] + [own[:, :64]]
    keys = [blocks[g][:, a : a + 64] for g in range(8) for a in (128, 256)] + [own[:, 64:128]]
    values = [blocks[g][:, a : a + 64] for g in range(8) for a in (192, 320)] + [own[:, 128:192]]
    return jnp.concatenate(queries + keys + values + [own[:, 192:]], axis=1)


def added(blocks):
    total = blocks[0].astype(F32)
    for block in blocks[1:]:
        total = total + block.astype(F32)
    return total.astype(BF16)


def last_kernel(at, kept, saved, hidden, above, turn_up_last, norms):
    def body(r):
        h = Here(r.sems)
        x, z = h.c // 4, lax.rem(h.c, 4)
        group = 2 * h.y + h.s
        loads = [h.local(r.qkv_w, r.qkv_vm), h.local(r.a_full, r.a_vm)]
        h.barrier()
        sort_grads(r)
        h.ready()
        up0 = Reduce16(h, None, (None, r.up0_mine, r.up0_in), True)
        up0.send_on()
        main = Reduce16(h, r.main_part, r.main_sums, True)
        side = Reduce16(h, r.side_part, r.side_sums, False)
        arrive_wide = h.sem()
        send_piece(h, r.qkv1_piece, r.wide_in, 1, arrive_wide)
        rows16 = Rows16(h, r, 0)
        rows16.start()
        rows16.start_out()
        arrive_last, arrive_late = h.sem(), h.sem()
        for i in range(SHARD):
            chip = 4 * i + h.y
            r.last_message[i, 0] = r.up_last[i]
            r.last_message[i, 1] = r.up1_last[i]
            r.last_message[i, 2] = r.qkv1_last[i]
            h.send_or_keep(r.last_message.at[i], r.last_in.at[h.c], (h.s, chip, h.y), chip == h.c, arrive_last)
        waits = start_tail(h, r)
        wide = [Spread16(h, parts, i == 0) for i, parts in enumerate((r.wide_low, r.wide_high))]

        def spread_wide():
            wait_bytes(r.wide_in, arrive_wide)
            blocks = [r.wide_in[g] for g in range(8)]

            @pl.when(h.s == 0)
            def _():
                rows = joined_up(blocks)
                r.wide_low[x, z] = rows[:, :2176]
                r.wide_high[x, z] = rows[:, 2176:]

            @pl.when(h.s == 1)
            def _():
                rows = joined_qkv(blocks, added([block[:, 384:] for block in blocks]))
                r.wide_low[x, z] = rows[:, :2176]
                r.wide_high[x, z] = jnp.concatenate([rows[:, 2176:], jnp.zeros((16, 1024), BF16)], axis=1)

            for each in wide:
                each.start()

        def arrived():
            rows16.middle()
            r.up0_piece[...] = up0.result()
            send_piece(h, r.up0_piece, r.wide_in, 0, arrive_wide)

        def beside():
            rows16.spread()
            spread_wide()

        finish = run_tail(
            h, r, 0, r.x[h.s].astype(F32), waits, loads, r.qkv_last, main.start, side.start, arrived, beside,
            lambda half, value: None)
        finish()
        for i in range(SHARD):
            chip = 4 * i + h.y
            h.send_or_keep(r.qkv_last.at[i], r.late_in.at[h.c], (h.s, chip, h.y), chip == h.c, arrive_late)
        main.middle()
        side.middle()
        for each in wide:
            each.middle()
        rows16.spread_on()
        arrive_rest = h.sem()
        reduces = z == h.y

        @pl.when(reduces)
        def _():
            wait_bytes(r.last_in, arrive_last)
            wait_bytes(r.late_in, arrive_late)
            early = added([r.last_in[c] for c in range(CTX)])
            r.rest_message[0, 0] = early[0]
            r.rest_message[0, 1] = added([r.late_in[c] for c in range(CTX)])
            r.rest_message[1] = early[1:]

        rest = []
        for layer in range(2):
            leave = h.sem()
            src, dst = r.rest_message.at[layer], r.rest.at[z, h.s]
            copy = pltpu.make_async_remote_copy(
                src_ref=src, dst_ref=dst, send_sem=leave, recv_sem=arrive_rest, device_id=(layer, h.c, x),
                device_id_type=MESH)
            kept = pltpu.make_async_copy(src, dst, arrive_rest)
            is_self = (h.s == layer) & (x == h.y)
            pl.when(reduces & is_self)(kept.start)
            away = reduces & jnp.logical_not(is_self)
            pl.when(away)(copy.start)
            rest.append((away, copy))
        r.qkv_piece[:, :, :384] = main.result()
        r.qkv_piece[:, :, 384:] = side.result()
        arrive_qkv = h.sem()
        send_piece(h, r.qkv_piece, r.qkv_in, 0, arrive_qkv)
        owner = x == h.y
        across = [h.sem() for _ in range(4)]
        along = [h.sem() for _ in range(3)]
        line = r.rest.at[z]
        lines = []
        for j in range(1, 4):
            lines.append(pltpu.make_async_remote_copy(
                src_ref=line, dst_ref=line, send_sem=across[j], recv_sem=across[0],
                device_id=(h.s, 4 * lax.rem(x + j, 4) + z, h.y), device_id_type=MESH))

        @pl.when(owner)
        def _():
            wait_bytes(line, arrive_rest)
            for copy in lines:
                copy.start()

        spreads = [Spread16(h, parts, i == 0, 0) for i, parts in enumerate((r.qkv_low, r.qkv_high))]

        @pl.when(h.s == 0)
        def _():
            wait_bytes(r.qkv_in, arrive_qkv)
            blocks = [r.qkv_in[g] for g in range(8)]
            rows = joined_qkv(blocks, added([block[:, 384:] for block in blocks]))
            r.qkv_low[x, z] = rows[:, :1664]
            r.qkv_high[x, z] = rows[:, 1664:]

        for each in spreads:
            each.start()
        for each in wide:
            each.finish()
        h.save(r.wide_low, r.wide_low_all)
        h.save(r.wide_high, r.wide_high_all)

        @pl.when(jnp.logical_not(owner))
        def _():
            wait_bytes(line, across[0])

        for j in range(1, 4):
            h.send(line, line, (h.s, 4 * x + lax.rem(z + j, 4), h.y), along[j - 1])
        for each in spreads:
            each.middle()
        rows16.finish()
        for sem in along:
            wait_bytes(line, sem)
        r.up_rest[...] = joined_up([r.rest[g // 2, g % 2, 0] for g in range(8)])
        blocks = [r.rest[g // 2, g % 2, 1] for g in range(8)]
        r.qkv_rest[...] = joined_qkv(blocks, added([block[:, 384:] for block in blocks]))
        for each in spreads:
            each.finish()
        h.save_on(0, r.qkv_low, r.qkv_low_all)
        h.save_on(0, r.qkv_high, r.qkv_high_all)

        @pl.when(owner)
        def _():
            for copy in lines:
                copy.wait_send()

        for away, copy in rest:
            pl.when(away)(copy.wait_send)
        h.finish()

    ins = dict(
        **tail_ins(at, kept, saved, kept.a_full, hidden, above, norms), qkv_w=(kept.qkv_w, ANY), up0_mine=(above.up0_mine, VMEM),
        qkv1_piece=(above.qkv1_piece, VMEM), up_last=(above.up_g_last, VMEM), qkv1_last=(above.qkv_g_last, VMEM),
        up1_last=(turn_up_last, VMEM), mine_a=(above.next_a, VMEM), mine_b=(above.next_b, VMEM), mine_beside=(above.next_beside, VMEM),
        out_sum=(above.out_sum, VMEM))
    up_half, qkv_half = (spec((4, 4, 16, 2176)), ANY), (spec((4, 4, 16, 1664)), ANY)
    outs = dict(
        **tail_outs(), wide_low_all=up_half, wide_high_all=up_half, qkv_low_all=qkv_half, qkv_high_all=qkv_half,
        up_rest=(spec((16, FF)), VMEM), qkv_rest=(spec((16, 3328)), VMEM), **rows_outs(), **rows_results())
    piece, eight = VMEM((SHARD, 16, WINDOW), BF16), VMEM((8, 16, WINDOW), BF16)
    scratch = dict(
        **tail_scratch(),
        main_sums=reduce_scratch(SHARD, 384), side_sums=reduce_scratch(SHARD, 256), **rows_scratch(), wide_low=VMEM((4, 4, 16, 2176), BF16), wide_high=VMEM((4, 4, 16, 2176), BF16),
        qkv_low=VMEM((4, 4, 16, 1664), BF16), qkv_high=VMEM((4, 4, 16, 1664), BF16), qkv_piece=piece, qkv_last=piece, last_message=VMEM((SHARD, 3, 16, WINDOW), BF16),
        last_in=VMEM((CTX, 3, 16, WINDOW), BF16), late_in=VMEM((CTX, 16, WINDOW), BF16), wide_in=eight, qkv_in=eight, up0_piece=piece,
        up0_in=VMEM((3, SHARD, 16, WINDOW), BF16),
        rest_message=VMEM((2, 2, 16, WINDOW), BF16), rest=VMEM((4, 2, 2, 16, WINDOW), BF16),
        sems=pltpu.SemaphoreType.DMA((440,)))
    return call("last", body, ins, outs, scratch, collective_id=5)


def join_kernel(back, last):
    def body(
        _, up_low, up_high, wide_low, wide_high, qkv_low, qkv_high, own0, cross0, out0, own1, cross1, out1, up_rest, qkv_rest,
        tiles0, tiles_other0, tiles1, tiles_other1, up_ref, qkv_ref, norm_ref, down_ref, out_ref):
        def store(rows, up_parts, qkv_parts):
            for at, block in up_parts:
                up_ref[:rows, at : at + block.shape[1]] = block.astype(F32)
            for at, block in qkv_parts:
                block = block.astype(F32)
                if at + block.shape[1] == 3328:
                    norm_ref[:rows] = block[:, -128:]
                    block = block[:, :-64]
                qkv_ref[:rows, at : at + block.shape[1]] = block

        def rows_from(halves, out, tiles):
            @pl.when(pl.program_id(0) < 4)
            def _():
                for c in range(4):
                    for i in range(2):
                        for half in range(2):
                            at = 32 * c + 16 * i
                            down_ref[half, at : at + 16] = halves[half][i, 0, c, 0].astype(F32)
                    out_ref[16 * c : 16 * c + 16] = out[0, c, 0].astype(F32)

            @pl.when(pl.program_id(0) == 4)
            def _():
                for half in range(2):
                    down_ref[half, :32] = tiles[half][:2].reshape(32, D).astype(F32)
                out_ref[:16] = tiles[2].astype(F32)

        first = lax.axis_index(SECTION) == 0
        pl.when(first)(lambda: rows_from((own0, cross0), out0, (tiles0, tiles_other0, tiles0[2])))
        pl.when(jnp.logical_not(first))(
            lambda: rows_from((cross1, own1), out1, (tiles_other1, tiles1, tiles1[2])))
        low, high = (ref[0].reshape(64, 2176) for ref in (wide_low, wide_high))

        @pl.when((pl.program_id(0) < 4) & first)
        def _():
            parts = [ref[0].reshape(64, 1664) for ref in (qkv_low, qkv_high)]
            store(64, ((0, low), (2176, high)), ((0, parts[0]), (1664, parts[1])))

        @pl.when((pl.program_id(0) < 4) & jnp.logical_not(first))
        def _():
            parts = [ref[0].reshape(64, 2176) for ref in (up_low, up_high)]
            store(64, ((0, parts[0]), (2176, parts[1])), ((0, low), (2176, high[:, :1152])))

        @pl.when(pl.program_id(0) == 4)
        def _():
            store(16, ((0, up_rest[...]),), ((0, qkv_rest[...]),))

    def place(i, section, core):
        return jnp.where((core < 0) | (section[0] == core), jnp.minimum(i, 3), 0)

    def line(width, core):
        return pl.BlockSpec((1, 4, 16, width), lambda i, section: (place(i, section, core), 0, 0, 0))

    def tile_line(core, *lead):
        zeros = (0,) * len(lead)
        return pl.BlockSpec(
            (*lead, 1, 4, 1, 16, D), lambda i, section: (*zeros, place(i, section, core), 0, 0, 0, 0))

    def tiles_of(count):
        return pl.BlockSpec((count, 16, D), lambda i, section: (0, 0, 0))

    def rows(width, count=64):
        return pl.BlockSpec((count, width), lambda i, section: (i, 0))

    def all_of(width):
        return pl.BlockSpec((16, width), lambda i, section: (0, 0))

    return pl.pallas_call(
        body,
        out_shape=(
            spec((SLICE, FF), F32), spec((SLICE, 3 * D), F32), spec((SLICE, 128), F32), spec((2, 544, D), F32),
            spec((SLICE, D), F32)),
        grid_spec=pltpu.PrefetchScalarGridSpec(
            num_scalar_prefetch=1,
            grid=(5,),
            in_specs=[
                line(2176, 1), line(2176, 1), line(2176, -1), line(2176, -1), line(1664, 0), line(1664, 0),
                tile_line(0, 2), tile_line(0, 2), tile_line(0), tile_line(1, 2), tile_line(1, 2), tile_line(1),
                all_of(FF), all_of(3328), *[tiles_of(3), tiles_of(2)] * 2],
            out_specs=(
                rows(FF), rows(3 * D), rows(128), pl.BlockSpec((2, 128, D), lambda i, section: (0, i, 0)), rows(D))),
        name="join",
    )(lax.axis_index(SECTION).astype(jnp.int32).reshape(1), back.up_low_all, back.up_high_all, last.wide_low_all, last.wide_high_all, last.qkv_low_all, last.qkv_high_all, last.rows_own,
      last.rows_cross, last.rows_out_all, back.rows_own, back.rows_cross, back.rows_out_all, last.up_rest, last.qkv_rest,
      last.tiles, last.tiles_other, back.tiles, back.tiles_other)


def token_positions(block_order):
    offsets = jnp.arange(32, dtype=jnp.int32)
    groups = jnp.arange(2, dtype=jnp.int32)[:, None, None] * GROUP
    return (groups + block_order[:, :, None] * 32 + offsets).reshape(2, GROUP)


def swapped(section, first, second):
    own = jnp.where(section == 0, first, second)
    other = lax.ppermute(jnp.where(section == 0, second, first), SECTION, [(0, 1), (1, 0)])
    return jnp.where(section == 0, own, other), jnp.where(section == 0, other, own)


def gathered(x):
    return lax.all_gather(x, CONTEXT)


def shards(hidden_in, cotangent, block_order, qkv_weight, out_weight, up_weight, down_weight, norm_gains, norm_biases):
    section, ctx = lax.axis_index(SECTION), lax.axis_index(CONTEXT)
    params = jnp.concatenate([norm_gains[0], norm_biases[0]], axis=0).astype(F32)
    params = jnp.pad(params, ((0, 4), (0, 0)))
    grid = token_positions(block_order)
    own_positions = lax.dynamic_slice(grid, (section, ctx * ROWS), (1, ROWS))
    positions = grid.reshape(1, SEQ)
    slots = jnp.arange(32, dtype=jnp.int32)
    slot = jnp.sum(jnp.where(block_order[:, None, :] == slots[None, :, None], slots[None, None, :], 0), axis=2)
    group, odd = jnp.arange(2, dtype=jnp.int32)[:, None], slot % 2
    chip = slot // 2
    places = jnp.stack([10 * chip + 4 * group + 2 * odd, 10 * chip + 8 + odd, 2 * chip + odd])
    at = (block_order, places, positions, own_positions.reshape(ROWS, 1))
    at_back = (block_order, places, positions.reshape(SEQ, 1), own_positions)
    hidden = hidden_in[0]
    spread = spread_kernel(params, qkv_weight, up_weight)
    norms = spread.norms
    mid_all = gathered(spread.mid_piece)
    first = first_kernel(hidden, norms, spread.side_piece, spread.side_last, out_weight, down_weight)
    up_piece, first.q16 = lax.optimization_barrier((spread.side_piece[SHARD:], first.q16))
    up_all = gathered(up_piece)
    middle = middle_kernel(at, hidden, norms, first, mid_all, spread.mid_last)
    turn = turn_kernel(at, middle, middle.y, norms, first, up_all, spread.side_last[SHARD:], cotangent[0])
    back = back_kernel(
        at_back, middle, turn, middle.y, turn, norms, first, middle.attended16, mid_all, spread.mid_last)
    last = last_kernel(at_back, first, middle, hidden, back, turn.up_g_last, norms)
    up, qkv, norm_sums, down, out = join_kernel(back, last)
    norm_sums = norm_sums[:, 64:68].T
    activations = jnp.stack(swapped(section, middle.y, turn.out))
    input_grads = jnp.stack(swapped(section, last.in_grad, back.in_grad))
    return (
        activations[None, None],
        input_grads[None, None],
        qkv[None],
        out[None],
        up[None],
        down.reshape(D, D)[None],
        norm_sums[None, 0::2],
        norm_sums[None, 1::2],
    )


def solution(mesh):
    tokens = P(LINE, None, CONTEXT, None)
    rows = P(SECTION, LINE, None)
    norms = P(SECTION, None, LINE)
    layers = P(SECTION, LINE, None, CONTEXT, None)
    return jax.shard_map(
        shards,
        mesh=mesh,
        in_specs=(tokens, tokens, P(), rows, rows, rows, rows, norms, norms),
        out_specs=(layers, layers, rows, rows, rows, rows, norms, norms),
        check_vma=False,
    )
```

time: 513 us -> 463 us (0.903)
  Pallas kernels: 451 us -> 409 us
  waiting for transfers between devices: 22.1 us -> 5.81 us
  starting transfers between devices: 2.33 us -> 13.1 us
    pallas_call x12 -> x6, Pallas kernels: 439 us -> 400 us  [call(): pl.pallas_call(kernel, out_shape=tuple((value[0] for value in outs.values...]
    psum x2 -> x0, waiting for transfers between devices: 21.8 us -> none  [the longest x1 21.8 us: shards(): down0, out0 = lax.psum((down_g, out_g), CONTEXT)]
    ppermute x2, starting transfers between devices: 1.76 us -> 13 us  [swapped(): lax.ppermute(jnp.where(section == 0, second, first), SECTION, [(0, 1), (1...]
    all_gather x2, waiting for transfers between devices: 0.01 us -> 5.22 us  [gathered(): return lax.all_gather(x, CONTEXT)]
  transfers between devices with their start and end apart: 6 -> 4, of which waited for: 2 -> 2; matrix products, arithmetic and copies ran while one was open for 2% -> 2% of each run, Pallas kernels for 69% -> 26%
where the time goes in v3:
time: 463 us; the launch traced here: 456 us
  Pallas kernels  409 us (88%)
  between operations  14.4 us (3%)
  starting transfers between devices  13.1 us (3%)
  local copies, waits for them, and re-layouts  8.86 us (2%)
  waiting for transfers between devices  5.81 us (1%)
  other arithmetic  4.86 us (1%)
    pallas_call x6, Pallas kernels, call(): pl.pallas_call(kernel, out_shape=tuple((value[0] for value in outs.values...  400 us
    ppermute x2, starting transfers between devices, swapped(): lax.ppermute(jnp.where(section == 0, second, first), SECTION, [(0, 1), (1...  13 us
    pallas_call x1, Pallas kernels, join_kernel(): pl.pallas_call(body, out_shape=(spec((SLICE, FF), F32), spec((SLICE, 3 *...  9.68 us
  transfers between devices with their start and end apart: 4, of which 2 were waited for; matrix products, arithmetic and copies ran while one was open for 2% of the time, Pallas kernels for 26%

profile of v3, /device:TPU:1, one launch (start us, length us, event | category | flops | bytes accessed | tf_op | source)
XLA Modules:
  0.0 456.3 jit_solution(15366970300618182945)
XLA Ops:
  7.2 1.3 fusion.3.refs_0_
  8.5 16.6 %spread.1 = (f32[2,8,1088]{2,1,0:T(8,128)}, bf16[8,16,640]{2,1,0:T(8,128)(2,1)}, bf16[8,16,640]{2,1,0:T(8,128)(2,1)}, bf16[8,16,640]{2,1,0:T(8,128)(2,1)}, bf16[8,16,640]{2,1,0:T(8,128)(2,1)}) custom-call(f32[8,272]{1,0:T(8,128)} %fusion.3.refs_0_, bf16[1,272,3264]{2,1,0:T(8,128)(2,1)} %refs_1_.1, bf16[1,272,4352]{2,1,0:T(8,128)(2,1)} %refs_2_.1), custom_call_target="tpu_custom_call" | custom-call | tf_op jit(solution)/shard_map/spread/pallas_call | solution.py:54
  25.2 1.5 slice.15
  26.8 45.1 %first.1 = (bf16[512,1088]{1,0:T(8,128)(2,1)}, bf16[16,160,128]{2,1,0:T(8,128)(2,1)}, bf16[2,16,64,128]{3,2,1,0:T(8,128)(2,1)}, bf16[64,64]{1,0:T(8,128)(2,1)}, ...) custom-call(bf16[2,64,1088]{2,1,0:T(8,128)(2,1)} %bitcast.60, ...), custom_call_target="tpu_custom_call" | custom-call | tf_op jit(solution)/shard_map/first/pallas_call | solution.py:54
  71.9 0.6 slice.16.refs_12_
  72.6 0.1 iota_add_fusion
  72.7 0.7 add.160.refs_2_
  73.4 2.0 add.166.refs_2_
  75.4 0.1 broadcast_in_dim.52
  75.6 0.1 add.161
  75.7 0.1 dynamic-slice
  75.7 0.1 dynamic-slice_add_fusion.refs_3_
  75.8 0.7 copy.33.refs_3_
  76.5 0.1 select_reduce_fusion
  76.6 0.1 multiply_add_fusion.2
  76.7 0.6 pad_add_fusion.refs_1_
  77.3 5.2 %all-gather.5.cloned.1.call-done = bf16[128,16,640]{2,1,0:T(8,128)(2,1)} async-done(((bf16[8,16,640]{2,1,0:T(8,128)(2,1)}), bf16[128,16,640]{2,1,0:T(8,128)(2,1)}) %all-gather.5.cloned.1.call-update) | async-done | bytes 2621456 | tf_op jit(solution)/shard_map/all_gather | solution.py:1783
  82.5 61.8 %middle.1 = (bf16[64,64]{1,0:T(8,128)(2,1)}, bf16[64,16,64]{2,1,0:T(8,128)(2,1)}, f32[1024,128]{1,0:T(8,128)}, f32[64,128]{1,0:T(8,128)}, bf16[512,128]{1,0:T(8,...) custom-call(s32[2,32]{1,0:T(2,128)} %refs_0_.7, ...), custom_call_target="tpu_custom_call" | custom-call | tf_op jit(solution)/shard_map/middle/pallas_call | solution.py:54
  144.3 73.2 %turn.1 = (bf16[64,64]{1,0:T(8,128)(2,1)}, bf16[64,16,64]{2,1,0:T(8,128)(2,1)}, f32[1024,128]{1,0:T(8,128)}, f32[64,128]{1,0:T(8,128)}, bf16[64,1088]{1,0:T(8,12...) custom-call(s32[2,32]{1,0:T(2,128)} %refs_0_.7, ...), custom_call_target="tpu_custom_call" | custom-call | tf_op jit(solution)/shard_map/turn/pallas_call | solution.py:54
  217.5 102.2 %back.1 = (bf16[64,1088]{1,0:T(8,128)(2,1)}, f32[64,1088]{1,0:T(8,128)}, bf16[16,32,128]{2,1,0:T(8,128)(2,1)}, bf16[64,64]{1,0:T(8,128)(2,1)}, bf16[4,16,640]{2,...) custom-call(s32[2,32]{1,0:T(2,128)} %refs_0_.7, ...), custom_call_target="tpu_custom_call" | custom-call | tf_op jit(solution)/shard_map/back/pallas_call | solution.py:54
  319.8 100.8 %last.1 = (bf16[64,1088]{1,0:T(8,128)(2,1)}, bf16[4,4,16,2176]{3,2,1,0:T(8,128)(2,1)}, bf16[4,4,16,2176]{3,2,1,0:T(8,128)(2,1)}, bf16[4,4,16,1664]{3,2,1,0:T(8,1...) custom-call(s32[2,32]{1,0:T(2,128)} %refs_0_.7, ...), custom_call_target="tpu_custom_call" | custom-call | tf_op jit(solution)/shard_map/last/pallas_call | solution.py:54
  420.5 0.9 broadcast_select_fusion
  421.5 13.0 %collective-permute-start.1 = (bf16[64,1088]{1,0:T(8,128)(2,1)S(1)}, bf16[64,1088]{1,0:T(8,128)(2,1)S(1)}, u32[]{:S(2)}, u32[]{:S(2)}) collective-permute-start(bf16[64,1088]{1,0:T(8,128)(2,1)S(1)} %broadcast_select_fusion), channel_id=1, source_target_pairs={{0,64},{64,0},{1,65},{65,1},{2,66},{66,2},{3,67},{67,3},{4,68},{68... | collective-permute-start | bytes 417800 | tf_op jit(solution)/shard_map/ppermute | solution.py:1778
  434.5 9.7 %join.1 = (f32[272,4352]{1,0:T(8,128)}, f32[272,3264]{1,0:T(8,128)}, f32[272,128]{1,0:T(8,128)}, f32[2,544,1088]{2,1,0:T(8,128)}, f32[272,1088]{1,0:T(8,128)}) custom-call(s32[1]{0:T(128)} %bitcast.18._, bf16[4,4,16,2176]{3,2,1,0:T(8,128)(2,1)} %get-tuple-element.145.up_low, bf16[4,4,16,2176]{3,2,1,0:T(8,128)(2,1)} %get-tuple-element.146.up_high, ...), custom_call_target="tpu_custom_call" | custom-call | tf_op jit(solution)/shard_map/join/pallas_call | solution.py:1750
  444.2 1.0 slice_bitcast_fusion
  445.2 0.2 slice.18
  445.5 0.3 slice.19
  445.8 0.7 copy.37
  446.5 0.7 copy.38
  447.2 0.8 maximum_bitcast_fusion.1
  448.0 0.6 collective-permute-done
  448.6 0.8 maximum_bitcast_fusion
  (29 shorter events, 0.4 us)
Async XLA Ops:
  7.2 75.3 %all-gather.5.cloned.1.call-start = ((), (), s32[]{:S(2)}) async-start(), calls=%async_computation | async-start | bytes 2785280 | tf_op jit(solution)/shard_map/all_gather | solution.py:1783
  25.2 119.1 %all-gather.7.cloned.1.call-start = ((), (), s32[]{:S(2)}) async-start(), calls=%async_computation.1 | async-start | bytes 1392640 | tf_op jit(solution)/shard_map/all_gather | solution.py:1783
  26.8 45.1 %copy-start.4 = (bf16[8,16,640]{2,1,0:T(8,128)(2,1)S(1)}, bf16[8,16,640]{2,1,0:T(8,128)(2,1)}, u32[]{:S(2)}) copy-start(bf16[8,16,640]{2,1,0:T(8,128)(2,1)} %get-tuple-element.90.refs_3_) | copy-start | bytes 491524
  26.8 45.8 %copy-start.5 = (s32[2,32]{1,0:T(2,128)S(1)}, s32[2,32]{1,0:T(2,128)}, u32[]{:S(2)}) copy-start(s32[2,32]{1,0:T(2,128)} %refs_0_.7) | copy-start | bytes 772
  75.8 68.5 %copy-start.6 = (s32[1,64]{1,0:T(1,128)}, s32[1,64]{1,0:T(1,128)S(1)}, u32[]{:S(2)}) copy-start(s32[1,64]{1,0:T(1,128)S(1)} %dynamic-slice_add_fusion.refs_3_) | copy-start | bytes 772
  319.7 100.8 %copy-start.2 = (bf16[64,1088]{1,0:T(8,128)(2,1)S(1)}, bf16[64,1088]{1,0:T(8,128)(2,1)}, u32[]{:S(2)}) copy-start(bf16[64,1088]{1,0:T(8,128)(2,1)} %get-tuple-element.144) | copy-start | bytes 417796
  319.7 114.8 %copy-start = (bf16[64,1088]{1,0:T(8,128)(2,1)S(1)}, bf16[64,1088]{1,0:T(8,128)(2,1)}, u32[]{:S(2)}) copy-start(bf16[64,1088]{1,0:T(8,128)(2,1)} %get-tuple-element.99.refs_7_.refs_14_) | copy-start | bytes 417796
  319.7 114.8 %copy-start.1 = (bf16[64,1088]{1,0:T(8,128)(2,1)S(1)}, bf16[64,1088]{1,0:T(8,128)(2,1)}, u32[]{:S(2)}) copy-start(bf16[64,1088]{1,0:T(8,128)(2,1)} %get-tuple-element.104) | copy-start | bytes 417796
  421.5 25.7 %collective-permute-start.1 = (bf16[64,1088]{1,0:T(8,128)(2,1)S(1)}, bf16[64,1088]{1,0:T(8,128)(2,1)S(1)}, u32[]{:S(2)}, u32[]{:S(2)}) collective-permute-start(bf16[64,1088]{1,0:T(8,128)(2,1)S(1)} %broadcast_select_fusion), channel_id=1, source_target_pairs={{0,64},{64,0},{1,65},{65,1},{2,66},{66,2},{3,67},{67,3},{4,68},{68... | collective-permute-start | bytes 417800 | tf_op jit(solution)/shard_map/ppermute | solution.py:1778
  434.5 12.6 %copy-start.3 = (bf16[64,1088]{1,0:T(8,128)(2,1)S(1)}, bf16[64,1088]{1,0:T(8,128)(2,1)}, u32[]{:S(2)}) copy-start(bf16[64,1088]{1,0:T(8,128)(2,1)} %get-tuple-element.143) | copy-start | bytes 417796
  447.1 1.4 collective-permute-start
Sparse Core Ops, SparseCore 0:
  25.3 57.1 all-gather.4
  85.3 42.4 all-gather.6

commit v4 on v3

--- a/solution.py
+++ b/solution.py
@@ -26,7 +26,7 @@
 MESH = pl.DeviceIdType.MESH
 VMEM = pltpu.VMEM
 ANY = pl.ANY
-VMEM_BYTES = 56 * 2**20
+VMEM_BYTES = 58 * 2**20
 SECTION, CONTEXT, LINE = "section", "ctx", "shard"
 TILES = (68, 16, WINDOW)
 
@@ -137,6 +137,9 @@
         copy = self.local(src, dst)
         self.sent.append(types.SimpleNamespace(wait_send=copy.wait))
 
+    def wait_later(self, ref, sem):
+        self.sent.append(types.SimpleNamespace(wait_send=lambda: wait_bytes(ref, sem)))
+
     def send(self, src, dst, to, arrive, leave=None):
         copy = pltpu.make_async_remote_copy(
             src_ref=src, dst_ref=dst, send_sem=self.sem() if leave is None else leave,
@@ -172,18 +175,42 @@
     pltpu.make_async_copy(ref, ref, sem).wait()
 
 
-HALF = ROWS // 2
+PARTS = 2
+HALF = ROWS // PARTS
 
 
 def half_rows(half):
     return slice(HALF * half, HALF * half + HALF)
+
+
+class Messages:
+    def __init__(self, h, arrived):
+        self.h, self.arrived, self.leave = h, arrived, h.sem()
+
+    def add(self, sends):
+        for src, dst, to, here, arrive in sends:
+            copy = pltpu.make_async_remote_copy(
+                src_ref=src, dst_ref=dst, send_sem=self.leave, recv_sem=arrive, device_id=to, device_id_type=MESH)
+            pl.when(jnp.logical_not(here))(copy.start)
+            pl.when(here)(pltpu.make_async_copy(src, dst, arrive).start)
+
+    def done(self):
+        h = self.h
+
+        def wait_send():
+            pl.when(h.c // 8 != h.s)(lambda: wait_bytes(self.arrived, self.leave))
+            pl.when(h.c // 8 == h.s)(lambda: wait_bytes(self.arrived.at[pl.ds(0, 15)], self.leave))
+
+        h.sent.append(types.SimpleNamespace(wait_send=wait_send))
 
 
 class Gather8:
     def __init__(self, here, full):
         self.here, self.full = here, full
-        self.own = [[here.sem() for _ in range(2)] for _ in range(SHARD)]
-        self.other = [[here.sem() for _ in range(2)] for _ in range(SHARD)]
+        self.own = [[here.sem() for _ in range(PARTS)] for _ in range(SHARD)]
+        self.other = [[here.sem() for _ in range(PARTS)] for _ in range(SHARD)]
+        self.leave = here.sem()
+        here.wait_later(full.at[pl.ds(0, 7 * ROWS)], self.leave)
 
     def rows(self, shard, core, half):
         return self.full.at[pl.ds(pl.multiple_of((shard * 2 + core) * ROWS + half * HALF, HALF), HALF)]
@@ -192,20 +219,20 @@
         h = self.here
         mine = self.rows(h.y, h.s, half)
         mine[...] = value
-        h.send(mine, mine, h.sibling(), self.other[0][half])
+        h.send(mine, mine, h.sibling(), self.other[0][half], self.leave)
         for step in (1, 3, 2):
-            h.send(mine, mine, (h.s, h.c, h.shard(step)), self.own[SHARD - step][half])
+            h.send(mine, mine, (h.s, h.c, h.shard(step)), self.own[SHARD - step][half], self.leave)
 
     def relay(self, step):
         h = self.here
-        for half in range(2):
+        for half in range(PARTS):
             part = self.rows(h.shard(step), h.s, half)
             wait_bytes(part, self.own[step][half])
-            h.send(part, part, h.sibling(), self.other[step][half])
+            h.send(part, part, h.sibling(), self.other[step][half], self.leave)
 
     def wait(self, step):
         h = self.here
-        for half in range(2):
+        for half in range(PARTS):
             wait_bytes(self.rows(h.shard(step), 1 - h.s, half), self.other[step][half])
 
 
@@ -213,8 +240,11 @@
     def __init__(self, here, bufs):
         self.here = here
         self.to_core, self.mine, self.from_core, self.to_shard, self.from_shard = bufs
-        self.core = [[here.sem() for _ in range(2)] for _ in range(SHARD)]
-        self.shard = [[here.sem() for _ in range(2)] for _ in range(SHARD)]
+        self.core = [[here.sem() for _ in range(PARTS)] for _ in range(SHARD)]
+        self.shard = [[here.sem() for _ in range(PARTS)] for _ in range(SHARD)]
+        self.leave = [here.sem(), here.sem()]
+        here.wait_later(self.from_core, self.leave[0])
+        here.wait_later(self.from_shard.at[pl.ds(0, 3)], self.leave[1])
 
     def part(self, ref, step, half):
         return ref.at[step, pl.ds(half * HALF, HALF)]
@@ -224,14 +254,14 @@
         low, high = block[:ROWS], block[ROWS:]
         self.to_core[step] = jnp.where(h.s == 0, high, low).astype(BF16)
         self.mine[step] = jnp.where(h.s == 0, low, high)
-        for half in range(2):
+        for half in range(PARTS):
             h.send(
                 self.part(self.to_core, step, half), self.part(self.from_core, step, half), h.sibling(),
-                self.core[step][half])
+                self.core[step][half], self.leave[0])
 
     def relay(self, steps):
         h = self.here
-        for half in range(2):
+        for half in range(PARTS):
             for step in steps:
                 part = self.part(self.from_core, step, half)
                 wait_bytes(part, self.core[step][half])
@@ -239,7 +269,8 @@
                 out = self.part(self.to_shard, step, half)
                 out[...] = total.astype(BF16)
                 h.send(
-                    out, self.part(self.from_shard, step, half), (h.s, h.c, h.shard(step)), self.shard[step][half])
+                    out, self.part(self.from_shard, step, half), (h.s, h.c, h.shard(step)), self.shard[step][half],
+                    self.leave[1])
 
     def result(self, half):
         part = self.part(self.from_core, 0, half)
@@ -338,16 +369,16 @@
         side_last=(spec((8, 16, WINDOW)), VMEM))
     scratch = dict(
         params_in=VMEM((8, 8, SLICE), F32), up_rows=VMEM((32, FF), BF16), qkv_rows=VMEM((32, 3 * D), BF16),
-        mid=VMEM((8, 2, 16, WINDOW), BF16), up=VMEM((8, 2, 16, WINDOW), BF16), sems=pltpu.SemaphoreType.DMA((64,)))
+        mid=VMEM((8, 2, 16, WINDOW), BF16), up=VMEM((8, 2, 16, WINDOW), BF16), sems=pltpu.SemaphoreType.DMA((42,)))
     return call("spread", body, ins, outs, scratch, collective_id=0)
 
 
 def load_tiles(h, gathered, last, dst, first=0):
-    copies = []
+    sem = h.sem()
     for i in range(SHARD):
-        copies.append(h.local(gathered.at[:, first + i], dst.at[pl.ds(17 * i, 16)]))
-        copies.append(h.local(last.at[first + i], dst.at[17 * i + 16]))
-    return copies
+        pltpu.make_async_copy(gathered.at[:, first + i], dst.at[pl.ds(17 * i, 16)], sem).start()
+        pltpu.make_async_copy(last.at[first + i], dst.at[17 * i + 16], sem).start()
+    return [types.SimpleNamespace(wait=lambda: wait_bytes(dst, sem))]
 
 
 def place(value, parts, last):
@@ -471,10 +502,12 @@
     leave16, arrive16, cross16 = h.sem(), h.sem(), h.sem()
     for step in range(1, CTX):
         h.send(own_kv, own_kv, (h.s, lax.rem(h.c + step, CTX), h.y), arrive16, leave16)
+    messages = Messages(h, r.message_in)
     for step in ORDER:
         if step:
             gather.relay(step)
         gather.wait(step)
+        sends = []
         shard = h.shard(step)
         block = r.a_vm[pl.ds(pl.multiple_of(shard * 128, 128), 128)]
         out = dot(block, r.qkv_vm[:, :, :384].reshape(D, 384)).astype(BF16)
@@ -487,9 +520,11 @@
                     packed = jnp.concatenate([out[at : at + 16, lanes], out[64 + at : 80 + at, lanes]], axis=1)
                     r.message[e, shard, core, 128 + 16 * b : 144 + 16 * b] = packed
                 chip = 8 * h.s + 4 * e + shard
-                h.send_or_keep(
+                sends.append((
                     r.message.at[e, shard, core], r.message_in.at[h.c], (core, chip, h.y),
-                    (chip == h.c) & (h.s == core), arrive)
+                    (chip == h.c) & (h.s == core), arrive))
+        messages.add(sends)
+    messages.done()
     h.save(r.a_vm, r.a_full)
     if after is not None:
         after()
@@ -513,7 +548,7 @@
         x = r.hidden[h.s].astype(F32)
         a_value = layer_norm(x, r.norms[0, 0:1], r.norms[0, 2:3]).astype(BF16)
         gather = Gather8(h, r.a_vm)
-        for half in range(2):
+        for half in range(PARTS):
             gather.start(a_value[half_rows(half)], half)
         weights.send_qkv_on()
         weights.wait_qkv()
@@ -529,7 +564,7 @@
     scratch = dict(
         **head_scratch(), qkv_low=VMEM((4, 4, 2, 16, WINDOW), BF16), qkv_high=VMEM((4, 4, 2, 16, WINDOW), BF16),
         down_rows=VMEM((D, D), BF16), out_rows=VMEM((SLICE, D), BF16), down_vm=VMEM((2, WINDOW, D), BF16),
-        out_vm=VMEM((2, 192, D), BF16), sems=pltpu.SemaphoreType.DMA((240,)))
+        out_vm=VMEM((2, 192, D), BF16), sems=pltpu.SemaphoreType.DMA((65,)))
     return call("first", body, ins, outs, scratch, collective_id=1)
 
 
@@ -622,9 +657,11 @@
     arrive = h.sem()
     to_core = h.c // 8
     e, j = lax.rem(h.c // 4, 2), lax.rem(h.c, 4)
-    for c in range(CTX):
-        h.send_or_keep(
-            r.attended.at[c], r.context_in.at[e, j, h.s], (to_core, c, h.y), (h.c == c) & (h.s == to_core), arrive)
+    messages = Messages(h, r.attended)
+    messages.add([
+        (r.attended.at[c], r.context_in.at[e, j, h.s], (to_core, c, h.y), (h.c == c) & (h.s == to_core), arrive)
+        for c in range(CTX)])
+    messages.done()
     return arrive
 
 
@@ -650,7 +687,7 @@
         sums.put(step, dot(r.context[block_rows(h, step)], r.out_vm[:128]))
     sums.relay((2, 1, 3))
     own = x + dot(r.attended16[...], r.out_vm[128:])
-    for half in range(2):
+    for half in range(PARTS):
         residual = own[half_rows(half)] + sums.result(half)
         r.residual[half_rows(half)] = residual
         ready(half, residual)
@@ -692,7 +729,7 @@
         for copy in head_loads:
             copy.wait()
         gather = Gather8(h, r.a_vm)
-        for half in range(2):
+        for half in range(PARTS):
             y = (r.residual[half_rows(half)] + sums.result(half)).astype(BF16)
             r.y[half_rows(half)] = y
             gather.start(layer_norm(y.astype(F32), r.norms[1, 0:1], r.norms[1, 2:3]).astype(BF16), half)
@@ -707,7 +744,7 @@
         pre=(spec((512, WINDOW), F32), ANY), y=(spec((ROWS, D)), VMEM), **head_outs())
     scratch = dict(
         **attend_scratch(), **middle_scratch(), **head_scratch(), b_vm=VMEM((512, D), BF16), pre_vm=VMEM((512, WINDOW), F32),
-        sems=pltpu.SemaphoreType.DMA((300,)))
+        sems=pltpu.SemaphoreType.DMA((85,)))
     return call("middle", body, ins, outs, scratch, collective_id=2)
 
 
@@ -758,12 +795,12 @@
 
 def finish_back(h, r, sums, layer, residual, out_grad, context, down_ready, up_ready, beside, near_end=None):
     r.down_grad[...] = dot_tn(r.hidden_low[...], r.m_full[...]).astype(BF16).reshape(40, 16, D)
-    down_ready(r.down_grad.at[pl.ds(2 * lax.rem(h.y * 2 + h.s, 4), 34)])
+    down_ready(r.down_grad, 2 * lax.rem(h.y * 2 + h.s, 4))
     place(dot_tn(r.b_vm[...], r.pre_grad[...]), r.up_grad, r.up_g_last)
     up_ready()
     gather = Gather8(h, r.z_full)
     gain_rows, normed_grad = [], []
-    for half in range(2):
+    for half in range(PARTS):
         rows = half_rows(half)
         normed_grad.append(sums.result(half))
         back, gains = norm_back(normed_grad[half], residual[rows], r.norms[layer, 1:2])
@@ -777,10 +814,12 @@
     beside()
     arrive = h.sem()
     r.context16_grad[...] = dot_nt(z, r.out_vm[128:]).astype(BF16)
+    messages = Messages(h, r.context_grad_in)
     for step in ORDER:
         if step:
             gather.relay(step)
         gather.wait(step)
+        sends = []
         shard = h.shard(step)
         out = dot_nt(r.z_full[block_rows(h, step)], r.out_vm[:128]).astype(BF16)
         for e in range(2):
@@ -791,9 +830,11 @@
                     r.context_message[e, shard, core, 16 * b : 16 * b + 16] = jnp.concatenate(
                         [out[at : at + 16, lanes], out[64 + at : 80 + at, lanes]], axis=1)
                 chip = 8 * h.s + 4 * e + shard
-                h.send_or_keep(
+                sends.append((
                     r.context_message.at[e, shard, core], r.context_grad_in.at[h.c], (core, chip, h.y),
-                    (chip == h.c) & (h.s == core), arrive)
+                    (chip == h.c) & (h.s == core), arrive))
+        messages.add(sends)
+    messages.done()
     r.out_g[:8] = dot_tn(context[...], r.z_full[...]).astype(BF16).reshape(8, 16, D)
     r.out_g[8:] = dot_tn(r.attended16[...], z).astype(BF16).reshape(4, 16, D)
     if near_end is not None:
@@ -810,7 +851,7 @@
         h.ready()
         out_grad = r.cotangent[h.s]
         gather_m = Gather8(h, r.m_full)
-        for half in range(2):
+        for half in range(PARTS):
             gather_m.start(out_grad[half_rows(half)], half)
         attend(h, r)
         arrive = gather_context(h, r)
@@ -827,7 +868,7 @@
             gather.start(layer_norm(residual, r.norms[1, 1:2], r.norms[1, 3:4]).astype(BF16), half)
 
         run_out(h, r, r.x[...].astype(F32), ready)
-        back_sums, sums = Scatter8(h, r.to_norm2), Scatter8(h, r.to_down)
+        back_sums = Scatter8(h, r.to_norm2)
         for step in ORDER:
             if step:
                 gather.relay(step)
@@ -837,9 +878,8 @@
             u = dot(r.b_vm[rows], whole(r.up_vm))
             g = gelu(u).astype(BF16)
             back_block(h, r, rows, back_sums, step, u, g)
-            sums.put(step, dot(g, r.down_vm[...]))
         back_sums.relay((1, 3, 2))
-        sums.relay((1, 3, 2))
+        h.save(r.hidden_low, r.hidden_out)
 
         ups = [
             Reduce16(h, r.up_grad.at[:, :, pl.ds(2 * i, 2)], (r.ups_in.at[i], (r.up_mine_a, r.up_mine_b)[i], None), i == 0)
@@ -856,14 +896,9 @@
                 each.add()
             first_rows.add()
 
-        def beside():
-            for half in range(2):
-                rows = half_rows(half)
-                r.out[rows] = (r.residual[rows] + sums.result(half)).astype(BF16)
-
         finish_back(
             h, r, back_sums, 1, r.residual[...], out_grad.astype(F32), r.context, first_rows.load,
-            up_ready, beside, near_end)
+            up_ready, lambda: None, near_end)
         h.finish()
 
     ins = dict(
@@ -871,11 +906,11 @@
         down_w=(first.down_w, ANY), up_all=(up_all, ANY), up_last=(up_last, ANY),
         cotangent=(cotangent, VMEM))
     outs = dict(
-        **attend_outs(), out=(spec((ROWS, D)), VMEM), **first_rows_outs(),
+        **attend_outs(), hidden_out=(spec((512, WINDOW)), ANY), residual=(spec((ROWS, D), F32), VMEM), **first_rows_outs(),
         up_mine_a=(spec((4, 2, 16, WINDOW)), VMEM), up_mine_b=(spec((4, 2, 16, WINDOW)), VMEM), out_g=(spec((12, 16, D)), VMEM), **back_outs())
     scratch = dict(
-        **attend_scratch(), context=VMEM((512, 128), BF16), residual=VMEM((ROWS, D), F32), **middle_scratch(),
-        **first_rows_scratch(), ups_in=VMEM((2, 3, 4, 2, 16, WINDOW), BF16), **back_scratch(), sems=pltpu.SemaphoreType.DMA((400,)))
+        **attend_scratch(), context=VMEM((512, 128), BF16), **middle_scratch(),
+        **first_rows_scratch(), ups_in=VMEM((2, 3, 4, 2, 16, WINDOW), BF16), **back_scratch(), sems=pltpu.SemaphoreType.DMA((107,)))
     return call("turn", body, ins, outs, scratch, collective_id=3)
 
 
@@ -966,17 +1001,20 @@
         side_part=VMEM((4, 4, SHARD, 16, 256), BF16), to_norm1=scatter_scratch())
 
 
-def start_tail(h, r):
+def start_tail(h, r, after_last=lambda: None):
     attend_back_last(r)
     cross = h.sem()
     h.send(r.kv16_grad.at[1 - h.s], r.core16, h.sibling(), cross)
+    after_last()
     attend_back(h, r)
     arrive = h.sem()
     to_core = h.c // 8
     e, j = lax.rem(h.c // 4, 2), lax.rem(h.c, 4)
-    for c in range(CTX):
-        h.send_or_keep(
-            r.message.at[c], r.message_in.at[e, j, h.s], (to_core, c, h.y), (h.c == c) & (h.s == to_core), arrive)
+    messages = Messages(h, r.message)
+    messages.add([
+        (r.message.at[c], r.message_in.at[e, j, h.s], (to_core, c, h.y), (h.c == c) & (h.s == to_core), arrive)
+        for c in range(CTX)])
+    messages.done()
     wait_bytes(r.core16, cross)
     r.sum16[...] = (r.kv16_grad[h.s].astype(F32) + r.core16[...].astype(F32)).astype(BF16)
     leave16, arrive16 = h.sem(), h.sem()
@@ -1021,7 +1059,7 @@
     own_grad = dot_tn(r.a_vm[h.rows(h.y, h.s)], grads16)
     beside()
     gain_rows, normed_grad = [], []
-    for half in range(2):
+    for half in range(PARTS):
         rows = half_rows(half)
         normed_grad.append(own[rows] + sums.result(half))
         back, gains = norm_back(normed_grad[half], x[rows], r.norms[layer, 0:1])
@@ -1057,6 +1095,7 @@
         h = Here(r.sems)
         tail_loads = load_tiles(h, r.up_all, r.up_last, r.qkv_vm, SHARD)
         tail_loads.append(h.local(r.a_full, r.a_vm))
+        out_loads = [h.local(r.hidden1, r.hidden_low), h.local(r.down_tiles.at[1], r.down_grad)]
         loads = load_layer(h, r, 0, 0)
         loads += [h.local(r.b_full, r.b_vm), h.local(r.pre, r.pre_vm), h.local(r.context, r.context_vm)]
         h.barrier()
@@ -1075,7 +1114,12 @@
             each.send_on()
         rows16.start()
         send_out(h, r, r.out1_g, 1, arrive_out, arrive_last)
-        waits = start_tail(h, r)
+        out_sums = Scatter8(h, r.to_down)
+        for copy in out_loads:
+            copy.wait()
+        for step in (2, 1, 3, 0):
+            out_sums.put(step, dot(r.hidden_low[block_rows(h, step)], r.down_grad[...].reshape(WINDOW, D)))
+        waits = start_tail(h, r, lambda: out_sums.relay((2, 1, 3)))
 
         def settle(core):
             @pl.when(h.s == core)
@@ -1094,6 +1138,9 @@
         spreads = [Spread16(h, parts, i == 0, 1) for i, parts in enumerate((r.up_low, r.up_high))]
 
         def arrived():
+            for half in range(PARTS):
+                rows = half_rows(half)
+                r.out[rows] = (r.residual1[rows] + out_sums.result(half)).astype(BF16)
             for i in range(2):
                 r.up1_piece[2 * i : 2 * i + 2] = ups[i].result()
             send_piece(h, r.up1_piece, r.up_in, 1, arrive_up)
@@ -1135,8 +1182,8 @@
             if step == 1:
                 rows16.spread_on()
         sums.relay((1, 3, 2))
-        def down_ready(rows):
-            first_rows.load(rows)
+        def down_ready(rows, first):
+            first_rows.load(rows, first)
             main.middle()
             side.middle()
 
@@ -1152,6 +1199,7 @@
             send_out(h, r, r.out_g, 0, arrive_out, arrive_last)
             up0.add()
             first_rows.add()
+            rows16.finish()
             for each in spreads:
                 each.finish()
             h.save_on(1, r.up_low, r.up_low_all)
@@ -1159,7 +1207,6 @@
 
         finish_back(
             h, r, sums, 0, r.residual[...], r.in_grad[...].astype(F32), r.context_vm, down_ready, up_ready, beside, near_end)
-        rows16.finish()
 
         settle(0)
         h.finish()
@@ -1169,20 +1216,22 @@
         context=(kept.context, ANY), residual=(kept.residual, VMEM), attended16=(attended16, VMEM),
         out_w=(first.out_w, ANY), down_w=(first.down_w, ANY), up_all=(mid_all, ANY), up_last=(mid_last, ANY),
         up_mine_a=(above.up_mine_a, VMEM), up_mine_b=(above.up_mine_b, VMEM), out1_g=(above.out_g, VMEM),
-        mine_a=(above.next_a, VMEM), mine_b=(above.next_b, VMEM), mine_beside=(above.next_beside, VMEM))
+        mine_a=(above.next_a, VMEM), mine_b=(above.next_b, VMEM), mine_beside=(above.next_beside, VMEM),
+        hidden1=(above.hidden_out, ANY), residual1=(above.residual, VMEM),
+        down_tiles=(first.down_w.reshape(2, 40, 16, D), ANY))
     piece, half = (spec((SHARD, 16, WINDOW)), VMEM), (spec((4, 4, 16, 2176)), ANY)
     outs = dict(
-        **tail_outs(), **back_outs(), qkv_g_last=piece, qkv1_piece=piece, up0_mine=(spec((4, SHARD, 16, WINDOW)), VMEM),
+        **tail_outs(), **back_outs(), out=(spec((ROWS, D)), VMEM), qkv_g_last=piece, qkv1_piece=piece, up0_mine=(spec((4, SHARD, 16, WINDOW)), VMEM),
         up_low_all=half, up_high_all=half, **rows_outs(), **rows_results(),
         **first_rows_outs(), out_sum=(spec((17, 16, D)), VMEM))
     scratch = dict(
         out_vm=VMEM((192, D), BF16), up_vm=VMEM(TILES, BF16), down_vm=VMEM((WINDOW, D), BF16),
-        pre_vm=VMEM((512, WINDOW), F32), context_vm=VMEM((512, 128), BF16), out_g=VMEM((12, 16, D), BF16),
+        pre_vm=VMEM((512, WINDOW), F32), to_down=scatter_scratch(), context_vm=VMEM((512, 128), BF16), out_g=VMEM((12, 16, D), BF16),
         ups_second=VMEM((2, 3, 2, 16, WINDOW), BF16), **first_rows_scratch(),
         up0_in=VMEM((3, 4, SHARD, 16, WINDOW), BF16), up_low=VMEM((4, 4, 16, 2176), BF16),
         up_high=VMEM((4, 4, 16, 2176), BF16), main_sums=reduce_scratch(SHARD, 384), side_sums=reduce_scratch(SHARD, 256),
         up1_piece=VMEM((SHARD, 16, WINDOW), BF16), up_in=VMEM((8, 16, WINDOW), BF16), last_in=VMEM((8, 4, 16, D), BF16), **tail_scratch(), **back_scratch(),
-        **rows_scratch(), sems=pltpu.SemaphoreType.DMA((520,)))
+        **rows_scratch(), sems=pltpu.SemaphoreType.DMA((200,)))
     return call("back", body, ins, outs, scratch, collective_id=4)
 
 
@@ -1191,8 +1240,7 @@
         self.h, self.x_first = h, x_first
         self.on = None if core is None else h.s == core
         self.x, self.z = h.c // 4, lax.rem(h.c, 4)
-        self.first = [h.sem() for _ in range(3)]
-        self.second = [h.sem() for _ in range(3)]
+        self.first, self.second = h.sem(), h.sem()
 
     def when(self, act):
         act() if self.on is None else pl.when(self.on)(act)
@@ -1203,22 +1251,19 @@
     def along(self, axis_x):
         return [self.chip(self.x + j, self.z) if axis_x else self.chip(self.x, self.z + j) for j in (1, 2, 3)]
 
-    def send(self, pairs, targets, sems):
+    def send(self, pairs, targets, arrive, spare):
+        leave = self.h.sem()
         copies = [
             pltpu.make_async_remote_copy(
-                src_ref=src, dst_ref=dst, send_sem=self.h.sem(), recv_sem=sem, device_id=to, device_id_type=MESH)
-            for (src, dst), to, sem in zip(pairs, targets, sems)]
+                src_ref=src, dst_ref=dst, send_sem=leave, recv_sem=arrive, device_id=to, device_id_type=MESH)
+            for (src, dst), to in zip(pairs, targets)]
 
         def start():
             for i in (0, 2, 1):
                 copies[i].start()
 
-        def wait_send():
-            for copy in copies:
-                copy.wait_send()
-
         self.when(start)
-        self.h.sent.append(types.SimpleNamespace(wait_send=lambda: self.when(wait_send)))
+        self.h.sent.append(types.SimpleNamespace(wait_send=lambda: self.when(lambda: wait_bytes(spare, leave))))
 
 
 class Reduce16(Plane16):
@@ -1232,12 +1277,11 @@
         for j in (1, 2, 3):
             src = self.part.at[lax.rem(self.x + j, 4)] if self.x_first else self.part.at[:, lax.rem(self.z + j, 4)]
             pairs.append((src, self.first_in.at[j - 1]))
-        self.send(pairs, self.along(self.x_first), self.first)
+        self.send(pairs, self.along(self.x_first), self.first, self.first_in)
 
     def add(self):
         def add():
-            for j in range(3):
-                wait_bytes(self.first_in.at[j], self.first[j])
+            wait_bytes(self.first_in, self.first)
             for k in range(4):
                 own = self.part[self.x, k] if self.x_first else self.part[k, self.z]
                 self.mine[k] = added([own] + [self.first_in[j, k] for j in range(3)])
@@ -1247,15 +1291,14 @@
     def send_on(self):
         at = self.z if self.x_first else self.x
         pairs = [(self.mine.at[lax.rem(at + j, 4)], self.second_in.at[j - 1]) for j in (1, 2, 3)]
-        self.send(pairs, self.along(not self.x_first), self.second)
+        self.send(pairs, self.along(not self.x_first), self.second, self.second_in)
 
     def middle(self):
         self.add()
         self.send_on()
 
     def result(self):
-        for j in range(3):
-            wait_bytes(self.second_in.at[j], self.second[j])
+        wait_bytes(self.second_in, self.second)
         return added([self.mine[self.z if self.x_first else self.x]] + [self.second_in[j] for j in range(3)])
 
 
@@ -1270,23 +1313,15 @@
 
     def start(self):
         own = self.parts.at[self.x, self.z]
-        self.send([(own, own)] * 3, self.along(self.x_first), self.first)
+        self.send([(own, own)] * 3, self.along(self.x_first), self.first, self.parts.at[0, pl.ds(0, 3)])
 
     def middle(self):
-        def wait():
-            for sem in self.first:
-                wait_bytes(self.parts.at[0, 0], sem)
-
-        self.when(wait)
+        self.when(lambda: wait_bytes(self.parts.at[0, pl.ds(0, 3)], self.first))
         line = self.parts.at[:, self.z] if self.x_first else self.parts.at[self.x]
-        self.send([(line, line)] * 3, self.along(not self.x_first), self.second)
+        self.send([(line, line)] * 3, self.along(not self.x_first), self.second, self.parts.at[pl.ds(0, 3)])
 
     def finish(self):
-        def wait():
-            for sem in self.second:
-                wait_bytes(self.parts.at[0], sem)
-
-        self.when(wait)
+        self.when(lambda: wait_bytes(self.parts.at[pl.ds(0, 3)], self.second))
 
 
 class FirstRows:
@@ -1296,16 +1331,15 @@
             Reduce16(h, r.rows_a, (r.rows_in.at[0], r.next_a, None), True),
             Reduce16(h, r.rows_b, (r.rows_in.at[1], r.next_b, None), False)]
 
-    def load(self, down):
-        h, r = self.h, self.r
-        self.loads = [h.local(down.at[pl.ds(32, 2)], r.next_beside)]
-        for x in range(4):
+    def load(self, down, first):
+        r = self.r
+        for c in range(CTX):
             for i, parts in enumerate((r.rows_a, r.rows_b)):
-                self.loads += [h.local(down.at[8 * x + 2 * z + i], parts.at[x, z, 0]) for z in range(4)]
+                parts[c // 4, c % 4, 0] = down[first + 2 * c + i]
+        for i in range(2):
+            r.next_beside[i] = down[first + 32 + i]
 
     def start(self):
-        for copy in self.loads:
-            copy.wait()
         for each in self.sums:
             each.start()
 
@@ -1390,9 +1424,10 @@
         for each in self.spreads:
             each.start()
         for i in range(3):
+            leave = h.sem()
             copies = [
                 pltpu.make_async_remote_copy(
-                    src_ref=r.tiles.at[i], dst_ref=r.tiles.at[i], send_sem=h.sem(), recv_sem=self.arrive_each[i],
+                    src_ref=r.tiles.at[i], dst_ref=r.tiles.at[i], send_sem=leave, recv_sem=self.arrive_each[i],
                     device_id=(h.s, lax.rem(h.c + step, CTX), h.y), device_id_type=MESH)
                 for step in range(1, CTX)]
 
@@ -1402,13 +1437,10 @@
                 for copy in copies:
                     copy.start()
 
-            def wait_send(copies=copies):
-                for copy in copies:
-                    copy.wait_send()
-
             self.when(i, start, h.c == 5 * i)
             h.sent.append(types.SimpleNamespace(
-                wait_send=functools.partial(self.when, i, wait_send, h.c == 5 * i)))
+                wait_send=functools.partial(
+                    self.when, i, functools.partial(wait_bytes, r.tile_in.at[pl.ds(0, 15)], leave), h.c == 5 * i)))
 
     def spread_on(self):
         for each in self.spreads:
@@ -1466,10 +1498,24 @@
 
 
 def send_piece(h, piece, dst, layer, arrive):
+    leave = h.sem()
     for step in (1, 3, 2, 0):
         shard = h.shard(step)
-        h.send_or_keep(
-            piece.at[shard], dst.at[2 * h.y + h.s], (layer, h.c, shard), (h.s == layer) & (step == 0), arrive)
+        src, to = piece.at[shard], dst.at[2 * h.y + h.s]
+        copy = pltpu.make_async_remote_copy(
+            src_ref=src, dst_ref=to, send_sem=leave, recv_sem=arrive, device_id=(layer, h.c, shard),
+            device_id_type=MESH)
+        if step:
+            copy.start()
+        else:
+            pl.when(h.s != layer)(copy.start)
+            pl.when(h.s == layer)(pltpu.make_async_copy(src, to, arrive).start)
+
+    def wait_send():
+        pl.when(h.s != layer)(lambda: wait_bytes(dst.at[pl.ds(0, 4)], leave))
+        pl.when(h.s == layer)(lambda: wait_bytes(dst.at[pl.ds(0, 3)], leave))
+
+    h.sent.append(types.SimpleNamespace(wait_send=wait_send))
 
 
 def joined_up(windows):
@@ -1673,7 +1719,7 @@
         last_in=VMEM((CTX, 3, 16, WINDOW), BF16), late_in=VMEM((CTX, 16, WINDOW), BF16), wide_in=eight, qkv_in=eight, up0_piece=piece,
         up0_in=VMEM((3, SHARD, 16, WINDOW), BF16),
         rest_message=VMEM((2, 2, 16, WINDOW), BF16), rest=VMEM((4, 2, 2, 16, WINDOW), BF16),
-        sems=pltpu.SemaphoreType.DMA((440,)))
+        sems=pltpu.SemaphoreType.DMA((124,)))
     return call("last", body, ins, outs, scratch, collective_id=5)
 
 
@@ -1811,7 +1857,7 @@
     last = last_kernel(at_back, first, middle, hidden, back, turn.up_g_last, norms)
     up, qkv, norm_sums, down, out = join_kernel(back, last)
     norm_sums = norm_sums[:, 64:68].T
-    activations = jnp.stack(swapped(section, middle.y, turn.out))
+    activations = jnp.stack(swapped(section, middle.y, back.out))
     input_grads = jnp.stack(swapped(section, last.in_grad, back.in_grad))
     return (
         activations[None, None],

time: 463 us -> 442 us (0.955)
  Pallas kernels: 409 us -> 386 us
    pallas_call x6, Pallas kernels: 400 us -> 376 us  [call(): pl.pallas_call(kernel, out_shape=tuple((value[0] for value in outs.values...]
where the time goes in v4:
time: 442 us; the launch traced here: 436 us
  Pallas kernels  386 us (87%)
  between operations  14.7 us (3%)
  starting transfers between devices  13.3 us (3%)
  local copies, waits for them, and re-layouts  8.86 us (2%)
  waiting for transfers between devices  7.8 us (2%)
  other arithmetic  4.86 us (1%)
    pallas_call x6, Pallas kernels, call(): pl.pallas_call(kernel, out_shape=tuple((value[0] for value in outs.values...  376 us
    ppermute x2, starting transfers between devices, swapped(): lax.ppermute(jnp.where(section == 0, second, first), SECTION, [(0, 1), (1...  13.2 us
    pallas_call x1, Pallas kernels, join_kernel(): pl.pallas_call(body, out_shape=(spec((SLICE, FF), F32), spec((SLICE, 3 *...  9.68 us
  transfers between devices with their start and end apart: 4, of which 2 were waited for; matrix products, arithmetic and copies ran while one was open for 2% of the time, Pallas kernels for 26%

profile of v4, /device:TPU:1, one launch (start us, length us, event | category | flops | bytes accessed | tf_op | source)
XLA Modules:
  0.0 435.6 jit_solution(18358009744827831588)
XLA Ops:
  7.2 1.3 fusion.3.refs_0_
  8.5 16.4 %spread.1 = (f32[2,8,1088]{2,1,0:T(8,128)}, bf16[8,16,640]{2,1,0:T(8,128)(2,1)}, bf16[8,16,640]{2,1,0:T(8,128)(2,1)}, bf16[8,16,640]{2,1,0:T(8,128)(2,1)}, bf16[8,16,640]{2,1,0:T(8,128)(2,1)}) custom-call(f32[8,272]{1,0:T(8,128)} %fusion.3.refs_0_, bf16[1,272,3264]{2,1,0:T(8,128)(2,1)} %refs_1_.1, bf16[1,272,4352]{2,1,0:T(8,128)(2,1)} %refs_2_.1), custom_call_target="tpu_custom_call" | custom-call | tf_op jit(solution)/shard_map/spread/pallas_call | solution.py:54
  25.0 1.5 slice.15
  26.5 43.0 %first.1 = (bf16[512,1088]{1,0:T(8,128)(2,1)}, bf16[16,160,128]{2,1,0:T(8,128)(2,1)}, bf16[2,16,64,128]{3,2,1,0:T(8,128)(2,1)}, bf16[64,64]{1,0:T(8,128)(2,1)}, ...) custom-call(bf16[2,64,1088]{2,1,0:T(8,128)(2,1)} %bitcast.62, ...), custom_call_target="tpu_custom_call" | custom-call | tf_op jit(solution)/shard_map/first/pallas_call | solution.py:54
  69.5 0.6 slice.16.refs_12_
  70.3 0.1 iota_add_fusion
  70.3 0.7 add.160.refs_2_
  71.0 2.0 add.166.refs_2_
  73.1 0.1 broadcast_in_dim.52
  73.2 0.1 add.161
  73.3 0.1 dynamic-slice
  73.4 0.1 dynamic-slice_add_fusion.refs_3_
  73.5 0.7 copy.33.refs_3_
  74.2 0.1 select_reduce_fusion
  74.3 0.1 multiply_add_fusion.2
  74.4 0.6 pad_add_fusion.refs_1_
  75.0 7.2 %all-gather.5.cloned.1.call-done = bf16[128,16,640]{2,1,0:T(8,128)(2,1)} async-done(((bf16[8,16,640]{2,1,0:T(8,128)(2,1)}), bf16[128,16,640]{2,1,0:T(8,128)(2,1)}) %all-gather.5.cloned.1.call-update) | async-done | bytes 2621456 | tf_op jit(solution)/shard_map/all_gather | solution.py:1829
  82.2 59.3 %middle.1 = (bf16[64,64]{1,0:T(8,128)(2,1)}, bf16[64,16,64]{2,1,0:T(8,128)(2,1)}, f32[1024,128]{1,0:T(8,128)}, f32[64,128]{1,0:T(8,128)}, bf16[512,128]{1,0:T(8,...) custom-call(s32[2,32]{1,0:T(2,128)} %refs_0_.7, ...), custom_call_target="tpu_custom_call" | custom-call | tf_op jit(solution)/shard_map/middle/pallas_call | solution.py:54
  141.5 64.5 %turn.1 = (bf16[64,64]{1,0:T(8,128)(2,1)}, bf16[64,16,64]{2,1,0:T(8,128)(2,1)}, f32[1024,128]{1,0:T(8,128)}, f32[64,128]{1,0:T(8,128)}, bf16[512,640]{1,0:T(8,12...) custom-call(s32[2,32]{1,0:T(2,128)} %refs_0_.7, ...), custom_call_target="tpu_custom_call" | custom-call | tf_op jit(solution)/shard_map/turn/pallas_call | solution.py:54
  206.0 98.4 %back.1 = (bf16[64,1088]{1,0:T(8,128)(2,1)}, f32[64,1088]{1,0:T(8,128)}, bf16[16,32,128]{2,1,0:T(8,128)(2,1)}, bf16[64,64]{1,0:T(8,128)(2,1)}, bf16[4,16,640]{2,...) custom-call(s32[2,32]{1,0:T(2,128)} %refs_0_.7, ...), custom_call_target="tpu_custom_call" | custom-call | tf_op jit(solution)/shard_map/back/pallas_call | solution.py:54
  304.4 94.9 %last.1 = (bf16[64,1088]{1,0:T(8,128)(2,1)}, bf16[4,4,16,2176]{3,2,1,0:T(8,128)(2,1)}, bf16[4,4,16,2176]{3,2,1,0:T(8,128)(2,1)}, bf16[4,4,16,1664]{3,2,1,0:T(8,1...) custom-call(s32[2,32]{1,0:T(2,128)} %refs_0_.7, ...), custom_call_target="tpu_custom_call" | custom-call | tf_op jit(solution)/shard_map/last/pallas_call | solution.py:54
  399.3 0.9 broadcast_select_fusion
  400.3 13.2 %collective-permute-start.1 = (bf16[64,1088]{1,0:T(8,128)(2,1)S(1)}, bf16[64,1088]{1,0:T(8,128)(2,1)S(1)}, u32[]{:S(2)}, u32[]{:S(2)}) collective-permute-start(bf16[64,1088]{1,0:T(8,128)(2,1)S(1)} %broadcast_select_fusion), channel_id=1, source_target_pairs={{0,64},{64,0},{1,65},{65,1},{2,66},{66,2},{3,67},{67,3},{4,68},{68... | collective-permute-start | bytes 417800 | tf_op jit(solution)/shard_map/ppermute | solution.py:1824
  413.5 9.7 %join.1 = (f32[272,4352]{1,0:T(8,128)}, f32[272,3264]{1,0:T(8,128)}, f32[272,128]{1,0:T(8,128)}, f32[2,544,1088]{2,1,0:T(8,128)}, f32[272,1088]{1,0:T(8,128)}) custom-call(s32[1]{0:T(128)} %bitcast.19._, bf16[4,4,16,2176]{3,2,1,0:T(8,128)(2,1)} %get-tuple-element.149.up_low, bf16[4,4,16,2176]{3,2,1,0:T(8,128)(2,1)} %get-tuple-element.150.up_high, ...), custom_call_target="tpu_custom_call" | custom-call | tf_op jit(solution)/shard_map/join/pallas_call | solution.py:1796
  423.2 1.0 slice_bitcast_fusion
  424.2 0.2 slice.18
  424.5 0.3 slice.19
  424.8 0.7 copy.37
  425.5 0.7 copy.38
  426.2 0.8 maximum_bitcast_fusion.1
  427.0 0.6 collective-permute-done
  427.6 0.8 maximum_bitcast_fusion
  (29 shorter events, 0.4 us)
Async XLA Ops:
  7.2 75.0 %all-gather.5.cloned.1.call-start = ((), (), s32[]{:S(2)}) async-start(), calls=%async_computation | async-start | bytes 2785280 | tf_op jit(solution)/shard_map/all_gather | solution.py:1829
  24.9 116.6 %all-gather.7.cloned.1.call-start = ((), (), s32[]{:S(2)}) async-start(), calls=%async_computation.1 | async-start | bytes 1392640 | tf_op jit(solution)/shard_map/all_gather | solution.py:1829
  26.5 43.0 %copy-start.4 = (bf16[8,16,640]{2,1,0:T(8,128)(2,1)S(1)}, bf16[8,16,640]{2,1,0:T(8,128)(2,1)}, u32[]{:S(2)}) copy-start(bf16[8,16,640]{2,1,0:T(8,128)(2,1)} %get-tuple-element.92.refs_3_) | copy-start | bytes 491524
  26.5 43.7 %copy-start.5 = (s32[2,32]{1,0:T(2,128)S(1)}, s32[2,32]{1,0:T(2,128)}, u32[]{:S(2)}) copy-start(s32[2,32]{1,0:T(2,128)} %refs_0_.7) | copy-start | bytes 772
  73.5 68.0 %copy-start.6 = (s32[1,64]{1,0:T(1,128)}, s32[1,64]{1,0:T(1,128)S(1)}, u32[]{:S(2)}) copy-start(s32[1,64]{1,0:T(1,128)S(1)} %dynamic-slice_add_fusion.refs_3_) | copy-start | bytes 772
  304.4 94.9 %copy-start.2 = (bf16[64,1088]{1,0:T(8,128)(2,1)S(1)}, bf16[64,1088]{1,0:T(8,128)(2,1)}, u32[]{:S(2)}) copy-start(bf16[64,1088]{1,0:T(8,128)(2,1)} %get-tuple-element.148) | copy-start | bytes 417796
  304.4 109.1 %copy-start = (bf16[64,1088]{1,0:T(8,128)(2,1)S(1)}, bf16[64,1088]{1,0:T(8,128)(2,1)}, u32[]{:S(2)}) copy-start(bf16[64,1088]{1,0:T(8,128)(2,1)} %get-tuple-element.101.refs_7_.refs_14_) | copy-start | bytes 417796
  304.4 109.1 %copy-start.1 = (bf16[64,1088]{1,0:T(8,128)(2,1)S(1)}, bf16[64,1088]{1,0:T(8,128)(2,1)}, u32[]{:S(2)}) copy-start(bf16[64,1088]{1,0:T(8,128)(2,1)} %get-tuple-element.128) | copy-start | bytes 417796
  400.3 25.9 %collective-permute-start.1 = (bf16[64,1088]{1,0:T(8,128)(2,1)S(1)}, bf16[64,1088]{1,0:T(8,128)(2,1)S(1)}, u32[]{:S(2)}, u32[]{:S(2)}) collective-permute-start(bf16[64,1088]{1,0:T(8,128)(2,1)S(1)} %broadcast_select_fusion), channel_id=1, source_target_pairs={{0,64},{64,0},{1,65},{65,1},{2,66},{66,2},{3,67},{67,3},{4,68},{68... | collective-permute-start | bytes 417800 | tf_op jit(solution)/shard_map/ppermute | solution.py:1824
  413.5 12.6 %copy-start.3 = (bf16[64,1088]{1,0:T(8,128)(2,1)S(1)}, bf16[64,1088]{1,0:T(8,128)(2,1)}, u32[]{:S(2)}) copy-start(bf16[64,1088]{1,0:T(8,128)(2,1)} %get-tuple-element.147) | copy-start | bytes 417796
  426.1 1.4 collective-permute-start
Sparse Core Ops, SparseCore 0:
  25.0 57.0 all-gather.4
  84.9 42.2 all-gather.6

commit v5 on v4

--- a/solution.py
+++ b/solution.py
@@ -314,7 +314,7 @@
     return slice(128 * (17 * g // 4), 128 * (17 * g // 4) + WINDOW)
 
 
-def spread_kernel(params, w_qkv, w_up):
+def spread_kernel(gains, biases, w_qkv, w_up):
     def body(r):
         h = Here(r.sems)
         own = pl.ds(pl.multiple_of(h.c * 16, 16), 16)
@@ -325,7 +325,8 @@
         h.ready()
         arrive, arrive_mid, arrive_up = h.sem(), h.sem(), h.sem()
         mine = r.params_in.at[h.s * SHARD + h.y]
-        mine[...] = r.params[...]
+        zeros = jnp.zeros((4, SLICE), F32)
+        mine[...] = jnp.concatenate([r.gains[0].astype(F32), r.biases[0].astype(F32), zeros], axis=0)
         for step, other, to in everyone(h):
             if step or other:
                 h.send(mine, mine, to, arrive)
@@ -362,7 +363,7 @@
         wait_bytes(r.up, arrive_up)
         h.finish()
 
-    ins = dict(params=(params, VMEM), w_qkv=(w_qkv, ANY), w_up=(w_up, ANY))
+    ins = dict(gains=(gains, VMEM), biases=(biases, VMEM), w_qkv=(w_qkv, ANY), w_up=(w_up, ANY))
     outs = dict(
         norms=(spec((2, 8, D), F32), VMEM), mid_piece=(spec((8, 16, WINDOW)), VMEM),
         mid_last=(spec((8, 16, WINDOW)), VMEM), side_piece=(spec((8, 16, WINDOW)), VMEM),
@@ -543,10 +544,10 @@
         weights.load()
         r.down_vm[...] = jnp.zeros_like(r.down_vm)
         h.barrier()
+        x = r.hidden[h.s].astype(F32)
+        a_value = layer_norm(x, r.norms[0, 0:1], r.norms[0, 2:3]).astype(BF16)
         h.ready()
         weights.send_qkv()
-        x = r.hidden[h.s].astype(F32)
-        a_value = layer_norm(x, r.norms[0, 0:1], r.norms[0, 2:3]).astype(BF16)
         gather = Gather8(h, r.a_vm)
         for half in range(PARTS):
             gather.start(a_value[half_rows(half)], half)
@@ -845,7 +846,7 @@
 def turn_kernel(at, kept, x, norms, first, up_all, up_last, cotangent):
     def body(r):
         h = Here(r.sems)
-        loads = load_layer(h, r, 1, 0)
+        loads = load_layer(h, r, 1, SHARD)
         h.barrier()
         sort_rows(r)
         h.ready()
@@ -1084,9 +1085,9 @@
         tile = 8 * group + i
         to = tile // 17
         h.send_or_keep(
-            out.at[i], r.out_sum.at[lax.rem(tile, 17)], (layer, h.c, to), (h.s == layer) & (to == h.y), arrive)
+            out.at[i], r.out_sum.at[lax.rem(tile, 17)], (1 - layer, h.c, to), (h.s != layer) & (to == h.y), arrive)
     h.send_or_keep(
-        out.at[pl.ds(8, 4)], r.last_in.at[group], (layer, h.c, SHARD - 1), (h.s == layer) & (h.y == SHARD - 1),
+        out.at[pl.ds(8, 4)], r.last_in.at[group], (1 - layer, h.c, SHARD - 1), (h.s != layer) & (h.y == SHARD - 1),
         arrive_last)
 
 
@@ -1144,7 +1145,7 @@
             for i in range(2):
                 r.up1_piece[2 * i : 2 * i + 2] = ups[i].result()
             send_piece(h, r.up1_piece, r.up_in, 1, arrive_up)
-            settle(1)
+            settle(0)
             rows16.start_out()
 
         def beside_sums():
@@ -1208,7 +1209,7 @@
         finish_back(
             h, r, sums, 0, r.residual[...], r.in_grad[...].astype(F32), r.context_vm, down_ready, up_ready, beside, near_end)
 
-        settle(0)
+        settle(1)
         h.finish()
 
     ins = dict(
@@ -1231,7 +1232,7 @@
         up0_in=VMEM((3, 4, SHARD, 16, WINDOW), BF16), up_low=VMEM((4, 4, 16, 2176), BF16),
         up_high=VMEM((4, 4, 16, 2176), BF16), main_sums=reduce_scratch(SHARD, 384), side_sums=reduce_scratch(SHARD, 256),
         up1_piece=VMEM((SHARD, 16, WINDOW), BF16), up_in=VMEM((8, 16, WINDOW), BF16), last_in=VMEM((8, 4, 16, D), BF16), **tail_scratch(), **back_scratch(),
-        **rows_scratch(), sems=pltpu.SemaphoreType.DMA((200,)))
+        **rows_scratch(), sems=pltpu.SemaphoreType.DMA((202,)))
     return call("back", body, ins, outs, scratch, collective_id=4)
 
 
@@ -1364,15 +1365,15 @@
         self.sums = [
             Reduce16(h, None, (None, r.mine_a, r.rows_second.at[0]), True),
             Reduce16(h, None, (None, r.mine_b, r.rows_second.at[1]), False),
-            Reduce16(h, r.rows_c, r.rows_sums_c, True, core)]
+            Reduce16(h, r.rows_c, r.rows_sums_c, True, 1 - core)]
         self.spreads = [
-            Spread16(h, r.rows_all.at[0], True), Spread16(h, r.rows_all.at[1], False), Spread16(h, r.rows_out, False, core)]
+            Spread16(h, r.rows_all.at[0], True), Spread16(h, r.rows_all.at[1], False), Spread16(h, r.rows_out, False, 1 - core)]
         self.arrive = h.sem()
         self.arrive_each = [h.sem() for _ in range(3)]
-        self.cross = [h.sem() for _ in range(2)]
+        self.cross = [h.sem() for _ in range(3)]
 
     def on(self, i):
-        return self.h.s == self.core if i == 2 else None
+        return self.h.s != self.core if i == 2 else None
 
     def when(self, i, act, also=None):
         conditions = [c for c in (self.on(i), also) if c is not None]
@@ -1388,7 +1389,7 @@
     def start_out(self):
         h, r = self.h, self.r
 
-        @pl.when(h.s == self.core)
+        @pl.when(h.s != self.core)
         def _():
             for c in range(CTX):
                 r.rows_c[c // 4, c % 4, 0] = r.out_sum[c]
@@ -1457,7 +1458,7 @@
                 src_ref=src, dst_ref=dst, send_sem=h.sem(), recv_sem=sem, device_id=h.sibling(), device_id_type=MESH)
             for src, dst, sem in (
                 (r.rows_all, r.rows_other, self.cross[0]),
-                (r.tiles.at[pl.ds(0, 2)], r.tiles_other, self.cross[1]))]
+                (r.tiles, r.tiles_other, self.cross[1]), (r.rows_out, r.rows_out, self.cross[2]))]
 
         @pl.when(h.s != self.core)
         def _():
@@ -1465,7 +1466,6 @@
                 copy.start()
 
         h.save_on(self.core, r.rows_all, r.rows_own)
-        h.save_on(self.core, r.rows_out, r.rows_out_all)
 
         @pl.when(h.s != self.core)
         def _():
@@ -1476,12 +1476,14 @@
         def _():
             wait_bytes(r.rows_other, self.cross[0])
             wait_bytes(r.tiles_other, self.cross[1])
+            wait_bytes(r.rows_out, self.cross[2])
 
         h.save_on(self.core, r.rows_other, r.rows_cross)
+        h.save_on(self.core, r.rows_out, r.rows_out_all)
 
 
 def rows_outs():
-    return dict(tiles=(spec((3, 16, D)), VMEM), tiles_other=(spec((2, 16, D)), VMEM))
+    return dict(tiles=(spec((3, 16, D)), VMEM), tiles_other=(spec((3, 16, D)), VMEM))
 
 
 def rows_scratch():
@@ -1569,36 +1571,44 @@
             r.last_message[i, 1] = r.up1_last[i]
             r.last_message[i, 2] = r.qkv1_last[i]
             h.send_or_keep(r.last_message.at[i], r.last_in.at[h.c], (h.s, chip, h.y), chip == h.c, arrive_last)
-        waits = start_tail(h, r)
-        wide = [Spread16(h, parts, i == 0) for i, parts in enumerate((r.wide_low, r.wide_high))]
-
-        def spread_wide():
-            wait_bytes(r.wide_in, arrive_wide)
-            blocks = [r.wide_in[g] for g in range(8)]
-
-            @pl.when(h.s == 0)
-            def _():
-                rows = joined_up(blocks)
-                r.wide_low[x, z] = rows[:, :2176]
-                r.wide_high[x, z] = rows[:, 2176:]
-
+        early, late = [
+            [Spread16(h, parts, i == 0, core) for i, parts in enumerate((r.wide_low, r.wide_high))] for core in (1, 0)]
+
+        def spread_early():
             @pl.when(h.s == 1)
             def _():
+                wait_bytes(r.wide_in, arrive_wide)
+                blocks = [r.wide_in[g] for g in range(8)]
                 rows = joined_qkv(blocks, added([block[:, 384:] for block in blocks]))
                 r.wide_low[x, z] = rows[:, :2176]
                 r.wide_high[x, z] = jnp.concatenate([rows[:, 2176:], jnp.zeros((16, 1024), BF16)], axis=1)
 
-            for each in wide:
+            for each in early:
                 each.start()
 
+        def spread_late():
+            @pl.when(h.s == 0)
+            def _():
+                wait_bytes(r.wide_in, arrive_wide)
+                rows = joined_up([r.wide_in[g] for g in range(8)])
+                r.wide_low[x, z] = rows[:, :2176]
+                r.wide_high[x, z] = rows[:, 2176:]
+
+            for each in late:
+                each.start()
+
+        waits = start_tail(h, r, spread_early)
+
         def arrived():
+            for each in early:
+                each.middle()
             rows16.middle()
             r.up0_piece[...] = up0.result()
             send_piece(h, r.up0_piece, r.wide_in, 0, arrive_wide)
 
         def beside():
             rows16.spread()
-            spread_wide()
+            spread_late()
 
         finish = run_tail(
             h, r, 0, r.x[h.s].astype(F32), waits, loads, r.qkv_last, main.start, side.start, arrived, beside,
@@ -1609,7 +1619,7 @@
             h.send_or_keep(r.qkv_last.at[i], r.late_in.at[h.c], (h.s, chip, h.y), chip == h.c, arrive_late)
         main.middle()
         side.middle()
-        for each in wide:
+        for each in late:
             each.middle()
         rows16.spread_on()
         arrive_rest = h.sem()
@@ -1669,7 +1679,7 @@
 
         for each in spreads:
             each.start()
-        for each in wide:
+        for each in early + late:
             each.finish()
         h.save(r.wide_low, r.wide_low_all)
         h.save(r.wide_high, r.wide_high_all)
@@ -1719,21 +1729,32 @@
         last_in=VMEM((CTX, 3, 16, WINDOW), BF16), late_in=VMEM((CTX, 16, WINDOW), BF16), wide_in=eight, qkv_in=eight, up0_piece=piece,
         up0_in=VMEM((3, SHARD, 16, WINDOW), BF16),
         rest_message=VMEM((2, 2, 16, WINDOW), BF16), rest=VMEM((4, 2, 2, 16, WINDOW), BF16),
-        sems=pltpu.SemaphoreType.DMA((124,)))
+        sems=pltpu.SemaphoreType.DMA((134,)))
     return call("last", body, ins, outs, scratch, collective_id=5)
 
 
 def join_kernel(back, last):
     def body(
         _, up_low, up_high, wide_low, wide_high, qkv_low, qkv_high, own0, cross0, out0, own1, cross1, out1, up_rest, qkv_rest,
-        tiles0, tiles_other0, tiles1, tiles_other1, up_ref, qkv_ref, norm_ref, down_ref, out_ref):
+        tiles0, tiles_other0, tiles1, tiles_other1, up_ref, qkv_ref, gain_ref, bias_ref, down_ref, out_ref):
+        def store_norms(rows, sums):
+            for i in range(5):
+
+                @pl.when(pl.program_id(0) == i)
+                def _():
+                    for k in range(2):
+                        part = slice(64 * i, 64 * i + min(rows, SLICE - 64 * i))
+                        count = part.stop - part.start
+                        gain_ref[0, k : k + 1, part] = sums[64 + 2 * k : 65 + 2 * k, :count]
+                        bias_ref[0, k : k + 1, part] = sums[65 + 2 * k : 66 + 2 * k, :count]
+
         def store(rows, up_parts, qkv_parts):
             for at, block in up_parts:
                 up_ref[:rows, at : at + block.shape[1]] = block.astype(F32)
             for at, block in qkv_parts:
                 block = block.astype(F32)
                 if at + block.shape[1] == 3328:
-                    norm_ref[:rows] = block[:, -128:]
+                    store_norms(rows, jnp.transpose(block[:, -128:]))
                     block = block[:, :-64]
                 qkv_ref[:rows, at : at + block.shape[1]] = block
 
@@ -1754,9 +1775,9 @@
                 out_ref[:16] = tiles[2].astype(F32)
 
         first = lax.axis_index(SECTION) == 0
-        pl.when(first)(lambda: rows_from((own0, cross0), out0, (tiles0, tiles_other0, tiles0[2])))
+        pl.when(first)(lambda: rows_from((own0, cross0), out0, (tiles0, tiles_other0, tiles_other0[2])))
         pl.when(jnp.logical_not(first))(
-            lambda: rows_from((cross1, own1), out1, (tiles_other1, tiles1, tiles1[2])))
+            lambda: rows_from((cross1, own1), out1, (tiles_other1, tiles1, tiles_other1[2])))
         low, high = (ref[0].reshape(64, 2176) for ref in (wide_low, wide_high))
 
         @pl.when((pl.program_id(0) < 4) & first)
@@ -1793,10 +1814,12 @@
     def all_of(width):
         return pl.BlockSpec((16, width), lambda i, section: (0, 0))
 
+    norms = pl.BlockSpec((1, 2, SLICE), lambda i, section: (0, 0, 0))
     return pl.pallas_call(
         body,
         out_shape=(
-            spec((SLICE, FF), F32), spec((SLICE, 3 * D), F32), spec((SLICE, 128), F32), spec((2, 544, D), F32),
+            spec((SLICE, FF), F32), spec((SLICE, 3 * D), F32), spec((1, 2, SLICE), F32), spec((1, 2, SLICE), F32),
+            spec((2, 544, D), F32),
             spec((SLICE, D), F32)),
         grid_spec=pltpu.PrefetchScalarGridSpec(
             num_scalar_prefetch=1,
@@ -1804,9 +1827,9 @@
             in_specs=[
                 line(2176, 1), line(2176, 1), line(2176, -1), line(2176, -1), line(1664, 0), line(1664, 0),
                 tile_line(0, 2), tile_line(0, 2), tile_line(0), tile_line(1, 2), tile_line(1, 2), tile_line(1),
-                all_of(FF), all_of(3328), *[tiles_of(3), tiles_of(2)] * 2],
+                all_of(FF), all_of(3328), *[tiles_of(3)] * 4],
             out_specs=(
-                rows(FF), rows(3 * D), rows(128), pl.BlockSpec((2, 128, D), lambda i, section: (0, i, 0)), rows(D))),
+                rows(FF), rows(3 * D), norms, norms, pl.BlockSpec((2, 128, D), lambda i, section: (0, i, 0)), rows(D))),
         name="join",
     )(lax.axis_index(SECTION).astype(jnp.int32).reshape(1), back.up_low_all, back.up_high_all, last.wide_low_all, last.wide_high_all, last.qkv_low_all, last.qkv_high_all, last.rows_own,
       last.rows_cross, last.rows_out_all, back.rows_own, back.rows_cross, back.rows_out_all, last.up_rest, last.qkv_rest,
@@ -1831,8 +1854,6 @@
 
 def shards(hidden_in, cotangent, block_order, qkv_weight, out_weight, up_weight, down_weight, norm_gains, norm_biases):
     section, ctx = lax.axis_index(SECTION), lax.axis_index(CONTEXT)
-    params = jnp.concatenate([norm_gains[0], norm_biases[0]], axis=0).astype(F32)
-    params = jnp.pad(params, ((0, 4), (0, 0)))
     grid = token_positions(block_order)
     own_positions = lax.dynamic_slice(grid, (section, ctx * ROWS), (1, ROWS))
     positions = grid.reshape(1, SEQ)
@@ -1844,19 +1865,18 @@
     at = (block_order, places, positions, own_positions.reshape(ROWS, 1))
     at_back = (block_order, places, positions.reshape(SEQ, 1), own_positions)
     hidden = hidden_in[0]
-    spread = spread_kernel(params, qkv_weight, up_weight)
+    spread = spread_kernel(norm_gains, norm_biases, qkv_weight, up_weight)
     norms = spread.norms
     mid_all = gathered(spread.mid_piece)
     first = first_kernel(hidden, norms, spread.side_piece, spread.side_last, out_weight, down_weight)
-    up_piece, first.q16 = lax.optimization_barrier((spread.side_piece[SHARD:], first.q16))
+    up_piece, first.q16 = lax.optimization_barrier((spread.side_piece, first.q16))
     up_all = gathered(up_piece)
     middle = middle_kernel(at, hidden, norms, first, mid_all, spread.mid_last)
-    turn = turn_kernel(at, middle, middle.y, norms, first, up_all, spread.side_last[SHARD:], cotangent[0])
+    turn = turn_kernel(at, middle, middle.y, norms, first, up_all, spread.side_last, cotangent[0])
     back = back_kernel(
         at_back, middle, turn, middle.y, turn, norms, first, middle.attended16, mid_all, spread.mid_last)
     last = last_kernel(at_back, first, middle, hidden, back, turn.up_g_last, norms)
-    up, qkv, norm_sums, down, out = join_kernel(back, last)
-    norm_sums = norm_sums[:, 64:68].T
+    up, qkv, gain, bias, down, out = join_kernel(back, last)
     activations = jnp.stack(swapped(section, middle.y, back.out))
     input_grads = jnp.stack(swapped(section, last.in_grad, back.in_grad))
     return (
@@ -1866,8 +1886,8 @@
         out[None],
         up[None],
         down.reshape(D, D)[None],
-        norm_sums[None, 0::2],
-        norm_sums[None, 1::2],
+        gain,
+        bias,
     )
 
 

time: 442 us -> 435 us (0.984)
  local copies, waits for them, and re-layouts: 8.86 us -> 3.8 us
  transfers between devices with their start and end apart: 4 -> 4, of which waited for: 2 -> 1; matrix products, arithmetic and copies ran while one was open for 2% -> 1% of each run, Pallas kernels for 26% -> 26%
where the time goes in v5:
time: 435 us; the launch traced here: 429 us
  Pallas kernels  385 us (89%)
  between operations  14.7 us (3%)
  starting transfers between devices  11.9 us (3%)
  waiting for transfers between devices  10.4 us (2%)
    pallas_call x6, Pallas kernels, call(): pl.pallas_call(kernel, out_shape=tuple((value[0] for value in outs.values...  375 us
    ppermute x2, starting transfers between devices, swapped(): lax.ppermute(jnp.where(section == 0, second, first), SECTION, [(0, 1), (1...  11.8 us
    all_gather x2, waiting for transfers between devices, gathered(): return lax.all_gather(x, CONTEXT)  10.3 us
    pallas_call x1, Pallas kernels, join_kernel(): pl.pallas_call(body, out_shape=(spec((SLICE, FF), F32), spec((SLICE, 3 *...  9.83 us
  transfers between devices with their start and end apart: 4, of which 1 were waited for; matrix products, arithmetic and copies ran while one was open for 1% of the time, Pallas kernels for 26%

profile of v5, /device:TPU:1, one launch (start us, length us, event | category | flops | bytes accessed | tf_op | source)
XLA Modules:
  0.0 428.9 jit_solution(7841873624366616179)
XLA Ops:
  7.2 0.0 all-gather.5.cloned.1.call-start
  7.2 16.5 %spread.1 = (f32[2,8,1088]{2,1,0:T(8,128)}, bf16[8,16,640]{2,1,0:T(8,128)(2,1)}, bf16[8,16,640]{2,1,0:T(8,128)(2,1)}, bf16[8,16,640]{2,1,0:T(8,128)(2,1)}, bf16[8,16,640]{2,1,0:T(8,128)(2,1)}) custom-call(bf16[1,2,272]{2,1,0:T(2,128)(2,1)} %refs_0_.5, bf16[1,2,272]{2,1,0:T(2,128)(2,1)} %refs_1_.1, bf16[1,272,3264]{2,1,0:T(8,128)(2,1)} %refs_2_.1, ...), custom_call_target="tpu_custom_call" | custom-call | tf_op jit(solution)/shard_map/spread/pallas_call | solution.py:54
  23.7 0.0 all-gather.5.cloned.1.call-update
  23.7 0.0 all-gather.7.cloned.1.call-start
  23.8 0.0 copy-start.4
  23.8 41.3 %first.1 = (bf16[512,1088]{1,0:T(8,128)(2,1)}, bf16[16,160,128]{2,1,0:T(8,128)(2,1)}, bf16[2,16,64,128]{3,2,1,0:T(8,128)(2,1)}, bf16[64,64]{1,0:T(8,128)(2,1)}, ...) custom-call(bf16[2,64,1088]{2,1,0:T(8,128)(2,1)} %bitcast.56, ...), custom_call_target="tpu_custom_call" | custom-call | tf_op jit(solution)/shard_map/first/pallas_call | solution.py:54
  65.0 0.0 all-gather.7.cloned.1.call-update
  65.1 0.1 multiply_add_fusion
  65.2 0.1 iota_add_fusion
  65.2 0.7 add.158.refs_2_
  65.9 2.0 add.164.refs_2_
  68.0 0.1 broadcast_in_dim.46
  68.0 0.1 add.156
  68.1 0.1 add.159
  68.2 0.1 dynamic-slice
  68.3 0.1 dynamic-slice_add_fusion.refs_3_
  68.4 0.7 copy.27.refs_3_
  69.1 0.1 select_reduce_fusion
  69.2 0.1 multiply_add_fusion.2
  69.3 0.6 pad_add_fusion.refs_1_
  69.9 10.3 %all-gather.5.cloned.1.call-done = bf16[128,16,640]{2,1,0:T(8,128)(2,1)} async-done(((bf16[8,16,640]{2,1,0:T(8,128)(2,1)}), bf16[128,16,640]{2,1,0:T(8,128)(2,1)}) %all-gather.5.cloned.1.call-update) | async-done | bytes 2621456 | tf_op jit(solution)/shard_map/all_gather | solution.py:1852
  80.2 58.9 %middle.1 = (bf16[64,64]{1,0:T(8,128)(2,1)}, bf16[64,16,64]{2,1,0:T(8,128)(2,1)}, f32[1024,128]{1,0:T(8,128)}, f32[64,128]{1,0:T(8,128)}, bf16[512,128]{1,0:T(8,...) custom-call(s32[2,32]{1,0:T(2,128)} %refs_0_.9, ...), custom_call_target="tpu_custom_call" | custom-call | tf_op jit(solution)/shard_map/middle/pallas_call | solution.py:54
  139.1 0.0 all-gather.7.cloned.1.call-done
  139.1 65.9 %turn.1 = (bf16[64,64]{1,0:T(8,128)(2,1)}, bf16[64,16,64]{2,1,0:T(8,128)(2,1)}, f32[1024,128]{1,0:T(8,128)}, f32[64,128]{1,0:T(8,128)}, bf16[512,640]{1,0:T(8,12...) custom-call(s32[2,32]{1,0:T(2,128)} %refs_0_.9, ...), custom_call_target="tpu_custom_call" | custom-call | tf_op jit(solution)/shard_map/turn/pallas_call | solution.py:54
  205.1 98.8 %back.1 = (bf16[64,1088]{1,0:T(8,128)(2,1)}, f32[64,1088]{1,0:T(8,128)}, bf16[16,32,128]{2,1,0:T(8,128)(2,1)}, bf16[64,64]{1,0:T(8,128)(2,1)}, bf16[4,16,640]{2,...) custom-call(s32[2,32]{1,0:T(2,128)} %refs_0_.9, ...), custom_call_target="tpu_custom_call" | custom-call | tf_op jit(solution)/shard_map/back/pallas_call | solution.py:54
  303.9 93.4 %last.1 = (bf16[64,1088]{1,0:T(8,128)(2,1)}, bf16[4,4,16,2176]{3,2,1,0:T(8,128)(2,1)}, bf16[4,4,16,2176]{3,2,1,0:T(8,128)(2,1)}, bf16[4,4,16,1664]{3,2,1,0:T(8,1...) custom-call(s32[2,32]{1,0:T(2,128)} %refs_0_.9, ...), custom_call_target="tpu_custom_call" | custom-call | tf_op jit(solution)/shard_map/last/pallas_call | solution.py:54
  397.3 0.9 broadcast_select_fusion
  398.3 11.7 %collective-permute-start.1 = (bf16[64,1088]{1,0:T(8,128)(2,1)S(1)}, bf16[64,1088]{1,0:T(8,128)(2,1)S(1)}, u32[]{:S(2)}, u32[]{:S(2)}) collective-permute-start(bf16[64,1088]{1,0:T(8,128)(2,1)S(1)} %broadcast_select_fusion), channel_id=1, source_target_pairs={{0,64},{64,0},{1,65},{65,1},{2,66},{66,2},{3,67},{67,3},{4,68},{68... | collective-permute-start | bytes 417800 | tf_op jit(solution)/shard_map/ppermute | solution.py:1847
  410.0 0.1 collective-permute-start
  410.1 9.8 %join.1 = (f32[272,4352]{1,0:T(8,128)}, f32[272,3264]{1,0:T(8,128)}, f32[1,2,272]{2,1,0:T(2,128)}, f32[1,2,272]{2,1,0:T(2,128)}, f32[2,544,1088]{2,1,0:T(8,128)}, /*index=5*/f32[272,1088]{1,0:T(8,128)}) custom-call(s32[1]{0:T(128)} %bitcast.17._, bf16[4,4,16,2176]{3,2,1,0:T(8,128)(2,1)} %get-tuple-element.150.up_low, ...), custom_call_target="tpu_custom_call" | custom-call | tf_op jit(solution)/shard_map/join/pallas_call | solution.py:1818
  420.0 0.8 maximum_bitcast_fusion.1
  420.8 0.8 maximum_bitcast_fusion
  (19 shorter events, 0.1 us)
Async XLA Ops:
  7.2 73.0 %all-gather.5.cloned.1.call-start = ((), (), s32[]{:S(2)}) async-start(), calls=%async_computation | async-start | bytes 2785280 | tf_op jit(solution)/shard_map/all_gather | solution.py:1852
  23.7 115.4 %all-gather.7.cloned.1.call-start = ((), (), s32[]{:S(2)}) async-start(), calls=%async_computation.1 | async-start | bytes 2785280 | tf_op jit(solution)/shard_map/all_gather | solution.py:1852
  23.8 41.3 %copy-start.4 = (s32[2,32]{1,0:T(2,128)S(1)}, s32[2,32]{1,0:T(2,128)}, u32[]{:S(2)}) copy-start(s32[2,32]{1,0:T(2,128)} %refs_0_.9) | copy-start | bytes 772
  68.4 70.7 %copy-start.5 = (s32[1,64]{1,0:T(1,128)}, s32[1,64]{1,0:T(1,128)S(1)}, u32[]{:S(2)}) copy-start(s32[1,64]{1,0:T(1,128)S(1)} %dynamic-slice_add_fusion.refs_3_) | copy-start | bytes 772
  303.9 93.5 %copy-start.2 = (bf16[64,1088]{1,0:T(8,128)(2,1)S(1)}, bf16[64,1088]{1,0:T(8,128)(2,1)}, u32[]{:S(2)}) copy-start(bf16[64,1088]{1,0:T(8,128)(2,1)} %get-tuple-element.149) | copy-start | bytes 417796
  303.9 106.1 %copy-start = (bf16[64,1088]{1,0:T(8,128)(2,1)S(1)}, bf16[64,1088]{1,0:T(8,128)(2,1)}, u32[]{:S(2)}) copy-start(bf16[64,1088]{1,0:T(8,128)(2,1)} %get-tuple-element.102.refs_7_.refs_14_) | copy-start | bytes 417796
  303.9 106.1 %copy-start.1 = (bf16[64,1088]{1,0:T(8,128)(2,1)S(1)}, bf16[64,1088]{1,0:T(8,128)(2,1)}, u32[]{:S(2)}) copy-start(bf16[64,1088]{1,0:T(8,128)(2,1)} %get-tuple-element.129) | copy-start | bytes 417796
  398.3 21.7 %collective-permute-start.1 = (bf16[64,1088]{1,0:T(8,128)(2,1)S(1)}, bf16[64,1088]{1,0:T(8,128)(2,1)S(1)}, u32[]{:S(2)}, u32[]{:S(2)}) collective-permute-start(bf16[64,1088]{1,0:T(8,128)(2,1)S(1)} %broadcast_select_fusion), channel_id=1, source_target_pairs={{0,64},{64,0},{1,65},{65,1},{2,66},{66,2},{3,67},{67,3},{4,68},{68... | collective-permute-start | bytes 417800 | tf_op jit(solution)/shard_map/ppermute | solution.py:1847
  410.0 10.8 %collective-permute-start = (bf16[64,1088]{1,0:T(8,128)(2,1)S(1)}, bf16[64,1088]{1,0:T(8,128)(2,1)S(1)}, u32[]{:S(2)}, u32[]{:S(2)}) collective-permute-start(bf16[64,1088]{1,0:T(8,128)(2,1)S(1)} %broadcast_select_fusion.2), channel_id=1, source_target_pairs={{0,64},{64,0},{1,65},{65,1},{2,66},{66,2},{3,67},{67,3},{4,68},{68... | collective-permute-start | bytes 417800 | tf_op jit(solution)/shard_map/ppermute | solution.py:1847
  410.1 9.9 %copy-start.3 = (bf16[64,1088]{1,0:T(8,128)(2,1)S(1)}, bf16[64,1088]{1,0:T(8,128)(2,1)}, u32[]{:S(2)}) copy-start(bf16[64,1088]{1,0:T(8,128)(2,1)} %get-tuple-element.148) | copy-start | bytes 417796
Sparse Core Ops, SparseCore 0:
  23.8 56.3 all-gather.4
  82.4 46.6 all-gather.6

commit v6 on v5

--- a/solution.py
+++ b/solution.py
@@ -322,14 +322,10 @@
             h.local(ref.at[0, rows], dst.at[pl.ds(16 * i, 16)])
             for ref, dst in ((r.w_up, r.up_rows), (r.w_qkv, r.qkv_rows)) for i, rows in enumerate((own, pl.ds(256, 16)))]
         h.barrier(whole=False)
-        h.ready()
         arrive, arrive_mid, arrive_up = h.sem(), h.sem(), h.sem()
         mine = r.params_in.at[h.s * SHARD + h.y]
         zeros = jnp.zeros((4, SLICE), F32)
         mine[...] = jnp.concatenate([r.gains[0].astype(F32), r.biases[0].astype(F32), zeros], axis=0)
-        for step, other, to in everyone(h):
-            if step or other:
-                h.send(mine, mine, to, arrive)
         for copy in loads:
             copy.wait()
 
@@ -345,6 +341,10 @@
                 r.mid[g] = packed_qkv(r.qkv_rows[...], g).reshape(2, 16, WINDOW)
                 r.up[g] = r.up_rows[:, window(g)].reshape(2, 16, WINDOW)
 
+        h.ready()
+        for step, other, to in everyone(h):
+            if step or other:
+                h.send(mine, mine, to, arrive)
         for step, other, to in everyone(h):
             g = 2 * to[2] + to[0]
             slot = h.s * SHARD + h.y
@@ -603,7 +603,8 @@
         for u in range(1, t + 1):
             out = out + dot(parts[u].astype(BF16), r.values[512 * u : 512 * u + 512])
         r.sorted_out[16 * t : 16 * t + 16] = (out / total).astype(BF16).reshape(16, 16, 64)
-        r.logs[256 * t : 256 * t + 256] = jnp.broadcast_to(top + jnp.log(total), (256, 128))
+        logs = jnp.transpose(jnp.broadcast_to(top + jnp.log(total), (256, 128)))
+        r.logs[:, 256 * t : 256 * t + 256] = logs[:8]
     for c in range(CTX):
         for m in range(2):
             for b in range(2):
@@ -633,7 +634,7 @@
 
 def attend_outs():
     return dict(
-        attended16=(spec((ROWS, 64)), VMEM), sorted_out=(spec((64, 16, 64)), VMEM), logs=(spec((1024, 128), F32), VMEM),
+        attended16=(spec((ROWS, 64)), VMEM), sorted_out=(spec((64, 16, 64)), VMEM), logs=(spec((8, 1024), F32), VMEM),
         logs16=(spec((ROWS, 128), F32), VMEM))
 
 
@@ -939,7 +940,7 @@
     for t in range(4):
         part = slice(256 * t, 256 * t + 256)
         query, grad = r.queries[part], r.grads[part]
-        logs = jnp.transpose(r.logs[part])[0:1]
+        logs = r.logs[0:1, part]
         delta = row_of(grad, r.sorted_out[16 * t : 16 * t + 16].reshape(256, 64))
         query_grad = jnp.zeros((256, 64), F32)
         for u in range(t + 1):

time: 435 us -> 435 us (level)
  no operation moved by 1% of the time
where the time goes in v6:
time: 435 us; the launch traced here: 428 us
  Pallas kernels  384 us (88%)
  between operations  14.7 us (3%)
  starting transfers between devices  11.9 us (3%)
  waiting for transfers between devices  10.4 us (2%)
    pallas_call x6, Pallas kernels, call(): pl.pallas_call(kernel, out_shape=tuple((value[0] for value in outs.values...  374 us
    ppermute x2, starting transfers between devices, swapped(): lax.ppermute(jnp.where(section == 0, second, first), SECTION, [(0, 1), (1...  11.8 us
    all_gather x2, waiting for transfers between devices, gathered(): return lax.all_gather(x, CONTEXT)  10.3 us
    pallas_call x1, Pallas kernels, join_kernel(): pl.pallas_call(body, out_shape=(spec((SLICE, FF), F32), spec((SLICE, 3 *...  9.83 us
  transfers between devices with their start and end apart: 4, of which 1 were waited for; matrix products, arithmetic and copies ran while one was open for 1% of the time, Pallas kernels for 26%

profile of v6, /device:TPU:1, one launch (start us, length us, event | category | flops | bytes accessed | tf_op | source)
XLA Modules:
  0.0 428.0 jit_solution(18413394956048155610)
XLA Ops:
  7.2 0.0 all-gather.5.cloned.1.call-start
  7.2 16.5 %spread.1 = (f32[2,8,1088]{2,1,0:T(8,128)}, bf16[8,16,640]{2,1,0:T(8,128)(2,1)}, bf16[8,16,640]{2,1,0:T(8,128)(2,1)}, bf16[8,16,640]{2,1,0:T(8,128)(2,1)}, bf16[8,16,640]{2,1,0:T(8,128)(2,1)}) custom-call(bf16[1,2,272]{2,1,0:T(2,128)(2,1)} %refs_0_.5, bf16[1,2,272]{2,1,0:T(2,128)(2,1)} %refs_1_.1, bf16[1,272,3264]{2,1,0:T(8,128)(2,1)} %refs_2_.1, ...), custom_call_target="tpu_custom_call" | custom-call | tf_op jit(solution)/shard_map/spread/pallas_call | solution.py:54
  23.7 0.0 all-gather.5.cloned.1.call-update
  23.7 0.0 all-gather.7.cloned.1.call-start
  23.7 0.0 copy-start.4
  23.8 41.3 %first.1 = (bf16[512,1088]{1,0:T(8,128)(2,1)}, bf16[16,160,128]{2,1,0:T(8,128)(2,1)}, bf16[2,16,64,128]{3,2,1,0:T(8,128)(2,1)}, bf16[64,64]{1,0:T(8,128)(2,1)}, ...) custom-call(bf16[2,64,1088]{2,1,0:T(8,128)(2,1)} %bitcast.56, ...), custom_call_target="tpu_custom_call" | custom-call | tf_op jit(solution)/shard_map/first/pallas_call | solution.py:54
  65.0 0.0 all-gather.7.cloned.1.call-update
  65.1 0.1 multiply_add_fusion
  65.1 0.1 iota_add_fusion
  65.2 0.7 add.158.refs_2_
  65.9 2.0 add.164.refs_2_
  68.0 0.1 broadcast_in_dim.46
  68.0 0.1 add.156
  68.1 0.1 add.159
  68.2 0.1 dynamic-slice
  68.3 0.1 dynamic-slice_add_fusion.refs_3_
  68.4 0.7 copy.27.refs_3_
  69.1 0.1 select_reduce_fusion
  69.2 0.1 multiply_add_fusion.2
  69.3 0.6 pad_add_fusion.refs_1_
  69.9 10.3 %all-gather.5.cloned.1.call-done = bf16[128,16,640]{2,1,0:T(8,128)(2,1)} async-done(((bf16[8,16,640]{2,1,0:T(8,128)(2,1)}), bf16[128,16,640]{2,1,0:T(8,128)(2,1)}) %all-gather.5.cloned.1.call-update) | async-done | bytes 2621456 | tf_op jit(solution)/shard_map/all_gather | solution.py:1853
  80.2 58.8 %middle.1 = (bf16[64,64]{1,0:T(8,128)(2,1)}, bf16[64,16,64]{2,1,0:T(8,128)(2,1)}, f32[8,1024]{1,0:T(8,128)}, f32[64,128]{1,0:T(8,128)}, bf16[512,128]{1,0:T(8,12...) custom-call(s32[2,32]{1,0:T(2,128)} %refs_0_.9, ...), custom_call_target="tpu_custom_call" | custom-call | tf_op jit(solution)/shard_map/middle/pallas_call | solution.py:54
  139.0 0.0 all-gather.7.cloned.1.call-done
  139.0 65.5 %turn.1 = (bf16[64,64]{1,0:T(8,128)(2,1)}, bf16[64,16,64]{2,1,0:T(8,128)(2,1)}, f32[8,1024]{1,0:T(8,128)}, f32[64,128]{1,0:T(8,128)}, bf16[512,640]{1,0:T(8,128)...) custom-call(s32[2,32]{1,0:T(2,128)} %refs_0_.9, ...), custom_call_target="tpu_custom_call" | custom-call | tf_op jit(solution)/shard_map/turn/pallas_call | solution.py:54
  204.5 98.6 %back.1 = (bf16[64,1088]{1,0:T(8,128)(2,1)}, f32[64,1088]{1,0:T(8,128)}, bf16[16,32,128]{2,1,0:T(8,128)(2,1)}, bf16[64,64]{1,0:T(8,128)(2,1)}, bf16[4,16,640]{2,...) custom-call(s32[2,32]{1,0:T(2,128)} %refs_0_.9, ...), custom_call_target="tpu_custom_call" | custom-call | tf_op jit(solution)/shard_map/back/pallas_call | solution.py:54
  303.2 93.3 %last.1 = (bf16[64,1088]{1,0:T(8,128)(2,1)}, bf16[4,4,16,2176]{3,2,1,0:T(8,128)(2,1)}, bf16[4,4,16,2176]{3,2,1,0:T(8,128)(2,1)}, bf16[4,4,16,1664]{3,2,1,0:T(8,1...) custom-call(s32[2,32]{1,0:T(2,128)} %refs_0_.9, ...), custom_call_target="tpu_custom_call" | custom-call | tf_op jit(solution)/shard_map/last/pallas_call | solution.py:54
  396.5 0.9 broadcast_select_fusion
  397.4 11.7 %collective-permute-start.1 = (bf16[64,1088]{1,0:T(8,128)(2,1)S(1)}, bf16[64,1088]{1,0:T(8,128)(2,1)S(1)}, u32[]{:S(2)}, u32[]{:S(2)}) collective-permute-start(bf16[64,1088]{1,0:T(8,128)(2,1)S(1)} %broadcast_select_fusion), channel_id=1, source_target_pairs={{0,64},{64,0},{1,65},{65,1},{2,66},{66,2},{3,67},{67,3},{4,68},{68... | collective-permute-start | bytes 417800 | tf_op jit(solution)/shard_map/ppermute | solution.py:1848
  409.1 0.1 collective-permute-start
  409.3 9.8 %join.1 = (f32[272,4352]{1,0:T(8,128)}, f32[272,3264]{1,0:T(8,128)}, f32[1,2,272]{2,1,0:T(2,128)}, f32[1,2,272]{2,1,0:T(2,128)}, f32[2,544,1088]{2,1,0:T(8,128)}, /*index=5*/f32[272,1088]{1,0:T(8,128)}) custom-call(s32[1]{0:T(128)} %bitcast.17._, bf16[4,4,16,2176]{3,2,1,0:T(8,128)(2,1)} %get-tuple-element.150.up_low, ...), custom_call_target="tpu_custom_call" | custom-call | tf_op jit(solution)/shard_map/join/pallas_call | solution.py:1819
  419.2 0.8 maximum_bitcast_fusion.1
  420.0 0.8 maximum_bitcast_fusion
  (19 shorter events, 0.1 us)
Async XLA Ops:
  7.2 73.0 %all-gather.5.cloned.1.call-start = ((), (), s32[]{:S(2)}) async-start(), calls=%async_computation | async-start | bytes 2785280 | tf_op jit(solution)/shard_map/all_gather | solution.py:1853
  23.7 115.3 %all-gather.7.cloned.1.call-start = ((), (), s32[]{:S(2)}) async-start(), calls=%async_computation.1 | async-start | bytes 2785280 | tf_op jit(solution)/shard_map/all_gather | solution.py:1853
  23.7 41.3 %copy-start.4 = (s32[2,32]{1,0:T(2,128)S(1)}, s32[2,32]{1,0:T(2,128)}, u32[]{:S(2)}) copy-start(s32[2,32]{1,0:T(2,128)} %refs_0_.9) | copy-start | bytes 772
  68.4 70.6 %copy-start.5 = (s32[1,64]{1,0:T(1,128)}, s32[1,64]{1,0:T(1,128)S(1)}, u32[]{:S(2)}) copy-start(s32[1,64]{1,0:T(1,128)S(1)} %dynamic-slice_add_fusion.refs_3_) | copy-start | bytes 772
  303.2 93.3 %copy-start.2 = (bf16[64,1088]{1,0:T(8,128)(2,1)S(1)}, bf16[64,1088]{1,0:T(8,128)(2,1)}, u32[]{:S(2)}) copy-start(bf16[64,1088]{1,0:T(8,128)(2,1)} %get-tuple-element.149) | copy-start | bytes 417796
  303.2 106.0 %copy-start = (bf16[64,1088]{1,0:T(8,128)(2,1)S(1)}, bf16[64,1088]{1,0:T(8,128)(2,1)}, u32[]{:S(2)}) copy-start(bf16[64,1088]{1,0:T(8,128)(2,1)} %get-tuple-element.102.refs_7_.refs_14_) | copy-start | bytes 417796
  303.2 106.0 %copy-start.1 = (bf16[64,1088]{1,0:T(8,128)(2,1)S(1)}, bf16[64,1088]{1,0:T(8,128)(2,1)}, u32[]{:S(2)}) copy-start(bf16[64,1088]{1,0:T(8,128)(2,1)} %get-tuple-element.129) | copy-start | bytes 417796
  397.4 21.7 %collective-permute-start.1 = (bf16[64,1088]{1,0:T(8,128)(2,1)S(1)}, bf16[64,1088]{1,0:T(8,128)(2,1)S(1)}, u32[]{:S(2)}, u32[]{:S(2)}) collective-permute-start(bf16[64,1088]{1,0:T(8,128)(2,1)S(1)} %broadcast_select_fusion), channel_id=1, source_target_pairs={{0,64},{64,0},{1,65},{65,1},{2,66},{66,2},{3,67},{67,3},{4,68},{68... | collective-permute-start | bytes 417800 | tf_op jit(solution)/shard_map/ppermute | solution.py:1848
  409.1 10.8 %collective-permute-start = (bf16[64,1088]{1,0:T(8,128)(2,1)S(1)}, bf16[64,1088]{1,0:T(8,128)(2,1)S(1)}, u32[]{:S(2)}, u32[]{:S(2)}) collective-permute-start(bf16[64,1088]{1,0:T(8,128)(2,1)S(1)} %broadcast_select_fusion.2), channel_id=1, source_target_pairs={{0,64},{64,0},{1,65},{65,1},{2,66},{66,2},{3,67},{67,3},{4,68},{68... | collective-permute-start | bytes 417800 | tf_op jit(solution)/shard_map/ppermute | solution.py:1848
  409.3 9.9 %copy-start.3 = (bf16[64,1088]{1,0:T(8,128)(2,1)S(1)}, bf16[64,1088]{1,0:T(8,128)(2,1)}, u32[]{:S(2)}) copy-start(bf16[64,1088]{1,0:T(8,128)(2,1)} %get-tuple-element.148) | copy-start | bytes 417796
Sparse Core Ops, SparseCore 0:
  23.8 56.3 all-gather.4
  82.4 46.5 all-gather.6
